TPU v7x, 32 devices: a whole 2x2x4 slice. The times are simulated.
32 devices in a mesh: ctx: 4 (over z), fsdp: 8 (over y, x, core).
Axes of the slice: x: 2, y: 2, z: 4, core: 2. Of those that a mesh axis runs over, the one named last changes fastest.
Arguments:
- tokens: bfloat16 [8, 8, 128, 2048], P('fsdp', 'ctx'), may hold values from -6 to 6
- pairs: int32 [4, 2], replicated, may hold values from 0 to 7, as said below
- valid: int32 [8, 8, 128], P('fsdp', 'ctx'), may hold values from 0 to 1, as said below
- teacher: bfloat16 [8, 8, 128, 2048], P('fsdp', 'ctx'), may hold values from -6 to 6
- w_query: bfloat16 [2048, 2048], P('fsdp'), may hold values from -0.125 to 0.125
- w_key: bfloat16 [2048, 2048], P('fsdp'), may hold values from -0.125 to 0.125
- w_value: bfloat16 [2048, 2048], P('fsdp'), may hold values from -0.125 to 0.125
- w_out: bfloat16 [2048, 2048], P('fsdp'), may hold values from -0.5 to 0.5
- w_gate: bfloat16 [2048, 8192], P('fsdp'), may hold values from -0.125 to 0.125
- w_up: bfloat16 [2048, 8192], P('fsdp'), may hold values from -0.125 to 0.125
- w_down: bfloat16 [8192, 2048], P('fsdp'), may hold values from -0.0625 to 0.0625
Outputs:
- activations: bfloat16 [8, 8, 128, 2048], P('fsdp', 'ctx')
- loss: float32 [], replicated
- input_grad: float32 [8, 8, 128, 2048], P('fsdp', 'ctx')
- grad_query: float32 [2048, 2048], P(('ctx', 'fsdp'))
- grad_key: float32 [2048, 2048], P(('ctx', 'fsdp'))
- grad_value: float32 [2048, 2048], P(('ctx', 'fsdp'))
- grad_out: float32 [2048, 2048], P(('ctx', 'fsdp'))
- grad_gate: float32 [2048, 8192], P(('ctx', 'fsdp'))
- grad_up: float32 [2048, 8192], P(('ctx', 'fsdp'))
- grad_down: float32 [8192, 2048], P(('ctx', 'fsdp'))
Inputs may be any that keep to these rules, and one draw needn't show every extreme that they name: `pairs`: row r lists some block j and block 7 - j, in either order; each j stands in exactly one row. `valid`: 1 marks a token that the loss counts; the first token of slot 0 of every sequence always counts.
All inputs are finite; a program needn't handle non-finite values.
Results may differ from a plain program's by a relative error of at most 0.015.
Values may be sent and summed in bfloat16 or wider, within the bound.
No kernel may reach another device: no remote copies, remote signals or barrier semaphores. Data moves between devices by JAX's collectives and lax.ppermute only.
A program may use at most 640 MiB of HBM per device.

v0:
```python
import jax
import jax.numpy as jnp
from jax import lax
from jax.sharding import PartitionSpec as P

HD = 128


epsilon = 1e-05


def normalize(stream_rows):
    centered = stream_rows - jnp.mean(stream_rows, -1, keepdims=True)
    inverse = lax.rsqrt(jnp.mean(centered * centered, -1, keepdims=True) + epsilon)
    return (centered * inverse, inverse)


def norm_back(gradient, normed, inverse):
    centered_grad = gradient - jnp.mean(gradient, -1, keepdims=True)
    return inverse * (centered_grad - normed * jnp.mean(gradient * normed, -1, keepdims=True))


def angles(blocks, block_len):
    offsets = jnp.arange(block_len, dtype=jnp.int32)
    positions = (blocks[:, None] * block_len + offsets[None, :]).reshape(-1).astype(jnp.float32)
    frequency = 10000.0 ** (-2.0 * jnp.arange(HD // 2, dtype=jnp.float32) / HD)
    phases = positions[:, None] * frequency[None, :]
    return (jnp.cos(phases)[:, None, :], jnp.sin(phases)[:, None, :])


def rotate(values, cosine_table, sine_table):
    half_width = values.shape[-1] // 2
    leading = values[..., :half_width]
    trailing = values[..., half_width:]
    return jnp.concatenate(
        [
            leading * cosine_table - trailing * sine_table,
            trailing * cosine_table + leading * sine_table,
        ],
        -1,
    )


def unrotate(gradient, cosine_table, sine_table):
    half_width = gradient.shape[-1] // 2
    leading = gradient[..., :half_width]
    trailing = gradient[..., half_width:]
    return jnp.concatenate(
        [
            leading * cosine_table + trailing * sine_table,
            trailing * cosine_table - leading * sine_table,
        ],
        -1,
    )


def times_transpose(left, right):
    return lax.dot_general(
        left, right, (((1,), (1,)), ((), ())), preferred_element_type=jnp.float32
    )


def contract_rows(left, right):
    return lax.dot_general(
        left, right, (((0,), (0,)), ((), ())), preferred_element_type=jnp.float32
    )


def fold_forward(inputs, pieces):
    return tuple(
        (jnp.dot(inputs, shard_rows, preferred_element_type=jnp.float32) for shard_rows in pieces)
    )


def fold_backward(gradients, pieces):
    update = times_transpose(gradients[0], pieces[0])
    for position in range(1, len(pieces)):
        update = update + times_transpose(gradients[position], pieces[position])
    return update


def body(tokens, pairs, valid, teacher, w_query, w_key, w_value, w_out, w_gate, w_up, w_down):
    sequences, slot_count, block_len, model_width = tokens.shape
    hidden_width = w_gate.shape[1]
    ratio = hidden_width // model_width
    head_count = model_width // HD
    row_count = sequences * slot_count * block_len
    query_len = slot_count * block_len
    devices_all = lax.axis_size("ctx") * lax.axis_size("fsdp")
    own_blocks = lax.dynamic_slice_in_dim(pairs, lax.axis_index("ctx"), 1, 0).reshape(-1)
    all_blocks = pairs.reshape(-1)
    cosine_table, sine_table = angles(own_blocks, block_len)
    allowed = (
        jnp.repeat(all_blocks, block_len)[None, :] <= jnp.repeat(own_blocks, block_len)[:, None]
    )
    query_scale = HD ** (-0.5)
    shaped = (sequences, query_len, head_count, HD)
    stream_rows = tokens.astype(jnp.float32).reshape(row_count, model_width)
    normed_one, inverse_one = normalize(stream_rows)
    input_one = normed_one.astype(jnp.bfloat16)
    query_raw, key_raw, value_raw = fold_forward(
        input_one,
        (
            lax.all_gather(w_query, "fsdp", axis=0, tiled=True),
            lax.all_gather(w_key, "fsdp", axis=0, tiled=True),
            lax.all_gather(w_value, "fsdp", axis=0, tiled=True),
        ),
    )
    query = (rotate(query_raw.reshape(shaped), cosine_table, sine_table) * query_scale).astype(
        jnp.bfloat16
    )
    keys_local = rotate(key_raw.reshape(shaped), cosine_table, sine_table).astype(jnp.bfloat16)
    values_local = value_raw.reshape(shaped).astype(jnp.bfloat16)
    keys, values = (
        lax.all_gather(keys_local, "ctx", axis=1, tiled=True),
        lax.all_gather(values_local, "ctx", axis=1, tiled=True),
    )

    def masked_scores(query_block, key_block):
        scores = jnp.einsum(
            "qhd,khd->hqk", query_block, key_block, preferred_element_type=jnp.float32
        )
        return jnp.where(allowed[None], scores, -1e30)

    def attend(inputs):
        query_block, key_block, value_block = inputs
        scores = masked_scores(query_block, key_block)
        highest_score = jnp.max(scores, -1, keepdims=True)
        exponent = jnp.exp(scores - highest_score)
        denominator = jnp.sum(exponent, -1, keepdims=True)
        attn_probs = (exponent / denominator).astype(jnp.bfloat16)
        mixed_block = jnp.einsum(
            "hqk,khd->qhd", attn_probs, value_block, preferred_element_type=jnp.float32
        )
        return (mixed_block, highest_score + jnp.log(denominator))

    mixed, log_total = lax.map(attend, (query, keys, values))
    attended = mixed.reshape(row_count, model_width).astype(jnp.bfloat16)
    (attn_branch,) = fold_forward(attended, (lax.all_gather(w_out, "fsdp", axis=0, tiled=True),))
    residual = stream_rows + attn_branch
    normed_two, inverse_two = normalize(residual)
    input_two = normed_two.astype(jnp.bfloat16)
    gate_pre, up_pre = fold_forward(
        input_two,
        (
            lax.all_gather(w_gate, "fsdp", axis=0, tiled=True),
            lax.all_gather(w_up, "fsdp", axis=0, tiled=True),
        ),
    )
    sigmoid_gate = jax.nn.sigmoid(gate_pre)
    silu_gate = gate_pre * sigmoid_gate
    hidden = (silu_gate * up_pre).astype(jnp.bfloat16)
    (mlp_branch,) = fold_forward(hidden, (lax.all_gather(w_down, "fsdp", axis=0, tiled=True),))
    output = residual + mlp_branch
    valid_float = valid.reshape(row_count).astype(jnp.float32)
    deviation = output - teacher.reshape(row_count, model_width).astype(jnp.float32)
    squares_local = jnp.sum(valid_float[:, None] * deviation * deviation)
    count_local = jnp.sum(valid_float)
    squares_all, count_all = lax.psum((squares_local, count_local), ("ctx", "fsdp"))
    loss_value = squares_all / (count_all * model_width)
    token_total = row_count * devices_all
    grad_output = token_total / count_all * valid_float[:, None] * deviation
    grad_mlp = grad_output.astype(jnp.bfloat16)
    grad_hidden = fold_backward((grad_mlp,), (lax.all_gather(w_down, "fsdp", axis=0, tiled=True),))
    grad_gate_pre = (
        grad_hidden * up_pre * sigmoid_gate * (1.0 + gate_pre * (1.0 - sigmoid_gate))
    ).astype(jnp.bfloat16)
    grad_up_pre = (grad_hidden * silu_gate).astype(jnp.bfloat16)
    grad_two = fold_backward(
        (grad_gate_pre, grad_up_pre),
        (
            lax.all_gather(w_gate, "fsdp", axis=0, tiled=True),
            lax.all_gather(w_up, "fsdp", axis=0, tiled=True),
        ),
    )
    grad_residual = grad_output + norm_back(grad_two, normed_two, inverse_two)
    grad_branch = grad_residual.astype(jnp.bfloat16)
    grad_attended = fold_backward(
        (grad_branch,), (lax.all_gather(w_out, "fsdp", axis=0, tiled=True),)
    )
    grad_mixed = grad_attended.astype(jnp.bfloat16).reshape(shaped)

    def attend_back(inputs):
        query_block, key_block, value_block, grad_block, mixed_block, log_block = inputs
        scores = masked_scores(query_block, key_block)
        attn_probs = jnp.exp(scores - log_block)
        grad_probs = jnp.einsum(
            "qhd,khd->hqk", grad_block, value_block, preferred_element_type=jnp.float32
        )
        row_delta = jnp.einsum("qhd,qhd->hq", grad_block.astype(jnp.float32), mixed_block)[
            ..., None
        ]
        grad_scores = (attn_probs * (grad_probs - row_delta)).astype(jnp.bfloat16)
        grad_query_block = jnp.einsum(
            "hqk,khd->qhd", grad_scores, key_block, preferred_element_type=jnp.float32
        )
        grad_key_block = jnp.einsum(
            "hqk,qhd->khd", grad_scores, query_block, preferred_element_type=jnp.float32
        )
        grad_value_block = jnp.einsum(
            "hqk,qhd->khd",
            attn_probs.astype(jnp.bfloat16),
            grad_block,
            preferred_element_type=jnp.float32,
        )
        return (grad_query_block, grad_key_block, grad_value_block)

    grad_query, grad_keys_all, grad_values_all = lax.map(
        attend_back, (query, keys, values, grad_mixed, mixed, log_total)
    )
    grad_keys, grad_values = (
        lax.psum_scatter(
            grad_keys_all.astype(jnp.bfloat16), "ctx", scatter_dimension=1, tiled=True
        ).astype(jnp.float32),
        lax.psum_scatter(
            grad_values_all.astype(jnp.bfloat16), "ctx", scatter_dimension=1, tiled=True
        ).astype(jnp.float32),
    )
    grad_query_pre = (
        unrotate(grad_query * query_scale, cosine_table, sine_table)
        .astype(jnp.bfloat16)
        .reshape(row_count, model_width)
    )
    grad_key_pre = (
        unrotate(grad_keys, cosine_table, sine_table)
        .astype(jnp.bfloat16)
        .reshape(row_count, model_width)
    )
    grad_value_pre = grad_values.astype(jnp.bfloat16).reshape(row_count, model_width)
    grad_one = fold_backward(
        (grad_query_pre, grad_key_pre, grad_value_pre),
        (
            lax.all_gather(w_query, "fsdp", axis=0, tiled=True),
            lax.all_gather(w_key, "fsdp", axis=0, tiled=True),
            lax.all_gather(w_value, "fsdp", axis=0, tiled=True),
        ),
    )
    grad_input = grad_residual + norm_back(grad_one, normed_one, inverse_one)
    down_part = contract_rows(hidden, grad_mlp).reshape(
        lax.axis_size(("ctx", "fsdp")) * (model_width // devices_all), ratio * model_width
    )
    stacked = lax.psum_scatter(
        jnp.concatenate(
            [
                contract_rows(input_one, grad_query_pre),
                contract_rows(input_one, grad_key_pre),
                contract_rows(input_one, grad_value_pre),
                contract_rows(attended, grad_branch),
                contract_rows(input_two, grad_gate_pre),
                contract_rows(input_two, grad_up_pre),
                down_part,
            ],
            1,
        ),
        ("ctx", "fsdp"),
        scatter_dimension=0,
        tiled=True,
    )
    down_start = 4 * model_width + 2 * hidden_width
    grad_down_rows = stacked[:, down_start:].reshape(-1, model_width)
    return (
        output.reshape(tokens.shape).astype(jnp.bfloat16),
        loss_value,
        grad_input.reshape(tokens.shape),
        stacked[:, 0:model_width],
        stacked[:, model_width : 2 * model_width],
        stacked[:, 2 * model_width : 3 * model_width],
        stacked[:, 3 * model_width : 4 * model_width],
        stacked[:, 4 * model_width : 4 * model_width + hidden_width],
        stacked[:, 4 * model_width + hidden_width : down_start],
        grad_down_rows,
    )


def solution(mesh):
    in_specs = (
        P("fsdp", "ctx", None, None),
        P(),
        P("fsdp", "ctx", None),
        P("fsdp", "ctx", None, None),
        P("fsdp", None),
        P("fsdp", None),
        P("fsdp", None),
        P("fsdp", None),
        P("fsdp", None),
        P("fsdp", None),
        P("fsdp", None),
    )
    out_specs = (
        P("fsdp", "ctx", None, None),
        P(),
        P("fsdp", "ctx", None, None),
        P(("ctx", "fsdp"), None),
        P(("ctx", "fsdp"), None),
        P(("ctx", "fsdp"), None),
        P(("ctx", "fsdp"), None),
        P(("ctx", "fsdp"), None),
        P(("ctx", "fsdp"), None),
        P(("ctx", "fsdp"), None),
    )
    return jax.shard_map(body, mesh=mesh, in_specs=in_specs, out_specs=out_specs, check_vma=False)
```

profile of v0, /device:TPU:16, one launch (start us, length us, event | category | flops | bytes accessed | tf_op | source)
XLA Modules:
  0.0 4114.7 jit_solution(11484245608797171111)
XLA Ops:
  12.3 53.2 %all-gather.13.cloned.1.call-done = bf16[2048,2048]{1,0:T(8,128)(2,1)} async-done(((bf16[256,2048]{1,0:T(8,128)(2,1)}), bf16[2048,2048]{1,0:T(8,128)(2,1)}) %all-gather.13.cloned.1.call-update) | async-done | bytes 8388624 | tf_op jit(solution)/shard_map/all_gather | solution.py:104
  77.8 43.9 %all-gather.15.cloned.1.call-done = bf16[2048,2048]{1,0:T(8,128)(2,1)} async-done(((bf16[256,2048]{1,0:T(8,128)(2,1)}), bf16[2048,2048]{1,0:T(8,128)(2,1)}) %all-gather.15.cloned.1.call-update) | async-done | bytes 8388624 | tf_op jit(solution)/shard_map/all_gather | solution.py:105
  145.8 32.3 all-gather.11.cloned.1.call-done
  200.6 58.2 %all-gather.17.cloned.1.call-done = bf16[1,1024,16,128]{1,3,2,0:T(8,128)(2,1)} async-done(((bf16[1,256,16,128]{1,3,2,0:T(8,128)(2,1)}), bf16[1,1024,16,128]{1,3,2,0:T(8,128)(2,1)}) %all-gather.17.cloned.1.call-update) | async-done | bytes 4194320 | tf_op jit(solution)/shard_map/all_gather | solution.py:115
  273.7 66.4 %all-gather.27.cloned.1.call-done = bf16[1024,16,128]{2,0,1:T(8,128)(2,1)} async-done(((bf16[256,16,128]{2,0,1:T(8,128)(2,1)}), bf16[1024,16,128]{2,0,1:T(8,128)(2,1)}) %all-gather.27.cloned.1.call-update) | async-done | bytes 4194320 | tf_op jit(solution)/shard_map/all_gather | solution.py:116
  351.6 44.7 %all-gather.19.cloned.1.call-done = bf16[2048,2048]{1,0:T(8,128)(2,1)} async-done(((bf16[256,2048]{1,0:T(8,128)(2,1)}), bf16[2048,2048]{1,0:T(8,128)(2,1)}) %all-gather.19.cloned.1.call-update) | async-done | bytes 8388624 | tf_op jit(solution)/shard_map/all_gather | solution.py:139
  403.4 155.6 %all-gather.21.cloned.1.call-done = bf16[2048,8192]{1,0:T(8,128)(2,1)} async-done(((bf16[256,8192]{1,0:T(8,128)(2,1)}), bf16[2048,8192]{1,0:T(8,128)(2,1)}) %all-gather.21.cloned.1.call-update) | async-done | bytes 33554448 | tf_op jit(solution)/shard_map/all_gather | solution.py:146
  559.0 19.5 fusion.43
  578.5 143.2 %all-gather.23.cloned.1.call-done = bf16[2048,8192]{1,0:T(8,128)(2,1)} async-done(((bf16[256,8192]{1,0:T(8,128)(2,1)}), bf16[2048,8192]{1,0:T(8,128)(2,1)}) %all-gather.23.cloned.1.call-update) | async-done | bytes 33554448 | tf_op jit(solution)/shard_map/all_gather | solution.py:147
  721.7 26.0 multiply_convert_fusion.3
  747.7 136.7 %all-gather.25.cloned.1.call-done = bf16[8192,2048]{1,0:T(8,128)(2,1)} async-done(((bf16[1024,2048]{1,0:T(8,128)(2,1)}), bf16[8192,2048]{1,0:T(8,128)(2,1)}) %all-gather.25.cloned.1.call-update) | async-done | bytes 33554448 | tf_op jit(solution)/shard_map/all_gather | solution.py:153
  884.4 18.3 fusion.15
  902.7 39.9 all-reduce
  945.4 22.0 multiply_convert_fusion.1
  967.4 16.9 fusion.44
  984.3 16.1 fusion.39
  1017.0 12.5 multiply_convert_fusion
  1046.8 25.6 fusion.46
  1072.4 79.9 %reshape.552 = f32[2048,8192]{1,0:T(8,128)} reshape(f32[8192,2048]{1,0:T(8,128)} %fusion.46) | data formatting | bytes 134217728 | tf_op jit(solution)/shard_map/reshape | solution.py:239
  1179.7 14.8 reduce-scatter.6.cloned.1.call-done
  1212.5 23.4 convolution_dynamic-update-slice_fusion.1
  1236.0 23.7 convolution_dynamic-update-slice_fusion
  1259.6 44.3 %constant_dynamic-update-slice_fusion = f32[2048,32768]{1,0:T(8,128)} fusion(f32[2048,32768]{1,0:T(8,128)} %convolution_dynamic-update-slice_fusion, f32[2048,8192]{1,0:T(8,128)} %reshape.552), kind=kLoop, calls=%fused_computation.80 | loop fusion | bytes 134217728 | tf_op jit(solution)/shard_map/concatenate | solution.py:243
  1322.2 2774.4 %reduce-scatter.8.cloned.1.call-done = f32[64,32768]{1,0:T(8,128)} async-done(((f32[2048,32768]{1,0:T(8,128)}), f32[64,32768]{1,0:T(8,128)}) %reduce-scatter.8.cloned.1.call-update) | async-done | bytes 8388624 | tf_op jit(solution)/shard_map/reduce_scatter | solution.py:242
  (173 shorter events, 205.1 us)
Async XLA Ops:
  7.2 58.2 %all-gather.13.cloned.1.call-start = ((), (), s32[]{:S(2)}) async-start(), calls=%async_computation.4 | async-start | bytes 9437184 | tf_op jit(solution)/shard_map/all_gather | solution.py:104
  7.9 113.8 %all-gather.15.cloned.1.call-start = ((), (), s32[]{:S(2)}) async-start(), calls=%async_computation.5 | async-start | bytes 9437184 | tf_op jit(solution)/shard_map/all_gather | solution.py:105
  8.7 169.4 %all-gather.11.cloned.1.call-start = ((), (), s32[]{:S(2)}) async-start(), calls=%async_computation.3 | async-start | bytes 9437184 | tf_op jit(solution)/shard_map/all_gather | solution.py:106
  9.4 249.4 %all-gather.17.cloned.1.call-start = ((), (), s32[]{:S(2)}) async-start(), calls=%async_computation.6 | async-start | bytes 5242880 | tf_op jit(solution)/shard_map/all_gather | solution.py:115
  10.9 129.1 %copy-start.15 = (f32[1,2,128,2048]{3,2,1,0:T(8,128)}, f32[1,2,128,2048]{3,2,1,0:T(8,128)S(1)}, u32[]{:S(2)}) copy-start(f32[1,2,128,2048]{3,2,1,0:T(8,128)S(1)} %convert_element_type.208) | copy-start | bytes 6291460
  11.4 128.7 %copy-start.33 = (f32[256]{0:T(256)}, f32[256]{0:T(256)S(1)}, u32[]{:S(2)}) copy-start(f32[256]{0:T(256)S(1)} %get-tuple-element.95) | copy-start | bytes 3076
  11.9 128.2 %copy-start.35 = (f32[256]{0:T(256)}, f32[256]{0:T(256)S(1)}, u32[]{:S(2)}) copy-start(f32[256]{0:T(256)S(1)} %get-tuple-element.97) | copy-start | bytes 3076
  12.2 130.4 %copy-start.29 = (f32[256,64]{0,1:T(8,128)}, f32[256,64]{0,1:T(8,128)S(1)}, u32[]{:S(2)}) copy-start(f32[256,64]{0,1:T(8,128)S(1)} %get-tuple-element.93) | copy-start | bytes 196612
  12.2 130.4 %copy-start.31 = (f32[256,64]{0,1:T(8,128)}, f32[256,64]{0,1:T(8,128)S(1)}, u32[]{:S(2)}) copy-start(f32[256,64]{0,1:T(8,128)S(1)} %get-tuple-element.94) | copy-start | bytes 196612
  144.2 114.6 %copy-start.10 = (f32[256,16,64]{0,2,1:T(8,128)}, f32[256,16,64]{0,2,1:T(8,128)S(1)}, u32[]{:S(2)}) copy-start(f32[256,16,64]{0,2,1:T(8,128)S(1)} %get-tuple-element.83) | copy-start | bytes 3145732
  145.4 194.8 %all-gather.27.cloned.1.call-start = ((), (), s32[]{:S(2)}) async-start(), calls=%async_computation.14 | async-start | bytes 5242880 | tf_op jit(solution)/shard_map/all_gather | solution.py:116
  145.8 44.6 %copy-start.6 = (bf16[1,2,128,2048]{3,2,1,0:T(8,128)(2,1)}, bf16[1,2,128,2048]{3,2,1,0:T(8,128)(2,1)S(1)}, u32[]{:S(2)}) copy-start(bf16[1,2,128,2048]{3,2,1,0:T(8,128)(2,1)S(1)} %multiply_convert_fusion.5) | copy-start | bytes 3145732
  196.4 199.9 %all-gather.19.cloned.1.call-start = ((), (), s32[]{:S(2)}) async-start(), calls=%async_computation.7 | async-start | bytes 9437184 | tf_op jit(solution)/shard_map/all_gather | solution.py:139
  197.0 362.0 %all-gather.21.cloned.1.call-start = ((), (), s32[]{:S(2)}) async-start(), calls=%async_computation.8 | async-start | bytes 37748736 | tf_op jit(solution)/shard_map/all_gather | solution.py:146
  197.8 61.1 %copy-start.12 = (f32[256,16,64]{0,2,1:T(8,128)S(1)}, f32[256,16,64]{0,2,1:T(8,128)}, u32[]{:S(2)}) copy-start(f32[256,16,64]{0,2,1:T(8,128)} %get-tuple-element.84) | copy-start | bytes 3145732
  197.8 523.9 %all-gather.23.cloned.1.call-start = ((), (), s32[]{:S(2)}) async-start(), calls=%async_computation.9 | async-start | bytes 37748736 | tf_op jit(solution)/shard_map/all_gather | solution.py:147
  198.5 685.9 %all-gather.25.cloned.1.call-start = ((), (), s32[]{:S(2)}) async-start(), calls=%async_computation.10 | async-start | bytes 37748736 | tf_op jit(solution)/shard_map/all_gather | solution.py:153
  199.3 960.7 %reduce-scatter.4.cloned.1.call-start = ((), (), s32[]{:S(2)}) async-start(), calls=%async_computation.11 | async-start | bytes 5242880 | tf_op jit(solution)/shard_map/reduce_scatter | solution.py:212
  351.6 51.1 %copy-start.17 = (bf16[256,16,128]{0,2,1:T(8,128)(2,1)}, bf16[256,16,128]{0,2,1:T(8,128)(2,1)S(1)}, u32[]{:S(2)}) copy-start(bf16[256,16,128]{0,2,1:T(8,128)(2,1)S(1)} %get-tuple-element.101) | copy-start | bytes 3145732
  403.4 318.3 %copy-start.8 = (bf16[256,2048]{1,0:T(8,128)(2,1)}, bf16[256,2048]{1,0:T(8,128)(2,1)S(1)}, u32[]{:S(2)}) copy-start(bf16[256,2048]{1,0:T(8,128)(2,1)S(1)} %fusion.19) | copy-start | bytes 3145732
  945.4 22.0 copy-start.19
  1036.2 158.3 %reduce-scatter.6.cloned.1.call-start = ((), (), s32[]{:S(2)}) async-start(), calls=%async_computation.12 | async-start | bytes 5242880 | tf_op jit(solution)/shard_map/reduce_scatter | solution.py:215
  1045.6 3051.0 %reduce-scatter.8.cloned.1.call-start = ((), (), s32[]{:S(2)}) async-start(), calls=%async_computation.13 | async-start | bytes 276824064 | tf_op jit(solution)/shard_map/reduce_scatter | solution.py:242
  1212.5 23.4 copy-start.21
  (29 other events, 213.2 us)
Sparse Core Ops, SparseCore 0:
  9.9 55.4 all-gather.12
  67.3 54.3 all-gather.14
  123.6 54.3 all-gather.10
  180.0 78.7 all-gather.16
  260.9 79.2 all-gather.26
  341.9 54.3 all-gather.18
  398.2 160.7 all-gather.20
  560.9 160.7 all-gather.22
  723.6 160.7 all-gather.24
  1036.3 78.4 reduce-scatter.3
  1117.2 77.2 reduce-scatter.5
  1304.0 2792.5 reduce-scatter.7
where the time goes:
time: 4130 us; the launch traced here: 4110 us
  waiting for transfers between devices  3530 us (85%)
  matrix products  321 us (8%)
  local copies, waits for them, and re-layouts  184 us (4%)
    reduce_scatter x1, waiting for transfers between devices, body(): lax.psum_scatter(jnp.concatenate([contract_rows(input_one, grad_query_pre...  2770 us
    all_gather x1, waiting for transfers between devices, body(): lax.all_gather(w_gate, 'fsdp', axis=0, tiled=True)  156 us
    all_gather x1, waiting for transfers between devices, body(): lax.all_gather(w_up, 'fsdp', axis=0, tiled=True)  143 us
    all_gather x1, waiting for transfers between devices, body(): lax.all_gather(w_down, 'fsdp', axis=0, tiled=True)  137 us
    dot_general x7, matrix products, contract_rows(): lax.dot_general(left, right, (((0,), (0,)), ((), ())), preferred_element_...  108 us
    dot_general x7, matrix products, fold_forward(): jnp.dot(inputs, shard_rows, preferred_element_type=jnp.float32)  84.6 us
  transfers between devices with their start and end apart: 12, of which 11 were waited for; matrix products, arithmetic and copies ran while one was open for 7% of the time, Pallas kernels for 0%

commit v1 on v0

v1 whole, which is shorter than its diff:
```python
import functools

import jax
import jax.numpy as jnp
from jax import lax
from jax.experimental import pallas as pl
from jax.experimental.pallas import tpu as pltpu
from jax.sharding import PartitionSpec as P

HD = 128
EPS = 1e-05
BF = jnp.bfloat16
F32 = jnp.float32
NEG = -1e30


def normalize(rows):
    centered = rows - jnp.mean(rows, -1, keepdims=True)
    inverse = lax.rsqrt(jnp.mean(centered * centered, -1, keepdims=True) + EPS)
    return centered * inverse, inverse


def norm_back(gradient, normed, inverse):
    centered = gradient - jnp.mean(gradient, -1, keepdims=True)
    return inverse * (centered - normed * jnp.mean(gradient * normed, -1, keepdims=True))


def mm(left, right):
    return jnp.dot(left, right, preferred_element_type=F32)


def mm_t(left, right):
    return lax.dot_general(left, right, (((1,), (1,)), ((), ())), preferred_element_type=F32)


def mm_rows(left, right):
    return lax.dot_general(left, right, (((0,), (0,)), ((), ())), preferred_element_type=F32)


def tables(length):
    frequency = 10000.0 ** (-2.0 * jnp.arange(HD // 2, dtype=F32) / HD)
    phases = jnp.arange(length, dtype=F32)[:, None] * frequency[None, :]
    cosine, sine = jnp.cos(phases), jnp.sin(phases)
    return jnp.concatenate([cosine, cosine], 1), jnp.concatenate([-sine, sine], 1)


def fwd_kernel(heads, order, qkv, cos, sin, out, lse, q_s, k_s, v_s):
    planes, _, slots, blk, _ = qkv.shape
    blocks = planes * slots
    scale = HD ** -0.5

    def head(h, carry):
        col = pl.multiple_of(h * HD, HD)

        def load(b, carry):
            where = order[b]
            s, t = where // slots, where % slots
            row = pl.ds(pl.multiple_of(b * blk, blk), blk)
            c, n = cos[row, :], sin[row, :]
            q = qkv[s, 0, t, :, pl.ds(col, HD)]
            k = qkv[s, 0, t, :, pl.ds(pl.multiple_of(heads * HD + col, HD), HD)]
            q_s[row, :] = ((q * c + pltpu.roll(q, HD // 2, 1) * n) * scale).astype(BF)
            k_s[row, :] = (k * c + pltpu.roll(k, HD // 2, 1) * n).astype(BF)
            v_s[row, :] = qkv[s, 0, t, :, pl.ds(pl.multiple_of(2 * heads * HD + col, HD), HD)].astype(BF)
            return carry

        lax.fori_loop(0, blocks, load, 0)
        for b in range(blocks):
            keys = (b + 1) * blk
            scores = mm_t(q_s[b * blk : keys, :], k_s[0:keys, :])
            top = jnp.max(scores, -1, keepdims=True)
            raised = jnp.exp(scores - top)
            total = jnp.sum(raised, -1, keepdims=True)
            probs = (raised * (1.0 / total)).astype(BF)
            mixed = mm(probs, v_s[0:keys, :])
            where = order[b]
            s, t = where // slots, where % slots
            out[s, 0, t, :, pl.ds(col, HD)] = mixed.astype(BF)
            lse[s, 0, t, :, pl.ds(col, HD)] = jnp.broadcast_to(top + jnp.log(total), (blk, HD))
        return carry

    lax.fori_loop(0, heads, head, 0)


def bwd_kernel(heads, order, qkv, lse, grad, cos, sin, dqkv, q_s, k_s, v_s, g_s, l_s, dk_s, dv_s):
    planes, _, slots, blk, _ = qkv.shape
    blocks = planes * slots
    scale = HD ** -0.5

    def head(h, carry):
        col = pl.multiple_of(h * HD, HD)
        kcol = pl.multiple_of(heads * HD + col, HD)
        vcol = pl.multiple_of(2 * heads * HD + col, HD)

        def load(b, carry):
            where = order[b]
            s, t = where // slots, where % slots
            row = pl.ds(pl.multiple_of(b * blk, blk), blk)
            c, n = cos[row, :], sin[row, :]
            q = qkv[s, 0, t, :, pl.ds(col, HD)]
            k = qkv[s, 0, t, :, pl.ds(kcol, HD)]
            q_s[row, :] = ((q * c + pltpu.roll(q, HD // 2, 1) * n) * scale).astype(BF)
            k_s[row, :] = (k * c + pltpu.roll(k, HD // 2, 1) * n).astype(BF)
            v_s[row, :] = qkv[s, 0, t, :, pl.ds(vcol, HD)].astype(BF)
            g_s[row, :] = grad[s, 0, t, :, pl.ds(col, HD)]
            l_s[row, :] = lse[s, 0, t, :, pl.ds(col, HD)]
            return carry

        lax.fori_loop(0, blocks, load, 0)
        dk_s[...] = jnp.zeros_like(dk_s)
        dv_s[...] = jnp.zeros_like(dv_s)
        for b in range(blocks):
            keys = (b + 1) * blk
            mine = slice(b * blk, keys)
            scores = mm_t(q_s[mine, :], k_s[0:keys, :])
            probs = jnp.exp(scores - l_s[mine, 0:1])
            dprobs = mm_t(g_s[mine, :], v_s[0:keys, :])
            delta = jnp.sum(probs * dprobs, -1, keepdims=True)
            dscores = (probs * (dprobs - delta)).astype(BF)
            dq = mm(dscores, k_s[0:keys, :]) * scale
            dk_s[0:keys, :] += mm_rows(dscores, q_s[mine, :])
            dv_s[0:keys, :] += mm_rows(probs.astype(BF), g_s[mine, :])
            where = order[b]
            s, t = where // slots, where % slots
            dq = dq * cos[mine, :] - pltpu.roll(dq, HD // 2, 1) * sin[mine, :]
            dqkv[s, 0, t, :, pl.ds(col, HD)] = dq.astype(BF)

        def store(b, carry):
            where = order[b]
            s, t = where // slots, where % slots
            row = pl.ds(pl.multiple_of(b * blk, blk), blk)
            dk = dk_s[row, :]
            dk = dk * cos[row, :] - pltpu.roll(dk, HD // 2, 1) * sin[row, :]
            dqkv[s, 0, t, :, pl.ds(kcol, HD)] = dk.astype(BF)
            dqkv[s, 0, t, :, pl.ds(vcol, HD)] = dv_s[row, :].astype(BF)
            return carry

        lax.fori_loop(0, blocks, store, 0)
        return carry

    lax.fori_loop(0, heads, head, 0)


VMEM_LIMIT = 56 * 1024 * 1024


def attend(order, qkv, cos, sin, heads):
    planes, seqs, slots, blk, width = qkv.shape
    length = planes * slots * blk
    spec = lambda w: pl.BlockSpec((planes, 1, slots, blk, w), lambda i, o: (0, i, 0, 0, 0))
    table = pl.BlockSpec((length, HD), lambda i, o: (0, 0))
    return pl.pallas_call(
        functools.partial(fwd_kernel, heads),
        grid_spec=pltpu.PrefetchScalarGridSpec(
            num_scalar_prefetch=1,
            grid=(seqs,),
            in_specs=[spec(width), table, table],
            out_specs=[spec(heads * HD), spec(heads * HD)],
            scratch_shapes=[pltpu.VMEM((length, HD), BF)] * 3,
        ),
        out_shape=[
            jax.ShapeDtypeStruct((planes, seqs, slots, blk, heads * HD), BF),
            jax.ShapeDtypeStruct((planes, seqs, slots, blk, heads * HD), F32),
        ],
        compiler_params=pltpu.CompilerParams(vmem_limit_bytes=VMEM_LIMIT),
        cost_estimate=pl.CostEstimate(
            flops=seqs * heads * length * length * HD * 4, bytes_accessed=seqs * length * width * 6, transcendentals=0
        ),
        name="attend",
    )(order, qkv, cos, sin)


def attend_back(order, qkv, lse, grad, cos, sin, heads):
    planes, seqs, slots, blk, width = qkv.shape
    length = planes * slots * blk
    spec = lambda w: pl.BlockSpec((planes, 1, slots, blk, w), lambda i, o: (0, i, 0, 0, 0))
    table = pl.BlockSpec((length, HD), lambda i, o: (0, 0))
    return pl.pallas_call(
        functools.partial(bwd_kernel, heads),
        grid_spec=pltpu.PrefetchScalarGridSpec(
            num_scalar_prefetch=1,
            grid=(seqs,),
            in_specs=[spec(width), spec(heads * HD), spec(heads * HD), table, table],
            out_specs=spec(width),
            scratch_shapes=[pltpu.VMEM((length, HD), BF)] * 4 + [pltpu.VMEM((length, HD), F32)] * 3,
        ),
        out_shape=jax.ShapeDtypeStruct((planes, seqs, slots, blk, width), BF),
        compiler_params=pltpu.CompilerParams(vmem_limit_bytes=VMEM_LIMIT),
        cost_estimate=pl.CostEstimate(
            flops=seqs * heads * length * length * HD * 10, bytes_accessed=seqs * length * width * 12, transcendentals=0
        ),
        name="attend_back",
    )(order, qkv, lse, grad, cos, sin)


TILE = 256


def up_kernel(count, *refs):
    hs, (wg, wu, wd) = refs[:count], refs[count : count + 3]
    refs = refs[count + 3 :]
    refs = refs[4:] if len(refs) > count + 6 else refs
    h_all, g_out, u_out, hidden_out = refs[:4]
    outs, (held, total) = refs[4 : 4 + count], refs[4 + count :]
    step = pl.program_id(0)
    rows = hs[0].shape[0]

    @pl.when(step == 0)
    def _():
        for i in range(count):
            held[i * rows : (i + 1) * rows, :] = hs[i][...]
        h_all[...] = held[...]
        total[...] = jnp.zeros_like(total)

    h = held[...]
    g, u = mm(h, wg[...]), mm(h, wu[...])
    hidden = (g * (1.0 / (1.0 + jnp.exp(-g))) * u).astype(BF)
    g_out[...], u_out[...], hidden_out[...] = g, u, hidden
    total[...] += mm(hidden, wd[...])

    @pl.when(step == pl.num_programs(0) - 1)
    def _():
        for i in range(count):
            outs[i][...] = total[i * rows : (i + 1) * rows, :].astype(outs[i].dtype)


def mlp(hs, gu_w, down_w, types, parts, which, held=None):
    rows, width = hs[0].shape
    part_ff = down_w.shape[0]
    count, tiles = len(hs), part_ff // TILE
    span = rows * count
    whole = pl.BlockSpec((rows, width), lambda i: (0, 0))
    tile = pl.BlockSpec((span, TILE), lambda i: (which, i))
    kept = [(width, BF), (part_ff, F32), (part_ff, F32), (part_ff, BF)]
    extra = [] if held is None else list(held)
    result = pl.pallas_call(
        functools.partial(up_kernel, count),
        grid=(tiles,),
        in_specs=[whole] * count
        + [
            pl.BlockSpec((width, TILE), lambda i: (0, i)),
            pl.BlockSpec((width, TILE), lambda i: (0, tiles + i)),
            pl.BlockSpec((TILE, width), lambda i: (i, 0)),
        ]
        + [pl.BlockSpec(memory_space=pl.ANY)] * len(extra),
        out_specs=[pl.BlockSpec((span, width), lambda i: (which, 0)), tile, tile, tile] + [whole] * count,
        out_shape=[jax.ShapeDtypeStruct((span * parts, w), t) for w, t in kept]
        + [jax.ShapeDtypeStruct((rows, width), t) for t in types],
        scratch_shapes=[pltpu.VMEM((span, width), BF), pltpu.VMEM((span, width), F32)],
        input_output_aliases={count + 3 + i: i for i in range(len(extra))},
        compiler_params=pltpu.CompilerParams(vmem_limit_bytes=48 * 1024 * 1024),
        cost_estimate=pl.CostEstimate(
            flops=6 * span * width * part_ff, bytes_accessed=6 * width * part_ff + 14 * span * part_ff, transcendentals=0
        ),
        name="mlp",
    )(*hs, gu_w, gu_w, down_w, *extra)
    return result[:4], result[4:]


def down_kernel(count, *refs):
    ds, (g_in, u_in, wg, wu, wd) = refs[:count], refs[count : count + 5]
    refs = refs[count + 5 :]
    refs = refs[3:] if len(refs) > count + 5 else refs
    d_all, dg_out, du_out = refs[:3]
    outs, (held, total) = refs[3 : 3 + count], refs[3 + count :]
    step = pl.program_id(0)
    rows = ds[0].shape[0]

    @pl.when(step == 0)
    def _():
        for i in range(count):
            held[i * rows : (i + 1) * rows, :] = ds[i][...]
        d_all[...] = held[...]
        total[...] = jnp.zeros_like(total)

    dh = mm_t(held[...], wd[...])
    g = g_in[...]
    sig = 1.0 / (1.0 + jnp.exp(-g))
    dg = (dh * u_in[...] * sig * (1.0 + g * (1.0 - sig))).astype(BF)
    du = (dh * (g * sig)).astype(BF)
    dg_out[...], du_out[...] = dg, du
    total[...] += mm_t(dg, wg[...]) + mm_t(du, wu[...])

    @pl.when(step == pl.num_programs(0) - 1)
    def _():
        for i in range(count):
            outs[i][...] = total[i * rows : (i + 1) * rows, :].astype(outs[i].dtype)


def mlp_back(ds, g, u, gu_w, down_w, types, parts, which, held=None):
    rows, width = ds[0].shape
    part_ff = down_w.shape[0]
    count, tiles = len(ds), part_ff // TILE
    span = rows * count
    whole = pl.BlockSpec((rows, width), lambda i: (0, 0))
    tile = pl.BlockSpec((span, TILE), lambda i: (which, i))
    kept = [(width, BF), (part_ff, BF), (part_ff, BF)]
    extra = [] if held is None else list(held)
    result = pl.pallas_call(
        functools.partial(down_kernel, count),
        grid=(tiles,),
        in_specs=[whole] * count
        + [
            tile,
            tile,
            pl.BlockSpec((width, TILE), lambda i: (0, i)),
            pl.BlockSpec((width, TILE), lambda i: (0, tiles + i)),
            pl.BlockSpec((TILE, width), lambda i: (i, 0)),
        ]
        + [pl.BlockSpec(memory_space=pl.ANY)] * len(extra),
        out_specs=[pl.BlockSpec((span, width), lambda i: (which, 0)), tile, tile] + [whole] * count,
        out_shape=[jax.ShapeDtypeStruct((span * parts, w), t) for w, t in kept]
        + [jax.ShapeDtypeStruct((rows, width), t) for t in types],
        scratch_shapes=[pltpu.VMEM((span, width), BF), pltpu.VMEM((span, width), F32)],
        input_output_aliases={count + 5 + i: i for i in range(len(extra))},
        compiler_params=pltpu.CompilerParams(vmem_limit_bytes=48 * 1024 * 1024),
        cost_estimate=pl.CostEstimate(
            flops=6 * span * width * part_ff, bytes_accessed=6 * width * part_ff + 12 * span * part_ff, transcendentals=0
        ),
        name="mlp_back",
    )(*ds, g, u, gu_w, gu_w, down_w, *extra)
    return result[:3], result[3:]


def assemble(places, pieces):
    count = len(pieces)
    depth, width = pieces[0].shape

    def kernel(places, *refs):
        sources, out, held, arrive, leave = refs[:count], *refs[count:]
        ins = [pltpu.make_async_copy(sources[i], held.at[i], arrive.at[i]) for i in range(count)]
        outs = [pltpu.make_async_copy(held.at[i], out.at[places[i]], leave.at[i]) for i in range(count)]
        for copy in ins:
            copy.start()
        for i in range(count):
            ins[i].wait()
            outs[i].start()
        for copy in outs:
            copy.wait()

    return pl.pallas_call(
        kernel,
        grid_spec=pltpu.PrefetchScalarGridSpec(
            num_scalar_prefetch=1,
            grid=(1,),
            in_specs=[pl.BlockSpec(memory_space=pl.ANY)] * count,
            out_specs=pl.BlockSpec(memory_space=pl.ANY),
            scratch_shapes=[
                pltpu.VMEM((count, depth, width), pieces[0].dtype),
                pltpu.SemaphoreType.DMA((count,)),
                pltpu.SemaphoreType.DMA((count,)),
            ],
        ),
        out_shape=jax.ShapeDtypeStruct((count, depth, width), pieces[0].dtype),
        compiler_params=pltpu.CompilerParams(vmem_limit_bytes=VMEM_LIMIT),
        name="assemble",
    )(places, *pieces).reshape(count * depth, width)


def take_columns(which, arrays, groups, members):
    depth, width = arrays[0].shape
    part = width // (groups * members)
    kept = len(which)
    if part % HD:
        views = [v.reshape(depth, groups, members, part) for v in arrays]
        return [
            jnp.concatenate(
                [lax.dynamic_slice_in_dim(v, k, 1, 2).reshape(depth, groups * part) for v in views], 1
            )
            for k in which
        ]

    def kernel(which, *refs):
        sources, outs = refs[: len(arrays)], refs[len(arrays) :]
        for k in range(kept):
            for n, source in enumerate(sources):
                for i in range(groups):
                    start = pl.multiple_of(i * members * part + which[k] * part, HD)
                    outs[k][:, (n * groups + i) * part : (n * groups + i + 1) * part] = source[:, pl.ds(start, part)]

    tile = min(64, depth)
    return pl.pallas_call(
        kernel,
        grid_spec=pltpu.PrefetchScalarGridSpec(
            num_scalar_prefetch=1,
            grid=(depth // tile,),
            in_specs=[pl.BlockSpec((tile, width), lambda i, w: (i, 0))] * len(arrays),
            out_specs=[pl.BlockSpec((tile, len(arrays) * groups * part), lambda i, w: (i, 0))] * kept,
        ),
        out_shape=[jax.ShapeDtypeStruct((depth, len(arrays) * groups * part), arrays[0].dtype)] * kept,
        name="take_columns",
    )(jnp.stack(which).astype(jnp.int32), *arrays)


def body(planes, shards, tokens, pairs, valid, teacher, w_query, w_key, w_value, w_out, w_gate, w_up, w_down):
    seqs, slots, blk, width = tokens.shape
    ff = w_gate.shape[1]
    rows = seqs * slots * blk
    world = planes * shards
    near = planes // 2
    all_heads = width // HD
    heads = all_heads // planes
    mine = heads * HD
    own_rows = width // shards
    part_ff = ff // planes
    length = planes * slots * blk
    unit = width // world
    both = ("ctx", "fsdp")

    c, f = lax.axis_index("ctx"), lax.axis_index("fsdp")
    far, low = c // near, c % near
    core, x, y = f % 2, f // 2 % 2, f // 4
    group = x * near + low

    def after(array, *others):
        return lax.optimization_barrier((array, *others))[0]

    def flip(array, bits):
        return lax.ppermute(array, "fsdp", [(i, i ^ bits) for i in range(shards)])

    def flip_ctx(array, bits):
        return lax.ppermute(array, "ctx", [(i, i ^ bits) for i in range(planes)])

    def hop(array, j):
        dx, dz = j // near, j % near
        if dz == 0:
            return flip(array, 2 * dx)
        if dx == 0:
            return flip_ctx(array, dz)
        return lax.ppermute(
            array,
            both,
            [(p * shards + s, (p ^ dz) * shards + (s ^ 2)) for p in range(planes) for s in range(shards)],
        )

    def swap(array):
        pairs_of = []
        for p in range(planes):
            for s in range(shards):
                to = (s // 2 % 2) * near + p % near
                pairs_of.append((p * shards + s, to * shards + (s - s // 2 % 2 * 2 + p // near * 2)))
        return lax.ppermute(array, both, pairs_of)

    cos, sin = tables(length)
    ranks = jnp.argsort(pairs.reshape(-1))
    owner = ranks // slots
    relative = ((owner // near) ^ x) * near + ((owner % near) ^ low)
    order = (relative * slots + ranks % slots).astype(jnp.int32)

    def over_y(piece):
        return [flip(piece, bits) for bits in range(4, shards, 4)]

    def put(own, own_y, other, other_y):
        pieces = [own, *own_y, other, *other_y]
        keys = [0, *range(4, shards, 4), 2, *range(6, shards, 4)]
        pieces += [flip(piece, 1) for piece in pieces]
        places = jnp.stack([f ^ k for k in keys] + [f ^ k ^ 1 for k in keys]).astype(jnp.int32)
        return assemble(places, pieces)

    def head_columns(g):
        return jnp.concatenate(
            [lax.dynamic_slice_in_dim(w, g * mine, mine, 1) for w in (w_query, w_key, w_value)], 1
        )

    def ff_rows(g):
        return lax.dynamic_slice_in_dim(w_down, g * (part_ff // shards), part_ff // shards, 0)

    def own_heads(weight):
        sends, spreads = [], {}
        for p in range(planes):
            for s in range(shards):
                q = s // 2
                if q % near == p % near:
                    at = s // 4 * 4 + q // near * 2 + s % 2
                    sends.append((p * shards + s, p * shards + at))
                    for d in range(4, shards, 4):
                        spreads.setdefault(d, []).append((p * shards + at, p * shards + (at ^ d)))
        first = lax.ppermute(weight, both, sends)
        found = first
        for pairs_of in spreads.values():
            found = found + lax.ppermute(first, both, pairs_of)
        other, even = flip(found, 1), core == 0
        return jnp.concatenate([jnp.where(even, found, other), jnp.where(even, other, found)], 0)

    def gather_group(own):
        return [own] + [hop(own, j) for j in range(1, planes)]

    def reduce_group(parts):
        total = parts[0]
        for j in reversed(range(1, planes)):
            total = total + hop(parts[j].astype(BF), j).astype(F32)
        return total

    cut = planes // 2
    early = list(range(1, cut + 1))
    late = [0, *range(cut + 1, planes)]
    early_types = [BF] * cut
    late_types = [F32] + [BF] * (planes - cut - 1)
    places = early + late
    back_to = [places.index(j) for j in range(planes)]

    valid_home = valid.reshape(rows, 1)
    stream_low = swap(tokens.reshape(rows, width))
    qkv_own = head_columns(group)
    qkv_other = flip(head_columns(group ^ near), 2)
    w_qkv = put(qkv_own, over_y(qkv_own), qkv_other, over_y(qkv_other))
    valid_float = swap(after(valid_home, stream_low)).astype(F32)
    gu_own, gu_send = take_columns([group, group ^ near], [w_gate, w_up], shards, planes)

    stream = stream_low.astype(F32)
    normed_one, inverse_one = normalize(stream)
    h1 = gather_group(normed_one.astype(BF))
    gu_own_y = over_y(gu_own)
    w_out_mine = own_heads(after(w_out, *h1))
    qkv = jnp.stack([mm(h, w_qkv).reshape(seqs, slots, blk, 3 * mine) for h in h1], 0)
    gu_other = flip(after(gu_send, *h1), 2)
    qkv, w_out_mine, *gu_own_y = lax.optimization_barrier((qkv, w_out_mine, *gu_own_y))
    mixed, lse = attend(order, qkv, cos, sin, heads)
    mixed, gu_other = lax.optimization_barrier((mixed, gu_other))
    gu_other_y = over_y(gu_other)
    down_own = ff_rows(group)
    down_own_y = over_y(after(down_own, mixed))
    down_other = flip(after(ff_rows(group ^ near), gu_other), 2)
    products = [mm(mixed[s].reshape(rows, mine), w_out_mine) for s in range(planes)]
    residual = stream + reduce_group(products)

    normed_two, inverse_two = normalize(residual)
    h2 = gather_group(normed_two.astype(BF))
    gu_w = put(gu_own, gu_own_y, gu_other, gu_other_y)
    down_w = put(down_own, down_own_y, down_other, over_y(down_other))
    goal_low = swap(after(teacher, *h2).reshape(rows, width))
    kept, outs = mlp([h2[j] for j in early], gu_w, down_w, early_types, 2, 0)
    (h2_all, gates, ups, hidden_all), more = mlp([h2[j] for j in late], gu_w, down_w, late_types, 2, 1, kept)
    outs = [*outs, *more]
    output = residual + reduce_group([outs[i] for i in back_to])

    deviation = output - goal_low.astype(F32)
    grad_output = valid_float * deviation
    sums = jnp.stack([jnp.sum(grad_output * deviation), jnp.sum(valid_float)])
    sums0 = jnp.broadcast_to(sums[:, None, None], (2, 8, HD))

    for bits in range(1, planes):
        sums = sums + hop(sums0, bits) if bits > 1 else sums0 + hop(sums0, bits)
    low_grad, sums = lax.optimization_barrier((grad_output.astype(BF), sums))

    steps = [1 << b for b in reversed(range(2, shards.bit_length() - 1))]

    def halve(part, axis, bit, move, bits):
        half = part.shape[axis] // 2
        take = lambda k: lax.dynamic_slice_in_dim(part, k * half, half, axis)
        away = move(take(1 - bit), bits)
        return (take(bit).astype(F32) + away.astype(F32)).astype(BF)

    def half_of(v, k):
        return lax.dynamic_slice_in_dim(v, k * (v.shape[1] // 2), v.shape[1] // 2, 1)

    def over_core(compute):
        away = flip(compute(1 - core).astype(BF), 1)
        return (compute(core) + away.astype(F32)).astype(BF)

    def by_rows(left, right):
        return over_core(lambda k: mm_rows(half_of(left, k), right))

    def by_columns(left, right):
        part = over_core(lambda k: mm_rows(left, half_of(right, k)))
        return part.reshape(2, near, shards // 4, 2, 2, unit, part.shape[1])

    def across_y(part, axis):
        for step in steps:
            part = halve(part, axis, f // step % 2, flip, step)
        return part

    def across_far(part):
        return halve(part, 0, far, flip_ctx, near)

    def place_rows(part, place):
        homes = []
        for p in range(planes):
            for s in range(shards):
                block = ((s % 2) * (shards // 4) + s // 4) * 2 + p // near
                homes.append((p * shards + s, place(block, (s // 2 % 2) * near + p % near)))
        return lax.ppermute(part, both, homes).astype(F32)

    def place_columns(part, columns):
        half = part.shape[-1]
        part = part.reshape(near, 2, 2, unit, half)
        take = lambda v, k, axis: lax.dynamic_index_in_dim(v, k, axis, keepdims=False)
        keep, away = take(part, core, 2), flip(take(part, 1 - core, 2), 1)
        even = core == 0
        part = jnp.concatenate([jnp.where(even, keep, away), jnp.where(even, away, keep)], -1)
        pieces = []
        for j in range(planes):
            piece = take(take(part, x ^ (j // near), 1), low ^ (j % near), 0)
            pieces.append(hop(piece, j) if j else piece)
        places = jnp.stack([group ^ j for j in range(planes)]).astype(jnp.int32)
        return columns(assemble(places, pieces).reshape(planes, unit, 2 * half)).astype(F32)

    dm = gather_group(low_grad)
    for bits in [1, *(1 << b for b in range(2, shards.bit_length() - 1))]:
        sums = sums + flip(sums, bits)
    dm[1], sums = lax.optimization_barrier((dm[1], sums))
    kept, backs = mlp_back([dm[j] for j in early], gates, ups, gu_w, down_w, early_types, 2, 0)
    kept, sums = lax.optimization_barrier((kept, sums))
    sums = sums + flip_ctx(sums, near)
    (dm_all, dg_all, du_all), more = mlp_back(
        [dm[j] for j in late], gates, ups, gu_w, down_w, late_types, 2, 1, kept
    )
    backs = [*backs, *more]
    received = [hop(backs[back_to[j]], j) for j in range(1, planes)]
    g_down = by_rows(hidden_all, dm_all)
    g_gate = by_columns(h2_all, dg_all)
    g_up = by_columns(h2_all, du_all)
    received, g_down, g_gate, g_up, sums = lax.optimization_barrier((received, g_down, g_gate, g_up, sums))
    grad_two = backs[back_to[0]]
    for v in received:
        grad_two = grad_two + v.astype(F32)
    activations = swap(after(output, *received).astype(BF))
    grad_residual = grad_output + norm_back(grad_two, normed_two, inverse_two)

    dab = gather_group(grad_residual.astype(BF))
    g_down = across_y(g_down, 0)
    g_gate = across_y(g_gate, 2)
    dab, g_down, g_gate = lax.optimization_barrier((dab, g_down, g_gate))
    do = jnp.stack([mm_t(d, w_out_mine).astype(BF).reshape(seqs, slots, blk, mine) for d in dab], 0)
    g_up = across_y(g_up, 2)
    g_down = across_far(g_down)
    dqkv = attend_back(order, qkv, lse, do, cos, sin, heads)
    dqkv, g_up, g_down, activations = lax.optimization_barrier((dqkv, g_up, g_down, activations))
    count = sums[1, 0, 0]
    loss = sums[0, 0, 0] / (count * width)
    factor = (rows * world) / count
    backs = [mm_t(dqkv[s].reshape(rows, 3 * mine), w_qkv) for s in range(planes)]
    backs = [v if i == 0 else v.astype(BF) for i, v in enumerate(backs)]
    dqkv, backs, h1_all, dab_all = lax.optimization_barrier(
        (dqkv, backs, jnp.concatenate(h1, 0), jnp.concatenate(dab, 0))
    )
    g_qkv = by_columns(h1_all, dqkv.reshape(planes * rows, 3 * mine))
    g_out = by_rows(mixed.reshape(planes * rows, mine), dab_all)
    g_gate = across_far(g_gate)
    g_up = across_far(g_up)
    grad_one = reduce_group(backs)
    grad_stream = grad_residual + norm_back(grad_one, normed_one, inverse_one)
    g_qkv = across_y(g_qkv, 2)
    g_out = across_y(g_out, 0)
    low_stream, g_gate, g_up, g_qkv, g_out = lax.optimization_barrier(
        (grad_stream.astype(BF), g_gate, g_up, g_qkv, g_out)
    )
    grad_input = swap(low_stream).astype(F32) * factor

    g_qkv = across_far(g_qkv)
    g_out = across_far(g_out)
    g_down = place_rows(
        g_down, lambda block, g: ((ff // shards) * block + (ff // world) * g) // (ff // world)
    )
    ff_order = lambda v: v.reshape(planes, unit, shards, -1).transpose(1, 2, 0, 3).reshape(unit, ff)
    g_gate = place_columns(g_gate, ff_order)
    g_up = place_columns(g_up, ff_order)
    g_qkv = place_columns(g_qkv, lambda v: v.reshape(planes, unit, 3, mine).transpose(2, 1, 0, 3).reshape(3, unit, width))
    g_out = place_rows(g_out, lambda block, g: g * shards + block)
    return (
        activations.reshape(tokens.shape),
        loss,
        grad_input.reshape(tokens.shape),
        g_qkv[0] * factor,
        g_qkv[1] * factor,
        g_qkv[2] * factor,
        g_out * factor,
        g_gate * factor,
        g_up * factor,
        g_down * factor,
    )


def solution(mesh):
    tokens = P("fsdp", "ctx", None, None)
    weight = P("fsdp", None)
    grad = P(("ctx", "fsdp"), None)
    in_specs = (tokens, P(), P("fsdp", "ctx", None), tokens) + (weight,) * 7
    out_specs = (tokens, P(), tokens) + (grad,) * 7
    step = functools.partial(body, mesh.shape["ctx"], mesh.shape["fsdp"])
    return jax.shard_map(step, mesh=mesh, in_specs=in_specs, out_specs=out_specs, check_vma=False)
```

time: 4130 us -> 1190 us (0.29)
  waiting for transfers between devices: 3530 us -> 655 us
  matrix products: 321 us -> 95.7 us
  Pallas kernels: 0 us -> 197 us
  local copies, waits for them, and re-layouts: 184 us -> 40 us
  starting transfers between devices: 0.64 us -> 126 us
    reduce_scatter x3 -> x0, waiting for transfers between devices: 2790 us -> none  [the longest x1 2770 us: body(): lax.psum_scatter(jnp.concatenate([contract_rows(input_one, grad_query_pre...]
    all_gather x9 -> x0, waiting for transfers between devices: 734 us -> none  [the longest x1 156 us: body(): lax.all_gather(w_gate, 'fsdp', axis=0, tiled=True)]
    ppermute x0 -> x88, waiting for transfers between devices: none -> 655 us  [the longest x49 298 us: flip(): return lax.ppermute(array, 'fsdp', [(i, i ^ bits) for i in range(shards)])]
    dot_general x27 -> x26, matrix products: 321 us -> 95.7 us  [the longest x10 60.6 us: mm_rows(): lax.dot_general(left, right, (((0,), (0,)), ((), ())), preferred_element_...]
    pallas_call x0 -> x13, Pallas kernels: none -> 197 us  [the longest x2 65.5 us: mlp_back(): pl.pallas_call(functools.partial(down_kernel, count), grid=(tiles,), in_s...]
    ppermute x0 -> x88, starting transfers between devices: none -> 126 us  [the longest x49 37.8 us: flip(): return lax.ppermute(array, 'fsdp', [(i, i ^ bits) for i in range(shards)])]
    reshape x3 -> x1, local copies, waits for them, and re-layouts: 81.6 us -> 0.09 us  [body(): ranks = jnp.argsort(pairs.reshape(-1))]
    concatenate x1 -> x0, local copies, waits for them, and re-layouts: 44.3 us -> none  [body(): jnp.concatenate([contract_rows(input_one, grad_query_pre), contract_rows(...]
  transfers between devices with their start and end apart: 12 -> 88, of which waited for: 11 -> 35; matrix products, arithmetic and copies ran while one was open for 7% -> 13% of each run, Pallas kernels for 0% -> 14%
where the time goes in v1:
time: 1190 us; the launch traced here: 1170 us
  waiting for transfers between devices  655 us (55%)
  Pallas kernels  197 us (17%)
  starting transfers between devices  126 us (11%)
  matrix products  95.7 us (8%)
  other arithmetic  51.6 us (4%)
  local copies, waits for them, and re-layouts  40 us (3%)
    ppermute x49, waiting for transfers between devices, flip(): return lax.ppermute(array, 'fsdp', [(i, i ^ bits) for i in range(shards)])  298 us
    ppermute x18, waiting for transfers between devices, flip_ctx(): return lax.ppermute(array, 'ctx', [(i, i ^ bits) for i in range(planes)])  182 us
    pallas_call x2, Pallas kernels, mlp_back(): pl.pallas_call(functools.partial(down_kernel, count), grid=(tiles,), in_s...  65.5 us
    ppermute x5, waiting for transfers between devices, swap(): return lax.ppermute(array, both, pairs_of)  62.9 us
    dot_general x10, matrix products, mm_rows(): lax.dot_general(left, right, (((0,), (0,)), ((), ())), preferred_element_...  60.6 us
    ppermute x1, waiting for transfers between devices, own_heads(): found = found + lax.ppermute(first, both, pairs_of)  51.3 us
    pallas_call x2, Pallas kernels, mlp(): pl.pallas_call(functools.partial(up_kernel, count), grid=(tiles,), in_spe...  42 us
    ppermute x49, starting transfers between devices, flip(): return lax.ppermute(array, 'fsdp', [(i, i ^ bits) for i in range(shards)])  37.8 us
  transfers between devices with their start and end apart: 88, of which 35 were waited for; matrix products, arithmetic and copies ran while one was open for 13% of the time, Pallas kernels for 14%

profile of v1, /device:TPU:16, one launch (start us, length us, event | category | flops | bytes accessed | tf_op | source)
XLA Modules:
  0.0 1170.4 jit_solution(674691823939149886)
XLA Ops:
  6.5 42.5 %collective-permute-done = bf16[256,2048]{1,0:T(8,128)(2,1)S(1)} collective-permute-done((bf16[256,2048]{1,0:T(8,128)(2,1)}, bf16[256,2048]{1,0:T(8,128)(2,1)S(1)}, u32[]{:S(2)}, u32[]{:S(2)}) %collective-permute-start) | collective-permute-done | bytes 1048608 | tf_op jit(solution)/shard_map/ppermute | solution.py:442
  58.3 19.0 %collective-permute-done.10 = bf16[256,2048]{1,0:T(8,128)(2,1)S(1)} collective-permute-done((bf16[256,2048]{1,0:T(8,128)(2,1)S(1)}, bf16[256,2048]{1,0:T(8,128)(2,1)S(1)}, u32[]{:S(2)}, u32[]{:S(2)}) %collective-permute-start.10) | collective-permute-done | bytes 1048608 | tf_op jit(solution)/shard_map/ppermute | solution.py:430
  77.3 22.1 %collective-permute-done.9 = bf16[256,2048]{1,0:T(8,128)(2,1)S(1)} collective-permute-done((bf16[256,2048]{1,0:T(8,128)(2,1)S(1)}, bf16[256,2048]{1,0:T(8,128)(2,1)S(1)}, u32[]{:S(2)}, u32[]{:S(2)}) %collective-permute-start.9) | collective-permute-done | bytes 1048608 | tf_op jit(solution)/shard_map/ppermute | solution.py:419
  140.7 51.3 %collective-permute-done.12 = bf16[256,2048]{1,0:T(8,128)(2,1)S(1)} collective-permute-done((bf16[256,2048]{1,0:T(8,128)(2,1)}, bf16[256,2048]{1,0:T(8,128)(2,1)S(1)}, u32[]{:S(2)}, u32[]{:S(2)}) %collective-permute-start.12) | collective-permute-done | bytes 1048608 | tf_op jit(solution)/shard_map/ppermute | solution.py:481
  200.8 21.6 %attend.1 = (bf16[4,1,2,128,512]{4,3,2,1,0:T(8,128)(2,1)}, f32[4,1,2,128,512]{4,3,2,1,0:T(8,128)}) custom-call(s32[8]{0:T(128)} %fusion.68.order, f32[4,1,2,128,1536]{4,3,2,1,0:T(8,128)} %pad_maximum_fusion.qkv, f32[1024,128]{1,0:T(8,128)} %get-tuple-element.220.cos, f32[1024,128]{1,0:T(8,128)} %get-tuple-element.221.sin), custom_call_target="tpu_custom_call" | custom-call | flops 2147483648 | bytes 9437184 | tf_op jit(solution)/shard_map/attend/pallas_call | solution.py:152
  253.9 24.5 %collective-permute-done.18 = bf16[256,2048]{1,0:T(8,128)(2,1)S(1)} collective-permute-done((bf16[256,2048]{1,0:T(8,128)(2,1)}, bf16[256,2048]{1,0:T(8,128)(2,1)S(1)}, u32[]{:S(2)}, u32[]{:S(2)}) %collective-permute-start.18) | collective-permute-done | bytes 1048608 | tf_op jit(solution)/shard_map/ppermute | solution.py:419
  284.1 22.3 %collective-permute-done.26.refs_1_ = bf16[256,2048]{1,0:T(8,128)(2,1)S(1)} collective-permute-done((bf16[256,2048]{1,0:T(8,128)(2,1)S(1)}, bf16[256,2048]{1,0:T(8,128)(2,1)S(1)}, u32[]{:S(2)}, u32[]{:S(2)}) %collective-permute-start.26) | collective-permute-done | bytes 1048608 | tf_op jit(solution)/shard_map/ppermute | solution.py:419
  309.7 38.5 %collective-permute-done.34.refs_1_ = bf16[256,2048]{1,0:T(8,128)(2,1)S(1)} collective-permute-done((bf16[256,2048]{1,0:T(8,128)(2,1)S(1)}, bf16[256,2048]{1,0:T(8,128)(2,1)S(1)}, u32[]{:S(2)}, u32[]{:S(2)}) %collective-permute-start.34) | collective-permute-done | bytes 1048608 | tf_op jit(solution)/shard_map/ppermute | solution.py:419
  379.7 21.0 %mlp.2 = (bf16[1024,2048]{1,0:T(8,128)(2,1)}, f32[1024,2048]{1,0:T(8,128)}, f32[1024,2048]{1,0:T(8,128)}, bf16[1024,2048]{1,0:T(8,128)(2,1)}, bf16[256,2048]{1,0...) custom-call(bf16[256,2048]{1,0:T(8,128)(2,1)S(1)} %collective-permute-done.33.refs_0_, ...), custom_call_target="tpu_custom_call" | custom-call | flops 12884901888 | bytes 39845888 | tf_op jit(solution)/shard_map/mlp/pallas_call | solution.py:236
  402.4 21.0 %mlp.3 = (bf16[1024,2048]{1,0:T(8,128)(2,1)}, f32[1024,2048]{1,0:T(8,128)}, f32[1024,2048]{1,0:T(8,128)}, bf16[1024,2048]{1,0:T(8,128)(2,1)}, f32[256,2048]{1,0:T(8,128)S(1)}, /*index=5*/bf16[256,2048]{1,0:T(8,128)(2,1)S(1)}) custom-call(bf16[256,2048]{1,0:T(8,128)(2,1)S(1)} %fusion.20.refs_0_, ...), custom_call_target="tpu_custom_call", output_to_operand_aliasing={{0}: (5, {}), {1}: (6, {}), {2}: (7, {}), {3}: (8, {})} | custom-call | flops 12884901888 | bytes 39845888 | tf_op jit(solution)/shard_map/mlp/pallas_call | solution.py:236
  430.7 20.3 %collective-permute-done.15 = s32[256,1]{0,1:T(1,128)S(1)} collective-permute-done((s32[256,1]{0,1:T(1,128)S(1)}, s32[256,1]{0,1:T(1,128)S(1)}, u32[]{:S(2)}, u32[]{:S(2)}) %collective-permute-start.15) | collective-permute-done | bytes 1056 | tf_op jit(solution)/shard_map/ppermute | solution.py:442
  468.9 20.7 %collective-permute-done.43.refs_0_ = bf16[256,2048]{1,0:T(8,128)(2,1)S(1)} collective-permute-done((bf16[256,2048]{1,0:T(8,128)(2,1)S(1)}, bf16[256,2048]{1,0:T(8,128)(2,1)S(1)}, u32[]{:S(2)}, u32[]{:S(2)}) %collective-permute-start.43) | collective-permute-done | bytes 1048608 | tf_op jit(solution)/shard_map/ppermute | solution.py:422
  489.6 20.2 %collective-permute-done.46.refs_1_ = bf16[256,2048]{1,0:T(8,128)(2,1)S(1)} collective-permute-done((bf16[256,2048]{1,0:T(8,128)(2,1)S(1)}, bf16[256,2048]{1,0:T(8,128)(2,1)S(1)}, u32[]{:S(2)}, u32[]{:S(2)}) %collective-permute-start.46) | collective-permute-done | bytes 1048608 | tf_op jit(solution)/shard_map/ppermute | solution.py:419
  509.8 36.5 %mlp_back.2 = (bf16[1024,2048]{1,0:T(8,128)(2,1)}, bf16[1024,2048]{1,0:T(8,128)(2,1)}, bf16[1024,2048]{1,0:T(8,128)(2,1)}, bf16[256,2048]{1,0:T(8,128)(2,1)S(1)}, bf16[256,2048]{1,0:T(8,128)(2,1)S(1)}) custom-call(bf16[256,2048]{1,0:T(8,128)(2,1)S(1)} %collective-permute-done.43.refs_0_, bf16[256,2048]{1,0:T(8,128)(2,1)S(1)} %collective-permute-done.46.refs_1_, ...), custom_call_target="tpu_custom_call" | custom-call | flops 12884901888 | bytes 37748736 | tf_op jit(solution)/shard_map/mlp_back/pallas_call | solution.py:299
  547.3 29.0 %mlp_back.3 = (bf16[1024,2048]{1,0:T(8,128)(2,1)}, bf16[1024,2048]{1,0:T(8,128)(2,1)}, bf16[1024,2048]{1,0:T(8,128)(2,1)}, f32[256,2048]{1,0:T(8,128)S(1)}, bf16[256,2048]{1,0:T(8,128)(2,1)S(1)}) custom-call(bf16[256,2048]{1,0:T(8,128)(2,1)S(1)} %multiply_convert_fusion.refs_0_, ...), custom_call_target="tpu_custom_call", output_to_operand_aliasing={{0}: (7, {}), {1}: (8, {}), {2}: (9, {})} | custom-call | flops 12884901888 | bytes 37748736 | tf_op jit(solution)/shard_map/mlp_back/pallas_call | solution.py:299
  628.2 21.6 %collective-permute-done.48 = bf16[256,2048]{1,0:T(8,128)(2,1)S(1)} collective-permute-done((bf16[256,2048]{1,0:T(8,128)(2,1)S(1)}, bf16[256,2048]{1,0:T(8,128)(2,1)S(1)}, u32[]{:S(2)}, u32[]{:S(2)}) %collective-permute-start.48) | collective-permute-done | bytes 1048608 | tf_op jit(solution)/shard_map/ppermute | solution.py:419
  666.5 35.1 %collective-permute-done.58 = bf16[2,2,1,2,2,64,1024]{6,5,4,3,2,1,0:T(8,128)(2,1)S(1)} collective-permute-done((bf16[2,2,1,2,2,64,1024]{6,5,4,3,2,1,0:T(8,128)(2,1)}, bf16[2,2,1,2,2,64,1024]{6,5,4,3,2,1,0:T(8,128)(2,1)S(1)}, u32[]{:S(2)}, u32[]{:S(2)}) %collective-permute-start.58) | collective-permute-done | bytes 2097184 | tf_op jit(solution)/shard_map/ppermute | solution.py:419
  702.9 43.7 %collective-permute-done.57 = bf16[512,2048]{1,0:T(8,128)(2,1)S(1)} collective-permute-done((bf16[512,2048]{1,0:T(8,128)(2,1)S(1)}, bf16[512,2048]{1,0:T(8,128)(2,1)S(1)}, u32[]{:S(2)}, u32[]{:S(2)}) %collective-permute-start.57) | collective-permute-done | bytes 2097184 | tf_op jit(solution)/shard_map/ppermute | solution.py:419
  757.9 31.0 %collective-permute-done.59 = bf16[2,2,1,2,2,64,1024]{6,5,4,3,2,1,0:T(8,128)(2,1)S(1)} collective-permute-done((bf16[2,2,1,2,2,64,1024]{6,5,4,3,2,1,0:T(8,128)(2,1)S(1)}, bf16[2,2,1,2,2,64,1024]{6,5,4,3,2,1,0:T(8,128)(2,1)S(1)}, u32[]{:S(2)}, u32[]{:S(2)}) %collective-permute-start.59) | collective-permute-done | bytes 2097184 | tf_op jit(solution)/shard_map/ppermute | solution.py:419
  794.3 27.2 %attend_back.1 = bf16[4,1,2,128,1536]{4,3,2,1,0:T(8,128)(2,1)} custom-call(s32[8]{0:T(128)} %fusion.68.order, f32[4,1,2,128,1536]{4,3,2,1,0:T(8,128)} %pad_maximum_fusion.qkv, f32[4,1,2,128,512]{4,3,2,1,0:T(8,128)} %get-tuple-element.90.lse, bf16[4,1,2,128,512]{4,3,2,1,0:T(8,128)(2,1)} %pad_maximum_fusion.4.grad, f32[1024,128]{1,0:T(8,128)} %get-tuple-element.220.cos, ...), custom_call_target="tpu_custom_call" | custom-call | flops 5368709120 | bytes 18874368 | tf_op jit(solution)/shard_map/attend_back/pallas_call | solution.py:178
  821.4 36.5 %collective-permute-done.60 = bf16[256,2048]{1,0:T(8,128)(2,1)} collective-permute-done((bf16[256,2048]{1,0:T(8,128)(2,1)}, bf16[256,2048]{1,0:T(8,128)(2,1)}, u32[]{:S(2)}, u32[]{:S(2)}) %collective-permute-start.60) | collective-permute-done | bytes 1048608 | tf_op jit(solution)/shard_map/ppermute | solution.py:422
  899.3 33.6 %collective-permute-done.64 = bf16[256,2048]{1,0:T(8,128)(2,1)S(1)} collective-permute-done((bf16[256,2048]{1,0:T(8,128)(2,1)}, bf16[256,2048]{1,0:T(8,128)(2,1)S(1)}, u32[]{:S(2)}, u32[]{:S(2)}) %collective-permute-start.64) | collective-permute-done | bytes 1048608 | tf_op jit(solution)/shard_map/ppermute | solution.py:422
  979.2 25.7 %collective-permute-done.68 = bf16[2,2,1,2,2,64,768]{6,5,4,3,2,1,0:T(8,128)(2,1)S(1)} collective-permute-done((bf16[2,2,1,2,2,64,768]{6,5,4,3,2,1,0:T(8,128)(2,1)S(1)}, bf16[2,2,1,2,2,64,768]{6,5,4,3,2,1,0:T(8,128)(2,1)S(1)}, u32[]{:S(2)}, u32[]{:S(2)}) %collective-permute-start.68) | collective-permute-done | bytes 1572896 | tf_op jit(solution)/shard_map/ppermute | solution.py:419
  1025.5 64.8 %collective-permute-done.77 = bf16[64,2048]{1,0:T(8,128)(2,1)S(1)} collective-permute-done((bf16[64,2048]{1,0:T(8,128)(2,1)S(1)}, bf16[64,2048]{1,0:T(8,128)(2,1)S(1)}, u32[]{:S(2)}, u32[]{:S(2)}) %collective-permute-start.77) | collective-permute-done | bytes 262176 | tf_op jit(solution)/shard_map/ppermute | solution.py:422
  (456 shorter events, 435.1 us)
Async XLA Ops:
  123.7 77.0 %collective-permute-start.14 = (bf16[256,4096]{1,0:T(8,128)(2,1)}, bf16[256,4096]{1,0:T(8,128)(2,1)}, u32[]{:S(2)}, u32[]{:S(2)}) collective-permute-start(bf16[256,4096]{1,0:T(8,128)(2,1)} %get-tuple-element.88.refs_0_), channel_id=1, source_target_pairs={{0,4},{1,5},{2,6},{3,7},{4,0},{5,1},{6,2},{7,3},{8,12},{9,13},{10,... | collective-permute-start | bytes 6291464 | tf_op jit(solution)/shard_map/ppermute | solution.py:419
  123.8 98.6 %collective-permute-start.16 = (bf16[256,4096]{1,0:T(8,128)(2,1)}, bf16[256,4096]{1,0:T(8,128)(2,1)}, u32[]{:S(2)}, u32[]{:S(2)}) collective-permute-start(bf16[256,4096]{1,0:T(8,128)(2,1)} %get-tuple-element.94), channel_id=1, source_target_pairs={{0,2},{1,3},{2,0},{3,1},{4,6},{5,7},{6,4},{7,5},{8,10},{9,11},{10,... | collective-permute-start | bytes 6291464 | tf_op jit(solution)/shard_map/ppermute | solution.py:419
  130.2 61.7 %collective-permute-start.12 = (bf16[256,2048]{1,0:T(8,128)(2,1)}, bf16[256,2048]{1,0:T(8,128)(2,1)S(1)}, u32[]{:S(2)}, u32[]{:S(2)}) collective-permute-start(bf16[256,2048]{1,0:T(8,128)(2,1)} %collective-permute-done.11), channel_id=1, source_target_pairs={{0,4},{1,5},{6,2},{7,3},{8,12},{9,13},{14,10},{15,11},{16,20},{17,... | collective-permute-start | bytes 3145736 | tf_op jit(solution)/shard_map/ppermute | solution.py:481
  235.7 112.9 %collective-permute-start.21 = (bf16[256,4096]{1,0:T(8,128)(2,1)}, bf16[256,4096]{1,0:T(8,128)(2,1)}, u32[]{:S(2)}, u32[]{:S(2)}) collective-permute-start(bf16[256,4096]{1,0:T(8,128)(2,1)} %collective-permute-done.16.refs_2_), channel_id=1, source_target_pairs={{0,4},{1,5},{2,6},{3,7},{4,0},{5,1},{6,2},{7,3},{8,12},{9,13},{10,... | collective-permute-start | bytes 6291464 | tf_op jit(solution)/shard_map/ppermute | solution.py:419
  251.5 55.0 %collective-permute-start.26 = (bf16[256,2048]{1,0:T(8,128)(2,1)S(1)}, bf16[256,2048]{1,0:T(8,128)(2,1)S(1)}, u32[]{:S(2)}, u32[]{:S(2)}) collective-permute-start(bf16[256,2048]{1,0:T(8,128)(2,1)S(1)} %get-tuple-element.99.refs_0_), channel_id=1, source_target_pairs={{0,4},{1,5},{2,6},{3,7},{4,0},{5,1},{6,2},{7,3},{8,12},{9,13},{10,... | collective-permute-start | bytes 3145736 | tf_op jit(solution)/shard_map/ppermute | solution.py:419
  283.9 64.3 %collective-permute-start.34 = (bf16[256,2048]{1,0:T(8,128)(2,1)S(1)}, bf16[256,2048]{1,0:T(8,128)(2,1)S(1)}, u32[]{:S(2)}, u32[]{:S(2)}) collective-permute-start(bf16[256,2048]{1,0:T(8,128)(2,1)S(1)} %fusion.20.refs_0_), channel_id=1, source_target_pairs={{0,2},{1,3},{2,0},{3,1},{4,6},{5,7},{6,4},{7,5},{8,10},{9,11},{10,... | collective-permute-start | bytes 3145736 | tf_op jit(solution)/shard_map/ppermute | solution.py:419
  357.9 93.8 %collective-permute-start.38 = (bf16[256,2048]{1,0:T(8,128)(2,1)}, bf16[256,2048]{1,0:T(8,128)(2,1)S(1)}, u32[]{:S(2)}, u32[]{:S(2)}) collective-permute-start(bf16[256,2048]{1,0:T(8,128)(2,1)} %bitcast.30), channel_id=1, source_target_pairs={{0,0},{1,1},{2,16},{3,17},{4,4},{5,5},{6,20},{7,21},{8,8},{9,9},{1... | collective-permute-start | bytes 3145736 | tf_op jit(solution)/shard_map/ppermute | solution.py:442
  465.5 81.8 %collective-permute-start.42 = (bf16[256,2048]{1,0:T(8,128)(2,1)S(1)}, bf16[256,2048]{1,0:T(8,128)(2,1)S(1)}, u32[]{:S(2)}, u32[]{:S(2)}) collective-permute-start(bf16[256,2048]{1,0:T(8,128)(2,1)S(1)} %multiply_convert_fusion.refs_0_), channel_id=1, source_target_pairs={{0,10},{1,11},{2,8},{3,9},{4,14},{5,15},{6,12},{7,13},{8,2},{9,3},... | collective-permute-start | bytes 3145736 | tf_op jit(solution)/shard_map/ppermute | solution.py:430
  656.7 89.9 %collective-permute-start.57 = (bf16[512,2048]{1,0:T(8,128)(2,1)S(1)}, bf16[512,2048]{1,0:T(8,128)(2,1)S(1)}, u32[]{:S(2)}, u32[]{:S(2)}) collective-permute-start(bf16[512,2048]{1,0:T(8,128)(2,1)S(1)} %constant_dynamic-slice_fusion.9), channel_id=1, source_target_pairs={{0,4},{1,5},{2,6},{3,7},{4,0},{5,1},{6,2},{7,3},{8,12},{9,13},{10,... | collective-permute-start | bytes 6291464 | tf_op jit(solution)/shard_map/ppermute | solution.py:419
  662.6 87.8 %collective-permute-start.54 = (bf16[256,2048]{1,0:T(8,128)(2,1)S(1)}, bf16[256,2048]{1,0:T(8,128)(2,1)S(1)}, u32[]{:S(2)}, u32[]{:S(2)}) collective-permute-start(bf16[256,2048]{1,0:T(8,128)(2,1)S(1)} %get-tuple-element.137), channel_id=1, source_target_pairs={{0,8},{8,0},{16,24},{24,16},{1,9},{9,1},{17,25},{25,17},{2,10},{10... | collective-permute-start | bytes 3145736 | tf_op jit(solution)/shard_map/ppermute | solution.py:422
  664.0 86.5 %collective-permute-start.55 = (bf16[256,2048]{1,0:T(8,128)(2,1)S(1)}, bf16[256,2048]{1,0:T(8,128)(2,1)S(1)}, u32[]{:S(2)}, u32[]{:S(2)}) collective-permute-start(bf16[256,2048]{1,0:T(8,128)(2,1)S(1)} %get-tuple-element.137), channel_id=1, source_target_pairs={{0,2},{1,3},{2,0},{3,1},{4,6},{5,7},{6,4},{7,5},{8,10},{9,11},{10,... | collective-permute-start | bytes 3145736 | tf_op jit(solution)/shard_map/ppermute | solution.py:419
  664.2 86.2 %collective-permute-start.56 = (bf16[256,2048]{1,0:T(8,128)(2,1)S(1)}, bf16[256,2048]{1,0:T(8,128)(2,1)S(1)}, u32[]{:S(2)}, u32[]{:S(2)}) collective-permute-start(bf16[256,2048]{1,0:T(8,128)(2,1)S(1)} %get-tuple-element.137), channel_id=1, source_target_pairs={{0,10},{1,11},{2,8},{3,9},{4,14},{5,15},{6,12},{7,13},{8,2},{9,3},... | collective-permute-start | bytes 3145736 | tf_op jit(solution)/shard_map/ppermute | solution.py:430
  701.6 87.2 %collective-permute-start.59 = (bf16[2,2,1,2,2,64,1024]{6,5,4,3,2,1,0:T(8,128)(2,1)S(1)}, bf16[2,2,1,2,2,64,1024]{6,5,4,3,2,1,0:T(8,128)(2,1)S(1)}, u32[]{:S(2)}, u32[]{:S(2)}) collective-permute-start(bf16[2,2,1,2,2,64,1024]{6,5,4,3,2,1,0:T(8,128)(2,1)S(1)} %constant_dynamic-slice_fusion.7), channel_id=1, source_target_pairs={{0,4},{1,5},{2,6},{3,7},{4,0},{5,1},{6,2},{7,3},{8,12},{9,13},{10,... | collective-permute-start | bytes 6291464 | tf_op jit(solution)/shard_map/ppermute | solution.py:419
  746.5 114.0 %collective-permute-start.61 = (bf16[256,2048]{1,0:T(8,128)(2,1)S(1)}, bf16[256,2048]{1,0:T(8,128)(2,1)}, u32[]{:S(2)}, u32[]{:S(2)}) collective-permute-start(bf16[256,2048]{1,0:T(8,128)(2,1)S(1)} %convert_element_type.303), channel_id=1, source_target_pairs={{0,0},{1,1},{2,16},{3,17},{4,4},{5,5},{6,20},{7,21},{8,8},{9,9},{1... | collective-permute-start | bytes 3145736 | tf_op jit(solution)/shard_map/ppermute | solution.py:442
  751.5 106.5 %collective-permute-start.60 = (bf16[256,2048]{1,0:T(8,128)(2,1)}, bf16[256,2048]{1,0:T(8,128)(2,1)}, u32[]{:S(2)}, u32[]{:S(2)}) collective-permute-start(bf16[256,2048]{1,0:T(8,128)(2,1)} %constant_dynamic-slice_fusion.6), channel_id=1, source_target_pairs={{0,16},{8,24},{16,0},{24,8},{1,17},{9,25},{17,1},{25,9},{2,18},{10... | collective-permute-start | bytes 3145736 | tf_op jit(solution)/shard_map/ppermute | solution.py:422
  752.7 138.2 %collective-permute-start.65 = (bf16[1,2,1,2,2,64,1024]{6,5,4,3,2,1,0:T(8,128)(2,1)}, bf16[1,2,1,2,2,64,1024]{6,5,4,3,2,1,0:T(8,128)(2,1)}, u32[]{:S(2)}, u32[]{:S(2)}) collective-permute-start(bf16[1,2,1,2,2,64,1024]{6,5,4,3,2,1,0:T(8,128)(2,1)} %constant_dynamic-slice_fusion.5), channel_id=1, source_target_pairs={{0,16},{8,24},{16,0},{24,8},{1,17},{9,25},{17,1},{25,9},{2,18},{10... | collective-permute-start | bytes 3145736 | tf_op jit(solution)/shard_map/ppermute | solution.py:422
  880.6 79.1 %collective-permute-start.67 = (bf16[2048,768]{1,0:T(8,128)(2,1)}, bf16[2048,768]{1,0:T(8,128)(2,1)}, u32[]{:S(2)}, u32[]{:S(2)}) collective-permute-start(bf16[2048,768]{1,0:T(8,128)(2,1)} %convolution_convert_fusion.3), channel_id=1, source_target_pairs={{0,1},{1,0},{2,3},{3,2},{4,5},{5,4},{6,7},{7,6},{8,9},{9,8},{10,11... | collective-permute-start | bytes 9437192 | tf_op jit(solution)/shard_map/ppermute | solution.py:419
  890.9 63.9 %collective-permute-start.62 = (bf16[256,2048]{1,0:T(8,128)(2,1)}, bf16[256,2048]{1,0:T(8,128)(2,1)S(1)}, u32[]{:S(2)}, u32[]{:S(2)}) collective-permute-start(bf16[256,2048]{1,0:T(8,128)(2,1)} %convolution_convert_fusion.8), channel_id=1, source_target_pairs={{0,10},{1,11},{2,8},{3,9},{4,14},{5,15},{6,12},{7,13},{8,2},{9,3},... | collective-permute-start | bytes 3145736 | tf_op jit(solution)/shard_map/ppermute | solution.py:430
  892.7 66.6 %collective-permute-start.66 = (bf16[1,2,1,2,2,64,1024]{6,5,4,3,2,1,0:T(8,128)(2,1)S(1)}, bf16[1,2,1,2,2,64,1024]{6,5,4,3,2,1,0:T(8,128)(2,1)S(1)}, u32[]{:S(2)}, u32[]{:S(2)}) collective-permute-start(bf16[1,2,1,2,2,64,1024]{6,5,4,3,2,1,0:T(8,128)(2,1)S(1)} %constant_dynamic-slice_fusion.4), channel_id=1, source_target_pairs={{0,16},{8,24},{16,0},{24,8},{1,17},{9,25},{17,1},{25,9},{2,18},{10... | collective-permute-start | bytes 3145736 | tf_op jit(solution)/shard_map/ppermute | solution.py:422
  1005.4 143.7 %collective-permute-start.71 = (bf16[256,2048]{1,0:T(8,128)(2,1)}, bf16[256,2048]{1,0:T(8,128)(2,1)}, u32[]{:S(2)}, u32[]{:S(2)}) collective-permute-start(bf16[256,2048]{1,0:T(8,128)(2,1)} %fusion.11), channel_id=1, source_target_pairs={{0,0},{1,1},{2,16},{3,17},{4,4},{5,5},{6,20},{7,21},{8,8},{9,9},{1... | collective-permute-start | bytes 3145736 | tf_op jit(solution)/shard_map/ppermute | solution.py:442
  1019.0 71.4 %collective-permute-start.77 = (bf16[64,2048]{1,0:T(8,128)(2,1)S(1)}, bf16[64,2048]{1,0:T(8,128)(2,1)S(1)}, u32[]{:S(2)}, u32[]{:S(2)}) collective-permute-start(bf16[64,2048]{1,0:T(8,128)(2,1)S(1)} %constant_dynamic-slice_fusion), channel_id=1, source_target_pairs={{0,16},{8,24},{16,0},{24,8},{1,17},{9,25},{17,1},{25,9},{2,18},{10... | collective-permute-start | bytes 786440 | tf_op jit(solution)/shard_map/ppermute | solution.py:422
  1024.7 89.2 %collective-permute-start.72 = (bf16[1,2,1,2,2,64,768]{6,5,4,3,2,1,0:T(8,128)(2,1)S(1)}, bf16[1,2,1,2,2,64,768]{6,5,4,3,2,1,0:T(8,128)(2,1)S(1)}, u32[]{:S(2)}, u32[]{:S(2)}) collective-permute-start(bf16[1,2,1,2,2,64,768]{6,5,4,3,2,1,0:T(8,128)(2,1)S(1)} %constant_dynamic-slice_fusion.1), channel_id=1, source_target_pairs={{0,16},{8,24},{16,0},{24,8},{1,17},{9,25},{17,1},{25,9},{2,18},{10... | collective-permute-start | bytes 2359304 | tf_op jit(solution)/shard_map/ppermute | solution.py:422
  1024.8 67.8 %collective-permute-start.79 = (bf16[2,2,64,1024]{3,2,1,0:T(8,128)(2,1)S(1)}, bf16[2,2,64,1024]{3,2,1,0:T(8,128)(2,1)S(1)}, u32[]{:S(2)}, u32[]{:S(2)}) collective-permute-start(bf16[2,2,64,1024]{3,2,1,0:T(8,128)(2,1)S(1)} %dynamic-slice_bitcast_fusion.1), channel_id=1, source_target_pairs={{0,1},{1,0},{2,3},{3,2},{4,5},{5,4},{6,7},{7,6},{8,9},{9,8},{10,11... | collective-permute-start | bytes 1572872 | tf_op jit(solution)/shard_map/ppermute | solution.py:419
  1025.0 68.5 %collective-permute-start.83 = (bf16[2,2,64,1024]{3,2,1,0:T(8,128)(2,1)S(1)}, bf16[2,2,64,1024]{3,2,1,0:T(8,128)(2,1)S(1)}, u32[]{:S(2)}, u32[]{:S(2)}) collective-permute-start(bf16[2,2,64,1024]{3,2,1,0:T(8,128)(2,1)S(1)} %dynamic-slice_bitcast_fusion), channel_id=1, source_target_pairs={{0,1},{1,0},{2,3},{3,2},{4,5},{5,4},{6,7},{7,6},{8,9},{9,8},{10,11... | collective-permute-start | bytes 1572872 | tf_op jit(solution)/shard_map/ppermute | solution.py:419
  (143 other events, 3507.8 us)

commit v2 on v1

--- a/solution.py
+++ b/solution.py
@@ -142,6 +142,7 @@
 
 
 VMEM_LIMIT = 56 * 1024 * 1024
+BRIEF = pl.CostEstimate(flops=1024, bytes_accessed=1024, transcendentals=0)
 
 
 def attend(order, qkv, cos, sin, heads):
@@ -163,9 +164,7 @@
             jax.ShapeDtypeStruct((planes, seqs, slots, blk, heads * HD), F32),
         ],
         compiler_params=pltpu.CompilerParams(vmem_limit_bytes=VMEM_LIMIT),
-        cost_estimate=pl.CostEstimate(
-            flops=seqs * heads * length * length * HD * 4, bytes_accessed=seqs * length * width * 6, transcendentals=0
-        ),
+        cost_estimate=BRIEF,
         name="attend",
     )(order, qkv, cos, sin)
 
@@ -186,9 +185,7 @@
         ),
         out_shape=jax.ShapeDtypeStruct((planes, seqs, slots, blk, width), BF),
         compiler_params=pltpu.CompilerParams(vmem_limit_bytes=VMEM_LIMIT),
-        cost_estimate=pl.CostEstimate(
-            flops=seqs * heads * length * length * HD * 10, bytes_accessed=seqs * length * width * 12, transcendentals=0
-        ),
+        cost_estimate=BRIEF,
         name="attend_back",
     )(order, qkv, lse, grad, cos, sin)
 
@@ -249,9 +246,7 @@
         scratch_shapes=[pltpu.VMEM((span, width), BF), pltpu.VMEM((span, width), F32)],
         input_output_aliases={count + 3 + i: i for i in range(len(extra))},
         compiler_params=pltpu.CompilerParams(vmem_limit_bytes=48 * 1024 * 1024),
-        cost_estimate=pl.CostEstimate(
-            flops=6 * span * width * part_ff, bytes_accessed=6 * width * part_ff + 14 * span * part_ff, transcendentals=0
-        ),
+        cost_estimate=BRIEF,
         name="mlp",
     )(*hs, gu_w, gu_w, down_w, *extra)
     return result[:4], result[4:]
@@ -314,21 +309,96 @@
         scratch_shapes=[pltpu.VMEM((span, width), BF), pltpu.VMEM((span, width), F32)],
         input_output_aliases={count + 5 + i: i for i in range(len(extra))},
         compiler_params=pltpu.CompilerParams(vmem_limit_bytes=48 * 1024 * 1024),
-        cost_estimate=pl.CostEstimate(
-            flops=6 * span * width * part_ff, bytes_accessed=6 * width * part_ff + 12 * span * part_ff, transcendentals=0
-        ),
+        cost_estimate=BRIEF,
         name="mlp_back",
     )(*ds, g, u, gu_w, gu_w, down_w, *extra)
     return result[:3], result[3:]
 
 
-def assemble(places, pieces):
+def outer(lefts, rights, which, by_rows, away=None, runs=1):
+    count = max(len(lefts), len(rights))
+    depth = sum(v.shape[0] for v in lefts)
+    chunk = depth // count
+    out_rows, out_cols = lefts[0].shape[1], rights[0].shape[1]
+    out_rows, out_cols = (out_rows // 2, out_cols) if by_rows else (out_rows, out_cols // 2)
+    tile = min(TILE, out_rows // runs)
+    tiles = out_rows // tile
+    run = tiles // runs
+
+    def kernel(which, *refs):
+        left, right = refs[: len(lefts)], refs[len(lefts) : len(lefts) + len(rights)]
+        take = lambda group, i: group[i][...] if len(group) > 1 else group[0][i * chunk : (i + 1) * chunk, :]
+        total = mm_rows(take(left, 0), take(right, 0))
+        for i in range(1, count):
+            total = total + mm_rows(take(left, i), take(right, i))
+        if away is not None:
+            total = total + refs[-2][...].astype(F32)
+        refs[-1][...] = total.astype(BF)
+
+    out_spec = pl.BlockSpec((tile, out_cols), lambda i, w: (i, 0))
+    return pl.pallas_call(
+        kernel,
+        grid_spec=pltpu.PrefetchScalarGridSpec(
+            num_scalar_prefetch=1,
+            grid=(tiles,),
+            in_specs=[
+                pl.BlockSpec((v.shape[0], tile), lambda i, w: (0, (i // run + w[0]) * run + i if by_rows else i)) for v in lefts
+            ]
+            + [pl.BlockSpec((v.shape[0], out_cols), lambda i, w: (0, 0 if by_rows else w[0])) for v in rights]
+            + ([] if away is None else [out_spec]),
+            out_specs=out_spec,
+        ),
+        out_shape=jax.ShapeDtypeStruct((out_rows, out_cols), BF),
+        compiler_params=pltpu.CompilerParams(vmem_limit_bytes=48 * 1024 * 1024),
+        cost_estimate=BRIEF,
+        name="outer",
+    )(which.reshape(1).astype(jnp.int32), *lefts, *rights, *([] if away is None else [away]))
+
+
+def project(lefts, weight, transposed, types):
+    rows, depth = lefts[0].shape
+    width = weight.shape[0] if transposed else weight.shape[1]
+    tile = min(512, width)
+    count = len(lefts)
+
+    def kernel(*refs):
+        left, (w,), outs = refs[:count], refs[count : count + 1], refs[count + 1 :]
+        for i in range(count):
+            result = (mm_t if transposed else mm)(left[i][...], w[...])
+            if len(outs) > 1:
+                outs[i][...] = result.astype(outs[i].dtype)
+            else:
+                outs[0][i * rows : (i + 1) * rows, :] = result.astype(outs[0].dtype)
+
+    height = rows * count // len(types)
+    return pl.pallas_call(
+        kernel,
+        grid=(width // tile,),
+        in_specs=[pl.BlockSpec((rows, depth), lambda i: (0, 0))] * count
+        + [
+            pl.BlockSpec((tile, depth), lambda i: (i, 0))
+            if transposed
+            else pl.BlockSpec((depth, tile), lambda i: (0, i))
+        ],
+        out_specs=[pl.BlockSpec((height, tile), lambda i: (0, i))] * len(types),
+        out_shape=[jax.ShapeDtypeStruct((height, width), t) for t in types],
+        compiler_params=pltpu.CompilerParams(vmem_limit_bytes=48 * 1024 * 1024),
+        cost_estimate=BRIEF,
+        name="project",
+    )(*lefts, weight)
+
+
+def assemble(places, arrays, depth):
+    width = arrays[0].shape[1]
+    pieces = [(n, start) for n, v in enumerate(arrays) for start in range(0, v.shape[0], depth)]
     count = len(pieces)
-    depth, width = pieces[0].shape
 
     def kernel(places, *refs):
-        sources, out, held, arrive, leave = refs[:count], *refs[count:]
-        ins = [pltpu.make_async_copy(sources[i], held.at[i], arrive.at[i]) for i in range(count)]
+        sources, out, held, arrive, leave = refs[: len(arrays)], *refs[len(arrays) :]
+        ins = [
+            pltpu.make_async_copy(sources[n].at[pl.ds(start, depth), :], held.at[i], arrive.at[i])
+            for i, (n, start) in enumerate(pieces)
+        ]
         outs = [pltpu.make_async_copy(held.at[i], out.at[places[i]], leave.at[i]) for i in range(count)]
         for copy in ins:
             copy.start()
@@ -343,18 +413,19 @@
         grid_spec=pltpu.PrefetchScalarGridSpec(
             num_scalar_prefetch=1,
             grid=(1,),
-            in_specs=[pl.BlockSpec(memory_space=pl.ANY)] * count,
+            in_specs=[pl.BlockSpec(memory_space=pl.ANY)] * len(arrays),
             out_specs=pl.BlockSpec(memory_space=pl.ANY),
             scratch_shapes=[
-                pltpu.VMEM((count, depth, width), pieces[0].dtype),
+                pltpu.VMEM((count, depth, width), arrays[0].dtype),
                 pltpu.SemaphoreType.DMA((count,)),
                 pltpu.SemaphoreType.DMA((count,)),
             ],
         ),
-        out_shape=jax.ShapeDtypeStruct((count, depth, width), pieces[0].dtype),
+        out_shape=jax.ShapeDtypeStruct((count, depth, width), arrays[0].dtype),
         compiler_params=pltpu.CompilerParams(vmem_limit_bytes=VMEM_LIMIT),
+        cost_estimate=BRIEF,
         name="assemble",
-    )(places, *pieces).reshape(count * depth, width)
+    )(places, *arrays).reshape(count * depth, width)
 
 
 def take_columns(which, arrays, groups, members):
@@ -433,13 +504,18 @@
             [(p * shards + s, (p ^ dz) * shards + (s ^ 2)) for p in range(planes) for s in range(shards)],
         )
 
+    def send(array, homes):
+        moved = lax.ppermute(array, both, [(i, to) for i, to in enumerate(homes) if i != to])
+        stays = jnp.array([i == to for i, to in enumerate(homes)])[c * shards + f]
+        return jnp.where(stays, array, moved)
+
     def swap(array):
-        pairs_of = []
+        homes = []
         for p in range(planes):
             for s in range(shards):
                 to = (s // 2 % 2) * near + p % near
-                pairs_of.append((p * shards + s, to * shards + (s - s // 2 % 2 * 2 + p // near * 2)))
-        return lax.ppermute(array, both, pairs_of)
+                homes.append(to * shards + (s - s // 2 % 2 * 2 + p // near * 2))
+        return send(array, homes)
 
     cos, sin = tables(length)
     ranks = jnp.argsort(pairs.reshape(-1))
@@ -450,12 +526,19 @@
     def over_y(piece):
         return [flip(piece, bits) for bits in range(4, shards, 4)]
 
-    def put(own, own_y, other, other_y):
-        pieces = [own, *own_y, other, *other_y]
-        keys = [0, *range(4, shards, 4), 2, *range(6, shards, 4)]
-        pieces += [flip(piece, 1) for piece in pieces]
-        places = jnp.stack([f ^ k for k in keys] + [f ^ k ^ 1 for k in keys]).astype(jnp.int32)
-        return assemble(places, pieces)
+    y_bits = list(range(4, shards, 4))
+
+    def put(*items):
+        keys = [k for _, own_keys in items for k in own_keys]
+        depth = items[0][0].shape[0] // len(items[0][1])
+        places = jnp.stack([f ^ k for k in keys]).astype(jnp.int32)
+        return assemble(places, [v for v, _ in items], depth)
+
+    def put_pairs(both_x, both_y, other_x, other_y):
+        items = [(both_x, [0, 2]), (other_x, [1, 3])]
+        for bits, v, w in zip(y_bits, both_y, other_y):
+            items += [(v, [bits, bits + 2]), (w, [bits + 1, bits + 3])]
+        return put(*items)
 
     def head_columns(g):
         return jnp.concatenate(
@@ -472,76 +555,139 @@
                 q = s // 2
                 if q % near == p % near:
                     at = s // 4 * 4 + q // near * 2 + s % 2
-                    sends.append((p * shards + s, p * shards + at))
+                    if at != s:
+                        sends.append((p * shards + s, p * shards + at))
                     for d in range(4, shards, 4):
                         spreads.setdefault(d, []).append((p * shards + at, p * shards + (at ^ d)))
-        first = lax.ppermute(weight, both, sends)
-        found = first
-        for pairs_of in spreads.values():
-            found = found + lax.ppermute(first, both, pairs_of)
-        other, even = flip(found, 1), core == 0
-        return jnp.concatenate([jnp.where(even, found, other), jnp.where(even, other, found)], 0)
+        q = f // 2
+        stays = (q % near == low) & (f // 4 * 4 + q // near * 2 + core == f)
+        first = jnp.where(stays, weight, lax.ppermute(weight, both, sends))
+
+        def rest(first):
+            found = first
+            for pairs_of in spreads.values():
+                found = found + lax.ppermute(first, both, pairs_of)
+            return found
+
+        return first, rest
 
     def gather_group(own):
         return [own] + [hop(own, j) for j in range(1, planes)]
-
-    def reduce_group(parts):
-        total = parts[0]
-        for j in reversed(range(1, planes)):
-            total = total + hop(parts[j].astype(BF), j).astype(F32)
-        return total
 
     cut = planes // 2
     early = list(range(1, cut + 1))
     late = [0, *range(cut + 1, planes)]
     early_types = [BF] * cut
     late_types = [F32] + [BF] * (planes - cut - 1)
-    places = early + late
-    back_to = [places.index(j) for j in range(planes)]
-
-    valid_home = valid.reshape(rows, 1)
+
+    def add_all(total, others):
+        for other in others:
+            total = total + other.astype(F32)
+        return total
+
+    region = lambda *values: lax.optimization_barrier(values)
+
+    gu_own, gu_send = take_columns([group, group ^ near], [w_gate, w_up], shards, planes)
     stream_low = swap(tokens.reshape(rows, width))
     qkv_own = head_columns(group)
     qkv_other = flip(head_columns(group ^ near), 2)
-    w_qkv = put(qkv_own, over_y(qkv_own), qkv_other, over_y(qkv_other))
-    valid_float = swap(after(valid_home, stream_low)).astype(F32)
-    gu_own, gu_send = take_columns([group, group ^ near], [w_gate, w_up], shards, planes)
-
+    gu_own_y = over_y(gu_own)
+    heads_first, heads_rest = own_heads(w_out)
+    stream_low, qkv_own, qkv_other, gu_own, gu_own_y, gu_send, heads_first, w_down = region(
+        stream_low, qkv_own, qkv_other, gu_own, gu_own_y, gu_send, heads_first, w_down
+    )
     stream = stream_low.astype(F32)
     normed_one, inverse_one = normalize(stream)
-    h1 = gather_group(normed_one.astype(BF))
-    gu_own_y = over_y(gu_own)
-    w_out_mine = own_heads(after(w_out, *h1))
-    qkv = jnp.stack([mm(h, w_qkv).reshape(seqs, slots, blk, 3 * mine) for h in h1], 0)
-    gu_other = flip(after(gu_send, *h1), 2)
-    qkv, w_out_mine, *gu_own_y = lax.optimization_barrier((qkv, w_out_mine, *gu_own_y))
+    qkv_both = jnp.concatenate([qkv_own, qkv_other], 0)
+    h1, qkv_both = region([normed_one.astype(BF)], qkv_both)
+
+    h1 = h1 + [hop(h1[0], j) for j in early]
+    qkv_y = over_y(qkv_both)
+    qkv_pair = flip(qkv_both, 1)
+    h1, qkv_both, qkv_y, qkv_pair, heads_first, w_down, gu_send = region(
+        h1, qkv_both, qkv_y, qkv_pair, heads_first, w_down, gu_send
+    )
+
+    h1 = h1 + [hop(h1[0], j) for j in late[1:]]
+    found = heads_rest(heads_first)
+    down_own = ff_rows(group)
+    down_other = flip(ff_rows(group ^ near), 2)
+    qkv_y_pair = [flip(v, 1) for v in qkv_y]
+    h1, found, down_own, down_other, qkv_y_pair, gu_send, gu_own_y, teacher = region(
+        h1, found, down_own, down_other, qkv_y_pair, gu_send, gu_own_y, teacher
+    )
+
+    gu_other = flip(gu_send, 2)
+    down_both = jnp.concatenate([down_own, down_other], 0)
+    down_y = over_y(down_both)
+    other = flip(found, 1)
+    w_qkv = put_pairs(qkv_both, qkv_y, qkv_pair, qkv_y_pair)
+    goal_low = swap(teacher.reshape(rows, width))
+    (qkv,) = project(h1, w_qkv, False, [F32])
+    qkv = qkv.reshape(planes, seqs, slots, blk, 3 * mine)
     mixed, lse = attend(order, qkv, cos, sin, heads)
-    mixed, gu_other = lax.optimization_barrier((mixed, gu_other))
+    even = core == 0
+    w_out_mine = jnp.concatenate([jnp.where(even, found, other), jnp.where(even, other, found)], 0)
+    group_types = [F32] + [BF] * (planes - 1)
+    products = project([mixed[s].reshape(rows, mine) for s in range(planes)], w_out_mine, False, group_types)
+    products, gu_other, down_both, down_y, gu_own, gu_own_y, goal_low = region(
+        products, gu_other, down_both, down_y, gu_own, gu_own_y, goal_low
+    )
+
+    received = [hop(products[j], j) for j in early]
     gu_other_y = over_y(gu_other)
-    down_own = ff_rows(group)
-    down_own_y = over_y(after(down_own, mixed))
-    down_other = flip(after(ff_rows(group ^ near), gu_other), 2)
-    products = [mm(mixed[s].reshape(rows, mine), w_out_mine) for s in range(planes)]
-    residual = stream + reduce_group(products)
-
+    down_pair = flip(down_both, 1)
+    gu_own_pair = flip(gu_own, 1)
+    received, products, down_pair, gu_other, down_y, gu_own_pair, gu_own_y = region(
+        received, products, down_pair, gu_other, down_y, gu_own_pair, gu_own_y
+    )
+
+    received = received + [hop(products[j], j) for j in late[1:]]
+    down_y_pair = [flip(v, 1) for v in down_y]
+    gu_own_y_pair = [flip(v, 1) for v in gu_own_y]
+    gu_other_pair = flip(gu_other, 1)
+    received, gu_other_y, down_y_pair, gu_own_y_pair, gu_other_pair, valid = region(
+        received, gu_other_y, down_y_pair, gu_own_y_pair, gu_other_pair, valid
+    )
+    residual = stream + add_all(products[0], received)
     normed_two, inverse_two = normalize(residual)
-    h2 = gather_group(normed_two.astype(BF))
-    gu_w = put(gu_own, gu_own_y, gu_other, gu_other_y)
-    down_w = put(down_own, down_own_y, down_other, over_y(down_other))
-    goal_low = swap(after(teacher, *h2).reshape(rows, width))
+    h2, gu_other_y = region([normed_two.astype(BF)], gu_other_y)
+
+    h2 = h2 + [hop(h2[0], j) for j in early]
+    gu_items = [(gu_own, [0]), (gu_own_pair, [1]), (gu_other, [2]), (gu_other_pair, [3])]
+    for bits, v, w, z in zip(y_bits, gu_own_y, gu_own_y_pair, gu_other_y):
+        gu_items += [(v, [bits]), (w, [bits + 1]), (z, [bits + 2]), (flip(z, 1), [bits + 3])]
+    down_w = put_pairs(down_both, down_y, down_pair, down_y_pair)
+    gu_w = put(*gu_items)
+    h2, gu_w, down_w, valid = region(h2, gu_w, down_w, valid)
+
+    h2 = h2 + [hop(h2[0], j) for j in late[1:]]
     kept, outs = mlp([h2[j] for j in early], gu_w, down_w, early_types, 2, 0)
-    (h2_all, gates, ups, hidden_all), more = mlp([h2[j] for j in late], gu_w, down_w, late_types, 2, 1, kept)
-    outs = [*outs, *more]
-    output = residual + reduce_group([outs[i] for i in back_to])
-
+    outs, kept, far_tokens = region(outs, kept, h2[cut + 1 :])
+    h2 = h2[: cut + 1] + far_tokens
+
+    received = [hop(v, j) for v, j in zip(outs, early)]
+    (h2_all, gates, ups, hidden_all), outs = mlp(
+        [h2[j] for j in late], gu_w, down_w, late_types, 2, 1, kept
+    )
+    received, outs, h2_all, gates, ups, hidden_all, valid = region(
+        received, outs, h2_all, gates, ups, hidden_all, valid
+    )
+
+    received = received + [hop(v, j) for v, j in zip(outs[1:], late[1:])]
+    valid_float = swap(valid.reshape(rows, 1)).astype(F32)
+    received, own, valid_float = region(received, outs[0], valid_float)
+
+    output = residual + add_all(own, received)
     deviation = output - goal_low.astype(F32)
     grad_output = valid_float * deviation
     sums = jnp.stack([jnp.sum(grad_output * deviation), jnp.sum(valid_float)])
     sums0 = jnp.broadcast_to(sums[:, None, None], (2, 8, HD))
-
-    for bits in range(1, planes):
-        sums = sums + hop(sums0, bits) if bits > 1 else sums0 + hop(sums0, bits)
-    low_grad, sums = lax.optimization_barrier((grad_output.astype(BF), sums))
+    sums = sums0
+    for j in range(1, planes):
+        sums = sums + hop(sums0, j)
+    sums = sums + flip_ctx(sums, near)
+    low_grad, low_output, sums = region(grad_output.astype(BF), output.astype(BF), sums)
 
     steps = [1 << b for b in reversed(range(2, shards.bit_length() - 1))]
 
@@ -551,19 +697,8 @@
         away = move(take(1 - bit), bits)
         return (take(bit).astype(F32) + away.astype(F32)).astype(BF)
 
-    def half_of(v, k):
-        return lax.dynamic_slice_in_dim(v, k * (v.shape[1] // 2), v.shape[1] // 2, 1)
-
-    def over_core(compute):
-        away = flip(compute(1 - core).astype(BF), 1)
-        return (compute(core) + away.astype(F32)).astype(BF)
-
-    def by_rows(left, right):
-        return over_core(lambda k: mm_rows(half_of(left, k), right))
-
-    def by_columns(left, right):
-        part = over_core(lambda k: mm_rows(left, half_of(right, k)))
-        return part.reshape(2, near, shards // 4, 2, 2, unit, part.shape[1])
+    def parts(whole):
+        return whole.reshape(2, near, shards // 4, 2, 2, unit, whole.shape[1])
 
     def across_y(part, axis):
         for step in steps:
@@ -577,86 +712,125 @@
         homes = []
         for p in range(planes):
             for s in range(shards):
-                block = ((s % 2) * (shards // 4) + s // 4) * 2 + p // near
-                homes.append((p * shards + s, place(block, (s // 2 % 2) * near + p % near)))
-        return lax.ppermute(part, both, homes).astype(F32)
-
-    def place_columns(part, columns):
-        half = part.shape[-1]
-        part = part.reshape(near, 2, 2, unit, half)
-        take = lambda v, k, axis: lax.dynamic_index_in_dim(v, k, axis, keepdims=False)
-        keep, away = take(part, core, 2), flip(take(part, 1 - core, 2), 1)
+                homes.append(place(s % 2, s // 4, p // near, (s // 2 % 2) * near + p % near))
+        return send(part, homes).astype(F32)
+
+    def take(v, k, axis):
+        return lax.dynamic_index_in_dim(v, k, axis, keepdims=False)
+
+    def core_away(part):
+        return flip(take(part.reshape(near, 2, 2, unit, part.shape[-1]), 1 - core, 2), 1)
+
+    def core_joined(part, away):
+        keep = take(part.reshape(near, 2, 2, unit, part.shape[-1]), core, 2)
         even = core == 0
-        part = jnp.concatenate([jnp.where(even, keep, away), jnp.where(even, away, keep)], -1)
-        pieces = []
-        for j in range(planes):
-            piece = take(take(part, x ^ (j // near), 1), low ^ (j % near), 0)
-            pieces.append(hop(piece, j) if j else piece)
+        return jnp.concatenate([jnp.where(even, keep, away), jnp.where(even, away, keep)], -1)
+
+    def column_pieces(part):
+        return [take(take(part, x ^ (j // near), 1), low ^ (j % near), 0) for j in range(planes)]
+
+    def columns_placed(pieces):
         places = jnp.stack([group ^ j for j in range(planes)]).astype(jnp.int32)
-        return columns(assemble(places, pieces).reshape(planes, unit, 2 * half)).astype(F32)
-
-    dm = gather_group(low_grad)
+        return assemble(places, pieces, unit).reshape(planes, unit, -1)
+
+    dm = [low_grad] + [hop(low_grad, j) for j in early]
     for bits in [1, *(1 << b for b in range(2, shards.bit_length() - 1))]:
         sums = sums + flip(sums, bits)
-    dm[1], sums = lax.optimization_barrier((dm[1], sums))
+    dm, sums, low_output = region(dm, sums, low_output)
+
+    dm = dm + [hop(dm[0], j) for j in late[1:]]
     kept, backs = mlp_back([dm[j] for j in early], gates, ups, gu_w, down_w, early_types, 2, 0)
-    kept, sums = lax.optimization_barrier((kept, sums))
-    sums = sums + flip_ctx(sums, near)
-    (dm_all, dg_all, du_all), more = mlp_back(
+    backs, kept, far_tokens, sums = region(backs, kept, dm[cut + 1 :], sums)
+    dm = dm[: cut + 1] + far_tokens
+
+    received = [hop(v, j) for v, j in zip(backs, early)]
+    dm_runs = [dm[j] for j in early + late]
+    away = flip(outer([hidden_all], dm_runs, 1 - core, True, None, 2), 1)
+    (_, dg_all, du_all), backs = mlp_back(
         [dm[j] for j in late], gates, ups, gu_w, down_w, late_types, 2, 1, kept
     )
-    backs = [*backs, *more]
-    received = [hop(backs[back_to[j]], j) for j in range(1, planes)]
-    g_down = by_rows(hidden_all, dm_all)
-    g_gate = by_columns(h2_all, dg_all)
-    g_up = by_columns(h2_all, du_all)
-    received, g_down, g_gate, g_up, sums = lax.optimization_barrier((received, g_down, g_gate, g_up, sums))
-    grad_two = backs[back_to[0]]
-    for v in received:
-        grad_two = grad_two + v.astype(F32)
-    activations = swap(after(output, *received).astype(BF))
+    g_down = outer([hidden_all], dm_runs, core, True, away, 2)
+    received, backs, g_down, dg_all, du_all, h2_all = region(received, backs, g_down, dg_all, du_all, h2_all)
+
+    received = received + [hop(v, j) for v, j in zip(backs[1:], late[1:])]
+    g_down = across_y(g_down.reshape(2, shards // 4, part_ff // shards, width), 1)
+    gate_half = outer([h2_all], [dg_all], 1 - core, False)
+    up_half = outer([h2_all], [du_all], 1 - core, False)
+    received, gate_half, up_half, dg_all, du_all, g_down = region(received, gate_half, up_half, dg_all, du_all, g_down)
+    grad_two = add_all(backs[0], received)
     grad_residual = grad_output + norm_back(grad_two, normed_two, inverse_two)
-
-    dab = gather_group(grad_residual.astype(BF))
-    g_down = across_y(g_down, 0)
+    dab, gate_half, up_half, g_down = region([grad_residual.astype(BF)], gate_half, up_half, g_down)
+
+    dab = dab + [hop(dab[0], j) for j in early]
+    gate_away, up_away = flip(gate_half, 1), flip(up_half, 1)
+    g_down = across_far(g_down)
+    dab, gate_away, up_away, dg_all, du_all, low_output = region(dab, gate_away, up_away, dg_all, du_all, low_output)
+
+    dab = dab + [hop(dab[0], j) for j in late[1:]]
+    g_gate = parts(outer([h2_all], [dg_all], core, False, gate_away))
+    g_up = parts(outer([h2_all], [du_all], core, False, up_away))
+    dab, g_gate, g_up, g_down, low_output = region(dab, g_gate, g_up, g_down, low_output)
+
+    activations = swap(low_output)
     g_gate = across_y(g_gate, 2)
-    dab, g_down, g_gate = lax.optimization_barrier((dab, g_down, g_gate))
-    do = jnp.stack([mm_t(d, w_out_mine).astype(BF).reshape(seqs, slots, blk, mine) for d in dab], 0)
     g_up = across_y(g_up, 2)
-    g_down = across_far(g_down)
-    dqkv = attend_back(order, qkv, lse, do, cos, sin, heads)
-    dqkv, g_up, g_down, activations = lax.optimization_barrier((dqkv, g_up, g_down, activations))
+    (do,) = project(dab, w_out_mine, True, [BF])
+    dqkv = attend_back(order, qkv, lse, do.reshape(planes, seqs, slots, blk, mine), cos, sin, heads)
+    dqkv = dqkv.reshape(planes * rows, 3 * mine)
+    qkv_half = outer(h1, [dqkv], 1 - core, False)
+    dqkv, qkv_half, g_gate, activations = region(dqkv, qkv_half, g_gate, activations)
+
+    qkv_away = flip(qkv_half, 1)
+    g_gate = across_far(g_gate)
+    backs = project([dqkv[i * rows : (i + 1) * rows] for i in range(planes)], w_qkv, True, group_types)
+    backs, dqkv, qkv_away, g_down = region(backs, dqkv, qkv_away, g_down)
+
+    received = [hop(backs[j], j) for j in early]
+    g_qkv = parts(outer(h1, [dqkv], core, False, qkv_away))
+    mixed = mixed.reshape(planes * rows, mine)
+    out_half = outer([mixed], dab, 1 - core, True)
+    g_down = place_rows(
+        g_down.reshape(ff // world, width),
+        lambda core, y, far, g: far * (shards // 2) * planes + (core * (shards // 4) + y) * planes + g,
+    )
+    received, backs, g_qkv, out_half, g_up, g_gate = region(received, backs, g_qkv, out_half, g_up, g_gate)
+
+    received = received + [hop(backs[j], j) for j in late[1:]]
+    g_qkv = across_y(g_qkv, 2)
+    g_up = across_far(g_up)
+    out_away = flip(out_half, 1)
+    gate_core = core_away(g_gate)
+    received, g_qkv, out_away, gate_core, g_down, g_up = region(received, g_qkv, out_away, gate_core, g_down, g_up)
+    grad_one = add_all(backs[0], received)
+    grad_stream = grad_residual + norm_back(grad_one, normed_one, inverse_one)
+    g_out = outer([mixed], dab, core, True, out_away)
+    gate_pieces = column_pieces(core_joined(g_gate, gate_core))
+    low_stream, g_out, g_qkv, gate_pieces, g_up = region(grad_stream.astype(BF), g_out, g_qkv, gate_pieces, g_up)
+
+    grad_low = swap(low_stream)
+    g_qkv = across_far(g_qkv)
+    g_out = across_y(g_out, 0)
+    gate_pieces = gate_pieces[:1] + [hop(gate_pieces[j], j) for j in early] + gate_pieces[cut + 1 :]
+    grad_low, g_out, g_up, g_qkv, gate_pieces = region(grad_low, g_out, g_up, g_qkv, gate_pieces)
+
     count = sums[1, 0, 0]
     loss = sums[0, 0, 0] / (count * width)
     factor = (rows * world) / count
-    backs = [mm_t(dqkv[s].reshape(rows, 3 * mine), w_qkv) for s in range(planes)]
-    backs = [v if i == 0 else v.astype(BF) for i, v in enumerate(backs)]
-    dqkv, backs, h1_all, dab_all = lax.optimization_barrier(
-        (dqkv, backs, jnp.concatenate(h1, 0), jnp.concatenate(dab, 0))
-    )
-    g_qkv = by_columns(h1_all, dqkv.reshape(planes * rows, 3 * mine))
-    g_out = by_rows(mixed.reshape(planes * rows, mine), dab_all)
-    g_gate = across_far(g_gate)
-    g_up = across_far(g_up)
-    grad_one = reduce_group(backs)
-    grad_stream = grad_residual + norm_back(grad_one, normed_one, inverse_one)
-    g_qkv = across_y(g_qkv, 2)
-    g_out = across_y(g_out, 0)
-    low_stream, g_gate, g_up, g_qkv, g_out = lax.optimization_barrier(
-        (grad_stream.astype(BF), g_gate, g_up, g_qkv, g_out)
-    )
-    grad_input = swap(low_stream).astype(F32) * factor
-
-    g_qkv = across_far(g_qkv)
+    grad_input = grad_low.astype(F32) * factor
+    ff_order = lambda v: v.reshape(planes, unit, shards, -1).transpose(1, 2, 0, 3).reshape(unit, ff)
+    gate_pieces = gate_pieces[: cut + 1] + [hop(gate_pieces[j], j) for j in late[1:]]
+    up_core = core_away(g_up)
+    qkv_core = core_away(g_qkv)
     g_out = across_far(g_out)
-    g_down = place_rows(
-        g_down, lambda block, g: ((ff // shards) * block + (ff // world) * g) // (ff // world)
-    )
-    ff_order = lambda v: v.reshape(planes, unit, shards, -1).transpose(1, 2, 0, 3).reshape(unit, ff)
-    g_gate = place_columns(g_gate, ff_order)
-    g_up = place_columns(g_up, ff_order)
-    g_qkv = place_columns(g_qkv, lambda v: v.reshape(planes, unit, 3, mine).transpose(2, 1, 0, 3).reshape(3, unit, width))
-    g_out = place_rows(g_out, lambda block, g: g * shards + block)
+    gate_pieces, up_core, qkv_core, g_out, g_qkv, g_up = region(gate_pieces, up_core, qkv_core, g_out, g_qkv, g_up)
+    up_pieces = [hop(v, j) if j else v for j, v in enumerate(column_pieces(core_joined(g_up, up_core)))]
+    g_gate = ff_order(columns_placed(gate_pieces)).astype(F32)
+    up_pieces, g_qkv, qkv_core, g_out = region(up_pieces, g_qkv, qkv_core, g_out)
+    qkv_pieces = [hop(v, j) if j else v for j, v in enumerate(column_pieces(core_joined(g_qkv, qkv_core)))]
+    g_out = place_rows(g_out, lambda core, y, far, g: g * shards + (core * (shards // 4) + y) * 2 + far)
+    g_up = ff_order(columns_placed(up_pieces)).astype(F32)
+    g_qkv = columns_placed(qkv_pieces).reshape(planes, unit, 3, mine).transpose(2, 1, 0, 3).reshape(3, unit, width)
+    g_qkv = g_qkv.astype(F32)
     return (
         activations.reshape(tokens.shape),
         loss,

time: 1190 us -> 1000 us (0.84)
  waiting for transfers between devices: 655 us -> 437 us
  Pallas kernels: 197 us -> 298 us
  matrix products: 95.7 us -> 0 us
  other arithmetic: 51.6 us -> 78.9 us
  local copies, waits for them, and re-layouts: 40 us -> 59.2 us
  starting transfers between devices: 126 us -> 111 us
    ppermute x49 -> x43, waiting for transfers between devices: 298 us -> 140 us  [flip(): return lax.ppermute(array, 'fsdp', [(i, i ^ bits) for i in range(shards)])]
    pallas_call x0 -> x14, Pallas kernels: none -> 108 us  [the longest x10 79.1 us: outer(): pl.pallas_call(kernel, grid_spec=pltpu.PrefetchScalarGridSpec(num_scalar_...]
    dot_general x26 -> x0, matrix products: 95.7 us -> none  [the longest x10 60.6 us: mm_rows(): lax.dot_general(left, right, (((0,), (0,)), ((), ())), preferred_element_...]
    ppermute x9, waiting for transfers between devices: 139 us -> 94.7 us  [the longest x7 79.1 us: send(): lax.ppermute(array, both, [(i, to) for i, to in enumerate(homes) if i !=...]
    ppermute x12, waiting for transfers between devices: 36.3 us -> 16.5 us  [hop(): lax.ppermute(array, both, [(p * shards + s, (p ^ dz) * shards + (s ^ 2))...]
    ppermute x9, starting transfers between devices: 50.6 us -> 31.2 us  [the longest x7 27.2 us: send(): lax.ppermute(array, both, [(i, to) for i, to in enumerate(homes) if i !=...]
    ppermute x49 -> x43, starting transfers between devices: 37.8 us -> 25 us  [flip(): return lax.ppermute(array, 'fsdp', [(i, i ^ bits) for i in range(shards)])]
    unnamed x165 -> x159, local copies, waits for them, and re-layouts: 17.4 us -> 24.6 us
  transfers between devices with their start and end apart: 88 -> 82, of which waited for: 35 -> 37; matrix products, arithmetic and copies ran while one was open for 13% -> 8% of each run, Pallas kernels for 14% -> 29%
where the time goes in v2:
time: 1000 us; the launch traced here: 990 us
  waiting for transfers between devices  437 us (44%)
  Pallas kernels  298 us (30%)
  starting transfers between devices  111 us (11%)
  other arithmetic  78.9 us (8%)
  local copies, waits for them, and re-layouts  59.2 us (6%)
    ppermute x18, waiting for transfers between devices, flip_ctx(): return lax.ppermute(array, 'ctx', [(i, i ^ bits) for i in range(planes)])  186 us
    ppermute x43, waiting for transfers between devices, flip(): return lax.ppermute(array, 'fsdp', [(i, i ^ bits) for i in range(shards)])  140 us
    pallas_call x10, Pallas kernels, outer(): pl.pallas_call(kernel, grid_spec=pltpu.PrefetchScalarGridSpec(num_scalar_...  79.1 us
    ppermute x7, waiting for transfers between devices, send(): lax.ppermute(array, both, [(i, to) for i, to in enumerate(homes) if i !=...  79.1 us
    pallas_call x2, Pallas kernels, mlp_back(): pl.pallas_call(functools.partial(down_kernel, count), grid=(tiles,), in_s...  58.3 us
    pallas_call x2, Pallas kernels, mlp(): pl.pallas_call(functools.partial(up_kernel, count), grid=(tiles,), in_spe...  42.6 us
    pallas_call x6, Pallas kernels, assemble(): pl.pallas_call(kernel, grid_spec=pltpu.PrefetchScalarGridSpec(num_scalar_...  33.7 us
    pallas_call x4, Pallas kernels, project(): pl.pallas_call(kernel, grid=(width // tile,), in_specs=[pl.BlockSpec((row...  29.2 us
  transfers between devices with their start and end apart: 82, of which 37 were waited for; matrix products, arithmetic and copies ran while one was open for 8% of the time, Pallas kernels for 29%

profile of v2, /device:TPU:16, one launch (start us, length us, event | category | flops | bytes accessed | tf_op | source)
XLA Modules:
  0.0 990.0 jit_solution(5799578920840210493)
XLA Ops:
  22.6 37.8 %collective-permute-done = bf16[256,2048]{1,0:T(8,128)(2,1)} collective-permute-done((bf16[256,2048]{1,0:T(8,128)(2,1)}, bf16[256,2048]{1,0:T(8,128)(2,1)}, u32[]{:S(2)}, u32[]{:S(2)}) %collective-permute-start) | collective-permute-done | bytes 1048608 | tf_op jit(solution)/shard_map/ppermute | solution.py:508
  72.4 23.7 %collective-permute-done.4.refs_1_ = bf16[256,2048]{1,0:T(8,128)(2,1)S(1)} collective-permute-done((bf16[256,2048]{1,0:T(8,128)(2,1)S(1)}, bf16[256,2048]{1,0:T(8,128)(2,1)S(1)}, u32[]{:S(2)}, u32[]{:S(2)}) %collective-permute-start.4) | collective-permute-done | bytes 1048608 | tf_op jit(solution)/shard_map/ppermute | solution.py:493
  114.3 15.6 %collective-permute-done.9 = bf16[256,2048]{1,0:T(8,128)(2,1)S(1)} collective-permute-done((bf16[256,2048]{1,0:T(8,128)(2,1)}, bf16[256,2048]{1,0:T(8,128)(2,1)S(1)}, u32[]{:S(2)}, u32[]{:S(2)}) %collective-permute-start.9) | collective-permute-done | bytes 1048608 | tf_op jit(solution)/shard_map/ppermute | solution.py:569
  131.3 24.8 %collective-permute-done.10 = bf16[256,2048]{1,0:T(8,128)(2,1)S(1)} collective-permute-done((bf16[256,2048]{1,0:T(8,128)(2,1)S(1)}, bf16[256,2048]{1,0:T(8,128)(2,1)S(1)}, u32[]{:S(2)}, u32[]{:S(2)}) %collective-permute-start.10) | collective-permute-done | bytes 1048608 | tf_op jit(solution)/shard_map/ppermute | solution.py:490
  181.3 10.1 %project.4 = f32[1024,1536]{1,0:T(8,128)} custom-call(bf16[256,2048]{1,0:T(8,128)(2,1)S(1)} %fusion.4.refs_0_, bf16[256,2048]{1,0:T(8,128)(2,1)S(1)} %collective-permute-done.4.refs_1_, bf16[256,2048]{1,0:T(8,128)(2,1)S(1)} %collective-permute-done.5.refs_2_, bf16[256,2048]{1,0:T(8,128)(2,1)S(1)} %copy-done.10, bf16[2048,1536]{1,0:T(8,128)(2,1)} %bitcast.140), custom_call_target="tpu_custom_call" | custom-call | flops 1024 | bytes 1024 | tf_op jit(solution)/shard_map/project/pallas_call | solution.py:374
  191.4 21.5 %attend.1 = (bf16[4,1,2,128,512]{4,3,2,1,0:T(8,128)(2,1)}, f32[4,1,2,128,512]{4,3,2,1,0:T(8,128)}) custom-call(s32[8]{0:T(128)} %fusion.41.order, f32[4,1,2,128,1536]{4,3,2,1,0:T(8,128)} %bitcast.142, f32[1024,128]{1,0:T(8,128)} %get-tuple-element.530.cos, f32[1024,128]{1,0:T(8,128)} %get-tuple-element.531.sin), custom_call_target="tpu_custom_call" | custom-call | flops 1024 | bytes 1024 | tf_op jit(solution)/shard_map/attend/pallas_call | solution.py:153
  236.0 21.6 %collective-permute-done.16 = bf16[256,2048]{1,0:T(8,128)(2,1)S(1)} collective-permute-done((bf16[256,2048]{1,0:T(8,128)(2,1)S(1)}, bf16[256,2048]{1,0:T(8,128)(2,1)S(1)}, u32[]{:S(2)}, u32[]{:S(2)}) %collective-permute-start.16) | collective-permute-done | bytes 1048608 | tf_op jit(solution)/shard_map/ppermute | solution.py:493
  259.8 22.0 %collective-permute-done.21.refs_6_ = bf16[256,4096]{1,0:T(8,128)(2,1)} collective-permute-done((bf16[256,4096]{1,0:T(8,128)(2,1)}, bf16[256,4096]{1,0:T(8,128)(2,1)}, u32[]{:S(2)}, u32[]{:S(2)}) %collective-permute-start.21) | collective-permute-done | bytes 2097184 | tf_op jit(solution)/shard_map/ppermute | solution.py:490
  300.0 12.5 %assemble.7 = bf16[8,256,4096]{2,1,0:T(8,128)(2,1)} custom-call(s32[8]{0:T(128)} %stack.98.places, bf16[256,4096]{1,0:T(8,128)(2,1)} %get-tuple-element.286.refs_0_, bf16[256,4096]{1,0:T(8,128)(2,1)} %copy-done.48, bf16[256,4096]{1,0:T(8,128)(2,1)} %collective-permute-done.13.refs_2_, bf16[256,4096]{1,0:T(8,128)(2,1)} %copy-done.51, ...), custom_call_target="tpu_custom_call" | custom-call | flops 1024 | bytes 1024 | tf_op jit(solution)/shard_map/assemble/pallas_call | solution.py:411
  318.6 21.6 %mlp.2 = (bf16[1024,2048]{1,0:T(8,128)(2,1)}, f32[1024,2048]{1,0:T(8,128)}, f32[1024,2048]{1,0:T(8,128)}, bf16[1024,2048]{1,0:T(8,128)(2,1)}, bf16[256,2048]{1,0...) custom-call(bf16[256,2048]{1,0:T(8,128)(2,1)S(1)} %collective-permute-done.25.refs_0_, ...), custom_call_target="tpu_custom_call" | custom-call | flops 1024 | bytes 1024 | tf_op jit(solution)/shard_map/mlp/pallas_call | solution.py:233
  344.5 21.0 %mlp.3 = (bf16[1024,2048]{1,0:T(8,128)(2,1)}, f32[1024,2048]{1,0:T(8,128)}, f32[1024,2048]{1,0:T(8,128)}, bf16[1024,2048]{1,0:T(8,128)(2,1)}, f32[256,2048]{1,0:T(8,128)S(1)}, /*index=5*/bf16[256,2048]{1,0:T(8,128)(2,1)S(1)}) custom-call(bf16[256,2048]{1,0:T(8,128)(2,1)S(1)} %fusion.12.refs_0_, ...), custom_call_target="tpu_custom_call", output_to_operand_aliasing={{0}: (5, {}), {1}: (6, {}), {2}: (7, {}), {3}: (8, {})} | custom-call | flops 1024 | bytes 1024 | tf_op jit(solution)/shard_map/mlp/pallas_call | solution.py:233
  373.7 18.7 %collective-permute-done.32 = s32[256,1]{0,1:T(1,128)S(1)} collective-permute-done((s32[256,1]{0,1:T(1,128)S(1)}, s32[256,1]{0,1:T(1,128)S(1)}, u32[]{:S(2)}, u32[]{:S(2)}) %collective-permute-start.32) | collective-permute-done | bytes 1056 | tf_op jit(solution)/shard_map/ppermute | solution.py:508
  417.6 12.5 %collective-permute-done.37.refs_0_.refs_1_ = bf16[256,2048]{1,0:T(8,128)(2,1)S(1)} collective-permute-done((bf16[256,2048]{1,0:T(8,128)(2,1)S(1)}, bf16[256,2048]{1,0:T(8,128)(2,1)S(1)}, u32[]{:S(2)}, u32[]{:S(2)}) %collective-permute-start.37) | collective-permute-done | bytes 1048608 | tf_op jit(solution)/shard_map/ppermute | solution.py:493
  445.7 29.2 %mlp_back.2 = (bf16[1024,2048]{1,0:T(8,128)(2,1)}, bf16[1024,2048]{1,0:T(8,128)(2,1)}, bf16[1024,2048]{1,0:T(8,128)(2,1)}, bf16[256,2048]{1,0:T(8,128)(2,1)}, bf16[256,2048]{1,0:T(8,128)(2,1)}) custom-call(bf16[256,2048]{1,0:T(8,128)(2,1)S(1)} %copy-done.14, bf16[256,2048]{1,0:T(8,128)(2,1)S(1)} %copy-done.17, f32[1024,2048]{1,0:T(8,128)} %get-tuple-element.348.refs_2_, ...), custom_call_target="tpu_custom_call" | custom-call | flops 1024 | bytes 1024 | tf_op jit(solution)/shard_map/mlp_back/pallas_call | solution.py:294
  484.3 29.1 %mlp_back.3 = (bf16[1024,2048]{1,0:T(8,128)(2,1)}, bf16[1024,2048]{1,0:T(8,128)(2,1)}, bf16[1024,2048]{1,0:T(8,128)(2,1)}, f32[256,2048]{1,0:T(8,128)S(1)}, bf16[256,2048]{1,0:T(8,128)(2,1)}) custom-call(bf16[256,2048]{1,0:T(8,128)(2,1)S(1)} %get-tuple-element.355.refs_0_.refs_3_, ...), custom_call_target="tpu_custom_call", output_to_operand_aliasing={{0}: (7, {}), {1}: (8, {}), {2}: (9, {})} | custom-call | flops 1024 | bytes 1024 | tf_op jit(solution)/shard_map/mlp_back/pallas_call | solution.py:294
  527.4 10.1 %outer.13 = bf16[2048,1024]{1,0:T(8,128)(2,1)} custom-call(s32[1]{0:T(128)} %bitcast.26.which, bf16[1024,2048]{1,0:T(8,128)(2,1)} %get-tuple-element.373.refs_0_, bf16[1024,2048]{1,0:T(8,128)(2,1)} %get-tuple-element.394.refs_1_), custom_call_target="tpu_custom_call" | custom-call | flops 1024 | bytes 1024 | tf_op jit(solution)/shard_map/outer/pallas_call | solution.py:339
  537.6 10.4 %outer.12 = bf16[2048,1024]{1,0:T(8,128)(2,1)} custom-call(s32[1]{0:T(128)} %bitcast.26.which, bf16[1024,2048]{1,0:T(8,128)(2,1)} %get-tuple-element.373.refs_0_, bf16[1024,2048]{1,0:T(8,128)(2,1)} %get-tuple-element.392.refs_1_), custom_call_target="tpu_custom_call" | custom-call | flops 1024 | bytes 1024 | tf_op jit(solution)/shard_map/outer/pallas_call | solution.py:339
  548.0 25.2 %collective-permute-done.46 = bf16[2,1,256,2048]{3,2,1,0:T(8,128)(2,1)S(1)} collective-permute-done((bf16[2,1,256,2048]{3,2,1,0:T(8,128)(2,1)}, bf16[2,1,256,2048]{3,2,1,0:T(8,128)(2,1)S(1)}, u32[]{:S(2)}, u32[]{:S(2)}) %collective-permute-start.46) | collective-permute-done | bytes 2097184 | tf_op jit(solution)/shard_map/ppermute | solution.py:490
  586.7 35.9 %collective-permute-done.47.refs_1_.refs_2_ = bf16[256,2048]{1,0:T(8,128)(2,1)S(1)} collective-permute-done((bf16[256,2048]{1,0:T(8,128)(2,1)S(1)}, bf16[256,2048]{1,0:T(8,128)(2,1)S(1)}, u32[]{:S(2)}, u32[]{:S(2)}) %collective-permute-start.47) | collective-permute-done | bytes 1048608 | tf_op jit(solution)/shard_map/ppermute | solution.py:493
  670.0 27.3 %attend_back.1 = bf16[4,1,2,128,1536]{4,3,2,1,0:T(8,128)(2,1)} custom-call(s32[8]{0:T(128)} %fusion.41.order, f32[4,1,2,128,1536]{4,3,2,1,0:T(8,128)} %bitcast.143, f32[4,1,2,128,512]{4,3,2,1,0:T(8,128)} %get-tuple-element.266.lse, bf16[4,1,2,128,512]{4,3,2,1,0:T(8,128)(2,1)} %bitcast.123, f32[1024,128]{1,0:T(8,128)} %get-tuple-element.530.cos, ...), custom_call_target="tpu_custom_call" | custom-call | flops 1024 | bytes 1024 | tf_op jit(solution)/shard_map/attend_back/pallas_call | solution.py:177
  735.7 29.3 %collective-permute-done.58 = bf16[2,2,1,2,2,64,1024]{6,5,4,3,2,1,0:T(8,128)(2,1)S(1)} collective-permute-done((bf16[2,2,1,2,2,64,1024]{6,5,4,3,2,1,0:T(8,128)(2,1)}, bf16[2,2,1,2,2,64,1024]{6,5,4,3,2,1,0:T(8,128)(2,1)S(1)}, u32[]{:S(2)}, u32[]{:S(2)}) %collective-permute-start.58) | collective-permute-done | bytes 2097184 | tf_op jit(solution)/shard_map/ppermute | solution.py:490
  796.3 34.5 %collective-permute-done.65 = bf16[1,2,1,2,2,64,1024]{6,5,4,3,2,1,0:T(8,128)(2,1)} collective-permute-done((bf16[1,2,1,2,2,64,1024]{6,5,4,3,2,1,0:T(8,128)(2,1)}, bf16[1,2,1,2,2,64,1024]{6,5,4,3,2,1,0:T(8,128)(2,1)}, u32[]{:S(2)}, u32[]{:S(2)}) %collective-permute-start.65) | collective-permute-done | bytes 1048608 | tf_op jit(solution)/shard_map/ppermute | solution.py:493
  865.0 40.7 %collective-permute-done.68 = bf16[1,2,1,2,2,64,768]{6,5,4,3,2,1,0:T(8,128)(2,1)S(1)} collective-permute-done((bf16[1,2,1,2,2,64,768]{6,5,4,3,2,1,0:T(8,128)(2,1)S(1)}, bf16[1,2,1,2,2,64,768]{6,5,4,3,2,1,0:T(8,128)(2,1)S(1)}, u32[]{:S(2)}, u32[]{:S(2)}) %collective-permute-start.68) | collective-permute-done | bytes 786464 | tf_op jit(solution)/shard_map/ppermute | solution.py:493
  905.9 22.2 %collective-permute-done.66 = bf16[256,2048]{1,0:T(8,128)(2,1)S(1)} collective-permute-done((bf16[256,2048]{1,0:T(8,128)(2,1)S(1)}, bf16[256,2048]{1,0:T(8,128)(2,1)S(1)}, u32[]{:S(2)}, u32[]{:S(2)}) %collective-permute-start.66) | collective-permute-done | bytes 1048608 | tf_op jit(solution)/shard_map/ppermute | solution.py:508
  (433 shorter events, 427.1 us)
Async XLA Ops:
  9.5 53.2 %collective-permute-start.2 = (bf16[256,4096]{1,0:T(8,128)(2,1)}, bf16[256,4096]{1,0:T(8,128)(2,1)S(1)}, u32[]{:S(2)}, u32[]{:S(2)}) collective-permute-start(bf16[256,4096]{1,0:T(8,128)(2,1)} %get-tuple-element.286.refs_0_), channel_id=1, source_target_pairs={{0,4},{1,5},{2,6},{3,7},{4,0},{5,1},{6,2},{7,3},{8,12},{9,13},{10,... | collective-permute-start | bytes 6291464 | tf_op jit(solution)/shard_map/ppermute | solution.py:490
  13.8 46.6 %collective-permute-start = (bf16[256,2048]{1,0:T(8,128)(2,1)}, bf16[256,2048]{1,0:T(8,128)(2,1)}, u32[]{:S(2)}, u32[]{:S(2)}) collective-permute-start(bf16[256,2048]{1,0:T(8,128)(2,1)} %bitcast.1), channel_id=1, source_target_pairs={{2,16},{3,17},{6,20},{7,21},{10,24},{11,25},{14,28},{15,29},{16,2}... | collective-permute-start | bytes 3145736 | tf_op jit(solution)/shard_map/ppermute | solution.py:508
  104.2 51.9 %collective-permute-start.11 = (bf16[512,1536]{1,0:T(8,128)(2,1)}, bf16[512,1536]{1,0:T(8,128)(2,1)}, u32[]{:S(2)}, u32[]{:S(2)}) collective-permute-start(bf16[512,1536]{1,0:T(8,128)(2,1)} %collective-permute-done.6.refs_2_), channel_id=1, source_target_pairs={{0,1},{1,0},{2,3},{3,2},{4,5},{5,4},{6,7},{7,6},{8,9},{9,8},{10,11... | collective-permute-start | bytes 4718600 | tf_op jit(solution)/shard_map/ppermute | solution.py:490
  108.3 47.8 %collective-permute-start.10 = (bf16[256,2048]{1,0:T(8,128)(2,1)S(1)}, bf16[256,2048]{1,0:T(8,128)(2,1)S(1)}, u32[]{:S(2)}, u32[]{:S(2)}) collective-permute-start(bf16[256,2048]{1,0:T(8,128)(2,1)S(1)} %get-tuple-element.482), channel_id=1, source_target_pairs={{0,2},{1,3},{2,0},{3,1},{4,6},{5,7},{6,4},{7,5},{8,10},{9,11},{10,... | collective-permute-start | bytes 3145736 | tf_op jit(solution)/shard_map/ppermute | solution.py:490
  108.4 47.8 %collective-permute-start.8 = (bf16[256,2048]{1,0:T(8,128)(2,1)S(1)}, bf16[256,2048]{1,0:T(8,128)(2,1)S(1)}, u32[]{:S(2)}, u32[]{:S(2)}) collective-permute-start(bf16[256,2048]{1,0:T(8,128)(2,1)S(1)} %fusion.4.refs_0_), channel_id=1, source_target_pairs={{0,10},{1,11},{2,8},{3,9},{4,14},{5,15},{6,12},{7,13},{8,2},{9,3},... | collective-permute-start | bytes 3145736 | tf_op jit(solution)/shard_map/ppermute | solution.py:501
  157.3 56.9 %collective-permute-start.12 = (bf16[256,2048]{1,0:T(8,128)(2,1)}, bf16[256,2048]{1,0:T(8,128)(2,1)}, u32[]{:S(2)}, u32[]{:S(2)}) collective-permute-start(bf16[256,2048]{1,0:T(8,128)(2,1)} %add.348), channel_id=1, source_target_pairs={{0,1},{1,0},{2,3},{3,2},{4,5},{5,4},{6,7},{7,6},{8,9},{9,8},{10,11... | collective-permute-start | bytes 3145736 | tf_op jit(solution)/shard_map/ppermute | solution.py:490
  158.4 65.9 %collective-permute-start.14 = (bf16[512,2048]{1,0:T(8,128)(2,1)}, bf16[512,2048]{1,0:T(8,128)(2,1)}, u32[]{:S(2)}, u32[]{:S(2)}) collective-permute-start(bf16[512,2048]{1,0:T(8,128)(2,1)} %constant_dynamic-update-slice_fusion.refs_0_), channel_id=1, source_target_pairs={{0,4},{1,5},{2,6},{3,7},{4,0},{5,1},{6,2},{7,3},{8,12},{9,13},{10,... | collective-permute-start | bytes 6291464 | tf_op jit(solution)/shard_map/ppermute | solution.py:490
  158.4 70.8 %collective-permute-start.13 = (bf16[256,4096]{1,0:T(8,128)(2,1)}, bf16[256,4096]{1,0:T(8,128)(2,1)}, u32[]{:S(2)}, u32[]{:S(2)}) collective-permute-start(bf16[256,4096]{1,0:T(8,128)(2,1)} %get-tuple-element.273), channel_id=1, source_target_pairs={{0,2},{1,3},{2,0},{3,1},{4,6},{5,7},{6,4},{7,5},{8,10},{9,11},{10,... | collective-permute-start | bytes 6291464 | tf_op jit(solution)/shard_map/ppermute | solution.py:490
  166.8 55.5 %collective-permute-start.15 = (bf16[256,2048]{1,0:T(8,128)(2,1)S(1)}, bf16[256,2048]{1,0:T(8,128)(2,1)S(1)}, u32[]{:S(2)}, u32[]{:S(2)}) collective-permute-start(bf16[256,2048]{1,0:T(8,128)(2,1)S(1)} %bitcast.161), channel_id=1, source_target_pairs={{2,16},{3,17},{6,20},{7,21},{10,24},{11,25},{14,28},{15,29},{16,2}... | collective-permute-start | bytes 3145736 | tf_op jit(solution)/shard_map/ppermute | solution.py:508
  234.3 47.6 %collective-permute-start.21 = (bf16[256,4096]{1,0:T(8,128)(2,1)}, bf16[256,4096]{1,0:T(8,128)(2,1)}, u32[]{:S(2)}, u32[]{:S(2)}) collective-permute-start(bf16[256,4096]{1,0:T(8,128)(2,1)} %collective-permute-done.13.refs_2_), channel_id=1, source_target_pairs={{0,4},{1,5},{2,6},{3,7},{4,0},{5,1},{6,2},{7,3},{8,12},{9,13},{10,... | collective-permute-start | bytes 6291464 | tf_op jit(solution)/shard_map/ppermute | solution.py:490
  525.5 47.7 %collective-permute-start.46 = (bf16[2,1,256,2048]{3,2,1,0:T(8,128)(2,1)}, bf16[2,1,256,2048]{3,2,1,0:T(8,128)(2,1)S(1)}, u32[]{:S(2)}, u32[]{:S(2)}) collective-permute-start(bf16[2,1,256,2048]{3,2,1,0:T(8,128)(2,1)} %constant_dynamic-slice_fusion.9), channel_id=1, source_target_pairs={{0,4},{1,5},{2,6},{3,7},{4,0},{5,1},{6,2},{7,3},{8,12},{9,13},{10,... | collective-permute-start | bytes 6291464 | tf_op jit(solution)/shard_map/ppermute | solution.py:490
  526.8 48.6 %collective-permute-start.45 = (bf16[256,2048]{1,0:T(8,128)(2,1)}, bf16[256,2048]{1,0:T(8,128)(2,1)}, u32[]{:S(2)}, u32[]{:S(2)}) collective-permute-start(bf16[256,2048]{1,0:T(8,128)(2,1)} %get-tuple-element.372), channel_id=1, source_target_pairs={{0,10},{1,11},{2,8},{3,9},{4,14},{5,15},{6,12},{7,13},{8,2},{9,3},... | collective-permute-start | bytes 3145736 | tf_op jit(solution)/shard_map/ppermute | solution.py:501
  656.3 55.5 %collective-permute-start.53 = (bf16[2,2,1,2,2,64,1024]{6,5,4,3,2,1,0:T(8,128)(2,1)}, bf16[2,2,1,2,2,64,1024]{6,5,4,3,2,1,0:T(8,128)(2,1)}, u32[]{:S(2)}, u32[]{:S(2)}) collective-permute-start(bf16[2,2,1,2,2,64,1024]{6,5,4,3,2,1,0:T(8,128)(2,1)} %constant_dynamic-slice_fusion.7), channel_id=1, source_target_pairs={{0,4},{1,5},{2,6},{3,7},{4,0},{5,1},{6,2},{7,3},{8,12},{9,13},{10,... | collective-permute-start | bytes 6291464 | tf_op jit(solution)/shard_map/ppermute | solution.py:490
  657.9 50.9 %collective-permute-start.54 = (bf16[256,2048]{1,0:T(8,128)(2,1)}, bf16[256,2048]{1,0:T(8,128)(2,1)}, u32[]{:S(2)}, u32[]{:S(2)}) collective-permute-start(bf16[256,2048]{1,0:T(8,128)(2,1)} %get-tuple-element.403), channel_id=1, source_target_pairs={{2,16},{3,17},{6,20},{7,21},{10,24},{11,25},{14,28},{15,29},{16,2}... | collective-permute-start | bytes 3145736 | tf_op jit(solution)/shard_map/ppermute | solution.py:508
  716.8 48.2 %collective-permute-start.58 = (bf16[2,2,1,2,2,64,1024]{6,5,4,3,2,1,0:T(8,128)(2,1)}, bf16[2,2,1,2,2,64,1024]{6,5,4,3,2,1,0:T(8,128)(2,1)S(1)}, u32[]{:S(2)}, u32[]{:S(2)}) collective-permute-start(bf16[2,2,1,2,2,64,1024]{6,5,4,3,2,1,0:T(8,128)(2,1)} %constant_dynamic-slice_fusion.6), channel_id=1, source_target_pairs={{0,4},{1,5},{2,6},{3,7},{4,0},{5,1},{6,2},{7,3},{8,12},{9,13},{10,... | collective-permute-start | bytes 6291464 | tf_op jit(solution)/shard_map/ppermute | solution.py:490
  718.4 49.5 %collective-permute-start.59 = (bf16[1,2,1,2,2,64,1024]{6,5,4,3,2,1,0:T(8,128)(2,1)}, bf16[1,2,1,2,2,64,1024]{6,5,4,3,2,1,0:T(8,128)(2,1)}, u32[]{:S(2)}, u32[]{:S(2)}) collective-permute-start(bf16[1,2,1,2,2,64,1024]{6,5,4,3,2,1,0:T(8,128)(2,1)} %constant_dynamic-slice_fusion.5), channel_id=1, source_target_pairs={{0,16},{8,24},{16,0},{24,8},{1,17},{9,25},{17,1},{25,9},{2,18},{10... | collective-permute-start | bytes 3145736 | tf_op jit(solution)/shard_map/ppermute | solution.py:493
  728.8 51.3 %collective-permute-start.56 = (bf16[256,2048]{1,0:T(8,128)(2,1)S(1)}, bf16[256,2048]{1,0:T(8,128)(2,1)}, u32[]{:S(2)}, u32[]{:S(2)}) collective-permute-start(bf16[256,2048]{1,0:T(8,128)(2,1)S(1)} %get-tuple-element.413), channel_id=1, source_target_pairs={{0,8},{8,0},{16,24},{24,16},{1,9},{9,1},{17,25},{25,17},{2,10},{10... | collective-permute-start | bytes 3145736 | tf_op jit(solution)/shard_map/ppermute | solution.py:493
  730.1 50.0 %collective-permute-start.57 = (bf16[256,2048]{1,0:T(8,128)(2,1)S(1)}, bf16[256,2048]{1,0:T(8,128)(2,1)}, u32[]{:S(2)}, u32[]{:S(2)}) collective-permute-start(bf16[256,2048]{1,0:T(8,128)(2,1)S(1)} %get-tuple-element.414), channel_id=1, source_target_pairs={{0,2},{1,3},{2,0},{3,1},{4,6},{5,7},{6,4},{7,5},{8,10},{9,11},{10,... | collective-permute-start | bytes 3145736 | tf_op jit(solution)/shard_map/ppermute | solution.py:490
  782.9 49.6 %collective-permute-start.61 = (bf16[2,2,1,2,2,64,768]{6,5,4,3,2,1,0:T(8,128)(2,1)}, bf16[2,2,1,2,2,64,768]{6,5,4,3,2,1,0:T(8,128)(2,1)}, u32[]{:S(2)}, u32[]{:S(2)}) collective-permute-start(bf16[2,2,1,2,2,64,768]{6,5,4,3,2,1,0:T(8,128)(2,1)} %constant_dynamic-slice_fusion.4), channel_id=1, source_target_pairs={{0,4},{1,5},{2,6},{3,7},{4,0},{5,1},{6,2},{7,3},{8,12},{9,13},{10,... | collective-permute-start | bytes 4718600 | tf_op jit(solution)/shard_map/ppermute | solution.py:490
  791.1 47.6 %collective-permute-start.60 = (bf16[256,2048]{1,0:T(8,128)(2,1)}, bf16[256,2048]{1,0:T(8,128)(2,1)S(1)}, u32[]{:S(2)}, u32[]{:S(2)}) collective-permute-start(bf16[256,2048]{1,0:T(8,128)(2,1)} %get-tuple-element.424), channel_id=1, source_target_pairs={{0,10},{1,11},{2,8},{3,9},{4,14},{5,15},{6,12},{7,13},{8,2},{9,3},... | collective-permute-start | bytes 3145736 | tf_op jit(solution)/shard_map/ppermute | solution.py:501
  848.2 57.4 %collective-permute-start.68 = (bf16[1,2,1,2,2,64,768]{6,5,4,3,2,1,0:T(8,128)(2,1)S(1)}, bf16[1,2,1,2,2,64,768]{6,5,4,3,2,1,0:T(8,128)(2,1)S(1)}, u32[]{:S(2)}, u32[]{:S(2)}) collective-permute-start(bf16[1,2,1,2,2,64,768]{6,5,4,3,2,1,0:T(8,128)(2,1)S(1)} %constant_dynamic-slice_fusion.1), channel_id=1, source_target_pairs={{0,16},{8,24},{16,0},{24,8},{1,17},{9,25},{17,1},{25,9},{2,18},{10... | collective-permute-start | bytes 2359304 | tf_op jit(solution)/shard_map/ppermute | solution.py:493
  853.8 74.2 %collective-permute-start.66 = (bf16[256,2048]{1,0:T(8,128)(2,1)S(1)}, bf16[256,2048]{1,0:T(8,128)(2,1)S(1)}, u32[]{:S(2)}, u32[]{:S(2)}) collective-permute-start(bf16[256,2048]{1,0:T(8,128)(2,1)S(1)} %fusion.9), channel_id=1, source_target_pairs={{2,16},{3,17},{6,20},{7,21},{10,24},{11,25},{14,28},{15,29},{16,2}... | collective-permute-start | bytes 3145736 | tf_op jit(solution)/shard_map/ppermute | solution.py:508
  855.7 73.1 %collective-permute-start.69 = (bf16[64,2048]{1,0:T(8,128)(2,1)S(1)}, bf16[64,2048]{1,0:T(8,128)(2,1)S(1)}, u32[]{:S(2)}, u32[]{:S(2)}) collective-permute-start(bf16[64,2048]{1,0:T(8,128)(2,1)S(1)} %get-tuple-element.442), channel_id=1, source_target_pairs={{0,8},{8,0},{16,24},{24,16},{1,9},{9,1},{17,25},{25,17},{2,10},{10... | collective-permute-start | bytes 786440 | tf_op jit(solution)/shard_map/ppermute | solution.py:493
  856.6 72.2 %collective-permute-start.70 = (bf16[64,2048]{1,0:T(8,128)(2,1)S(1)}, bf16[64,2048]{1,0:T(8,128)(2,1)S(1)}, u32[]{:S(2)}, u32[]{:S(2)}) collective-permute-start(bf16[64,2048]{1,0:T(8,128)(2,1)S(1)} %get-tuple-element.443), channel_id=1, source_target_pairs={{0,2},{1,3},{2,0},{3,1},{4,6},{5,7},{6,4},{7,5},{8,10},{9,11},{10,... | collective-permute-start | bytes 786440 | tf_op jit(solution)/shard_map/ppermute | solution.py:490
  (134 other events, 2358.4 us)

commit v3 on v2

--- a/solution.py
+++ b/solution.py
@@ -571,14 +571,35 @@
 
         return first, rest
 
-    def gather_group(own):
-        return [own] + [hop(own, j) for j in range(1, planes)]
-
     cut = planes // 2
     early = list(range(1, cut + 1))
     late = [0, *range(cut + 1, planes)]
     early_types = [BF] * cut
     late_types = [F32] + [BF] * (planes - cut - 1)
+
+    def gather_far(found):
+        if near != 2:
+            return [hop(found[0], j) for j in late[1:]]
+        half = rows // 2
+        return [hop(found[1][:half], 2), hop(found[2][half:], 1)]
+
+    def joined(found, others):
+        return found + (others if near != 2 else [jnp.concatenate(others, 0)])
+
+    def reduce_far(parts):
+        if near != 2:
+            return [hop(parts[j], j) for j in late[1:]]
+        half = rows // 2
+        return [hop(parts[3][:half], 2), hop(parts[3][half:], 1)]
+
+    def reduce_near(parts, received):
+        if near != 2:
+            return add_all(parts[0], received), [hop(parts[j], j) for j in early]
+        half = rows // 2
+        more = lambda part, other: (part.astype(F32) + other.astype(F32)).astype(BF)
+        to_low = jnp.concatenate([more(parts[1][:half], received[0]), parts[1][half:]], 0)
+        to_x = jnp.concatenate([parts[2][:half], more(parts[2][half:], received[1])], 0)
+        return parts[0], [hop(to_low, 1), hop(to_x, 2)]
 
     def add_all(total, others):
         for other in others:
@@ -593,36 +614,33 @@
     qkv_other = flip(head_columns(group ^ near), 2)
     gu_own_y = over_y(gu_own)
     heads_first, heads_rest = own_heads(w_out)
-    stream_low, qkv_own, qkv_other, gu_own, gu_own_y, gu_send, heads_first, w_down = region(
-        stream_low, qkv_own, qkv_other, gu_own, gu_own_y, gu_send, heads_first, w_down
-    )
     stream = stream_low.astype(F32)
     normed_one, inverse_one = normalize(stream)
     qkv_both = jnp.concatenate([qkv_own, qkv_other], 0)
-    h1, qkv_both = region([normed_one.astype(BF)], qkv_both)
+    h1, stream_low, qkv_both, gu_own, gu_own_y, gu_send, heads_first, w_down = region(
+        [normed_one.astype(BF)], stream_low, qkv_both, gu_own, gu_own_y, gu_send, heads_first, w_down
+    )
 
     h1 = h1 + [hop(h1[0], j) for j in early]
     qkv_y = over_y(qkv_both)
     qkv_pair = flip(qkv_both, 1)
-    h1, qkv_both, qkv_y, qkv_pair, heads_first, w_down, gu_send = region(
-        h1, qkv_both, qkv_y, qkv_pair, heads_first, w_down, gu_send
-    )
-
-    h1 = h1 + [hop(h1[0], j) for j in late[1:]]
     found = heads_rest(heads_first)
+    h1, qkv_both, qkv_pair, w_down, gu_send = region(h1, qkv_both, qkv_pair, w_down, gu_send)
+
+    others = gather_far(h1)
     down_own = ff_rows(group)
     down_other = flip(ff_rows(group ^ near), 2)
-    qkv_y_pair = [flip(v, 1) for v in qkv_y]
-    h1, found, down_own, down_other, qkv_y_pair, gu_send, gu_own_y, teacher = region(
-        h1, found, down_own, down_other, qkv_y_pair, gu_send, gu_own_y, teacher
-    )
+    others, found, down_own, down_other, qkv_y, gu_send, gu_own_y, teacher = region(
+        others, found, down_own, down_other, qkv_y, gu_send, gu_own_y, teacher
+    )
+    h1 = joined(h1, others)
 
     gu_other = flip(gu_send, 2)
     down_both = jnp.concatenate([down_own, down_other], 0)
     down_y = over_y(down_both)
     other = flip(found, 1)
+    qkv_y_pair = [flip(v, 1) for v in qkv_y]
     w_qkv = put_pairs(qkv_both, qkv_y, qkv_pair, qkv_y_pair)
-    goal_low = swap(teacher.reshape(rows, width))
     (qkv,) = project(h1, w_qkv, False, [F32])
     qkv = qkv.reshape(planes, seqs, slots, blk, 3 * mine)
     mixed, lse = attend(order, qkv, cos, sin, heads)
@@ -630,11 +648,11 @@
     w_out_mine = jnp.concatenate([jnp.where(even, found, other), jnp.where(even, other, found)], 0)
     group_types = [F32] + [BF] * (planes - 1)
     products = project([mixed[s].reshape(rows, mine) for s in range(planes)], w_out_mine, False, group_types)
-    products, gu_other, down_both, down_y, gu_own, gu_own_y, goal_low = region(
-        products, gu_other, down_both, down_y, gu_own, gu_own_y, goal_low
-    )
-
-    received = [hop(products[j], j) for j in early]
+    products, gu_other, down_both, down_y, gu_own, gu_own_y, teacher = region(
+        products, gu_other, down_both, down_y, gu_own, gu_own_y, teacher
+    )
+
+    received = reduce_far(products)
     gu_other_y = over_y(gu_other)
     down_pair = flip(down_both, 1)
     gu_own_pair = flip(gu_own, 1)
@@ -642,47 +660,48 @@
         received, products, down_pair, gu_other, down_y, gu_own_pair, gu_own_y
     )
 
-    received = received + [hop(products[j], j) for j in late[1:]]
+    own, received = reduce_near(products, received)
     down_y_pair = [flip(v, 1) for v in down_y]
     gu_own_y_pair = [flip(v, 1) for v in gu_own_y]
+    residual = stream + add_all(own, received)
+    normed_two, inverse_two = normalize(residual)
+    h2, gu_other_y, gu_other, down_y_pair, gu_own_y_pair, valid = region(
+        [normed_two.astype(BF)], gu_other_y, gu_other, down_y_pair, gu_own_y_pair, valid
+    )
+
+    h2 = h2 + [hop(h2[0], j) for j in early]
     gu_other_pair = flip(gu_other, 1)
-    received, gu_other_y, down_y_pair, gu_own_y_pair, gu_other_pair, valid = region(
-        received, gu_other_y, down_y_pair, gu_own_y_pair, gu_other_pair, valid
-    )
-    residual = stream + add_all(products[0], received)
-    normed_two, inverse_two = normalize(residual)
-    h2, gu_other_y = region([normed_two.astype(BF)], gu_other_y)
-
-    h2 = h2 + [hop(h2[0], j) for j in early]
     gu_items = [(gu_own, [0]), (gu_own_pair, [1]), (gu_other, [2]), (gu_other_pair, [3])]
     for bits, v, w, z in zip(y_bits, gu_own_y, gu_own_y_pair, gu_other_y):
         gu_items += [(v, [bits]), (w, [bits + 1]), (z, [bits + 2]), (flip(z, 1), [bits + 3])]
     down_w = put_pairs(down_both, down_y, down_pair, down_y_pair)
     gu_w = put(*gu_items)
-    h2, gu_w, down_w, valid = region(h2, gu_w, down_w, valid)
-
-    h2 = h2 + [hop(h2[0], j) for j in late[1:]]
+    h2, gu_w, down_w, valid, teacher = region(h2, gu_w, down_w, valid, teacher)
+
+    others = gather_far(h2)
+    goal_low = swap(teacher.reshape(rows, width))
     kept, outs = mlp([h2[j] for j in early], gu_w, down_w, early_types, 2, 0)
-    outs, kept, far_tokens = region(outs, kept, h2[cut + 1 :])
-    h2 = h2[: cut + 1] + far_tokens
+    outs, kept, others = region(outs, kept, others)
+    h2 = joined(h2, others)
 
     received = [hop(v, j) for v, j in zip(outs, early)]
     (h2_all, gates, ups, hidden_all), outs = mlp(
         [h2[j] for j in late], gu_w, down_w, late_types, 2, 1, kept
     )
-    received, outs, h2_all, gates, ups, hidden_all, valid = region(
-        received, outs, h2_all, gates, ups, hidden_all, valid
+    received, outs, h2_all, gates, ups, hidden_all, valid, goal_low = region(
+        received, outs, h2_all, gates, ups, hidden_all, valid, goal_low
     )
 
     received = received + [hop(v, j) for v, j in zip(outs[1:], late[1:])]
     valid_float = swap(valid.reshape(rows, 1)).astype(F32)
-    received, own, valid_float = region(received, outs[0], valid_float)
-
-    output = residual + add_all(own, received)
+
+    output = residual + add_all(outs[0], received)
     deviation = output - goal_low.astype(F32)
     grad_output = valid_float * deviation
     sums = jnp.stack([jnp.sum(grad_output * deviation), jnp.sum(valid_float)])
     sums0 = jnp.broadcast_to(sums[:, None, None], (2, 8, HD))
+    sums0, grad_output, output = region(sums0, grad_output, output)
+
     sums = sums0
     for j in range(1, planes):
         sums = sums + hop(sums0, j)
@@ -738,10 +757,10 @@
         sums = sums + flip(sums, bits)
     dm, sums, low_output = region(dm, sums, low_output)
 
-    dm = dm + [hop(dm[0], j) for j in late[1:]]
+    others = gather_far(dm)
     kept, backs = mlp_back([dm[j] for j in early], gates, ups, gu_w, down_w, early_types, 2, 0)
-    backs, kept, far_tokens, sums = region(backs, kept, dm[cut + 1 :], sums)
-    dm = dm[: cut + 1] + far_tokens
+    backs, kept, others, sums, low_output = region(backs, kept, others, sums, low_output)
+    dm = joined(dm, others)
 
     received = [hop(v, j) for v, j in zip(backs, early)]
     dm_runs = [dm[j] for j in early + late]
@@ -750,87 +769,102 @@
         [dm[j] for j in late], gates, ups, gu_w, down_w, late_types, 2, 1, kept
     )
     g_down = outer([hidden_all], dm_runs, core, True, away, 2)
-    received, backs, g_down, dg_all, du_all, h2_all = region(received, backs, g_down, dg_all, du_all, h2_all)
+    received, backs, g_down, dg_all, du_all, h2_all, low_output = region(
+        received, backs, g_down, dg_all, du_all, h2_all, low_output
+    )
 
     received = received + [hop(v, j) for v, j in zip(backs[1:], late[1:])]
+    activations = swap(low_output)
     g_down = across_y(g_down.reshape(2, shards // 4, part_ff // shards, width), 1)
     gate_half = outer([h2_all], [dg_all], 1 - core, False)
     up_half = outer([h2_all], [du_all], 1 - core, False)
-    received, gate_half, up_half, dg_all, du_all, g_down = region(received, gate_half, up_half, dg_all, du_all, g_down)
     grad_two = add_all(backs[0], received)
     grad_residual = grad_output + norm_back(grad_two, normed_two, inverse_two)
-    dab, gate_half, up_half, g_down = region([grad_residual.astype(BF)], gate_half, up_half, g_down)
+    dab, gate_half, up_half, g_down, dg_all, du_all, activations = region(
+        [grad_residual.astype(BF)], gate_half, up_half, g_down, dg_all, du_all, activations
+    )
 
     dab = dab + [hop(dab[0], j) for j in early]
     gate_away, up_away = flip(gate_half, 1), flip(up_half, 1)
+    g_gate = outer([h2_all], [dg_all], core, False, gate_away)
+    dab, g_gate, up_away, du_all, g_down = region(dab, g_gate, up_away, du_all, g_down)
+
+    others = gather_far(dab)
+    g_gate = across_y(parts(g_gate), 2)
+    g_up = outer([h2_all], [du_all], core, False, up_away)
+    others, g_up, g_down = region(others, g_up, g_down)
+    dab = joined(dab, others)
+
+    up_first, up_second = jnp.split(parts(g_up), 2, -1)
+    up_first = across_y(up_first, 2)
     g_down = across_far(g_down)
-    dab, gate_away, up_away, dg_all, du_all, low_output = region(dab, gate_away, up_away, dg_all, du_all, low_output)
-
-    dab = dab + [hop(dab[0], j) for j in late[1:]]
-    g_gate = parts(outer([h2_all], [dg_all], core, False, gate_away))
-    g_up = parts(outer([h2_all], [du_all], core, False, up_away))
-    dab, g_gate, g_up, g_down, low_output = region(dab, g_gate, g_up, g_down, low_output)
-
-    activations = swap(low_output)
-    g_gate = across_y(g_gate, 2)
-    g_up = across_y(g_up, 2)
     (do,) = project(dab, w_out_mine, True, [BF])
     dqkv = attend_back(order, qkv, lse, do.reshape(planes, seqs, slots, blk, mine), cos, sin, heads)
     dqkv = dqkv.reshape(planes * rows, 3 * mine)
     qkv_half = outer(h1, [dqkv], 1 - core, False)
-    dqkv, qkv_half, g_gate, activations = region(dqkv, qkv_half, g_gate, activations)
-
-    qkv_away = flip(qkv_half, 1)
-    g_gate = across_far(g_gate)
-    backs = project([dqkv[i * rows : (i + 1) * rows] for i in range(planes)], w_qkv, True, group_types)
-    backs, dqkv, qkv_away, g_down = region(backs, dqkv, qkv_away, g_down)
-
-    received = [hop(backs[j], j) for j in early]
-    g_qkv = parts(outer(h1, [dqkv], core, False, qkv_away))
     mixed = mixed.reshape(planes * rows, mine)
     out_half = outer([mixed], dab, 1 - core, True)
+    dqkv, qkv_half, out_half, g_gate, g_down, up_first, up_second = region(
+        dqkv, qkv_half, out_half, g_gate, g_down, up_first, up_second
+    )
+
+    qkv_away, out_away = flip(qkv_half, 1), flip(out_half, 1)
+    backs = project([dqkv[i * rows : (i + 1) * rows] for i in range(planes)], w_qkv, True, group_types)
+    up_second = across_y(up_second, 2)
+    gate_first, gate_second = jnp.split(g_gate, 2, -1)
+    gate_first = across_far(gate_first)
+    backs, dqkv, qkv_away, out_away, up_second, gate_first, gate_second = region(
+        backs, dqkv, qkv_away, out_away, up_second, gate_first, gate_second
+    )
+
+    gate_second = across_far(gate_second)
+    g_up = jnp.concatenate([up_first, up_second], -1)
+    received = reduce_far(backs)
+    g_qkv = parts(outer(h1, [dqkv], core, False, qkv_away))
+    g_out = outer([mixed], dab, core, True, out_away)
+    received, backs, g_qkv, g_out, g_down, gate_first, gate_second, g_up = region(
+        received, backs, g_qkv, g_out, g_down, gate_first, gate_second, g_up
+    )
+
+    own, received = reduce_near(backs, received)
+    g_up = across_far(g_up)
+    g_out = across_y(g_out, 0)
+    g_gate = jnp.concatenate([gate_first, gate_second], -1)
     g_down = place_rows(
         g_down.reshape(ff // world, width),
         lambda core, y, far, g: far * (shards // 2) * planes + (core * (shards // 4) + y) * planes + g,
     )
-    received, backs, g_qkv, out_half, g_up, g_gate = region(received, backs, g_qkv, out_half, g_up, g_gate)
-
-    received = received + [hop(backs[j], j) for j in late[1:]]
+    grad_one = add_all(own, received)
+    grad_stream = grad_residual + norm_back(grad_one, normed_one, inverse_one)
+    low_stream, g_out, g_qkv, g_gate, g_up, g_down = region(
+        grad_stream.astype(BF), g_out, g_qkv, g_gate, g_up, g_down
+    )
+
+    grad_low = swap(low_stream)
     g_qkv = across_y(g_qkv, 2)
-    g_up = across_far(g_up)
-    out_away = flip(out_half, 1)
-    gate_core = core_away(g_gate)
-    received, g_qkv, out_away, gate_core, g_down, g_up = region(received, g_qkv, out_away, gate_core, g_down, g_up)
-    grad_one = add_all(backs[0], received)
-    grad_stream = grad_residual + norm_back(grad_one, normed_one, inverse_one)
-    g_out = outer([mixed], dab, core, True, out_away)
-    gate_pieces = column_pieces(core_joined(g_gate, gate_core))
-    low_stream, g_out, g_qkv, gate_pieces, g_up = region(grad_stream.astype(BF), g_out, g_qkv, gate_pieces, g_up)
-
-    grad_low = swap(low_stream)
+    g_out = across_far(g_out)
+    gate_core, up_core = core_away(g_gate), core_away(g_up)
+    pieces = [column_pieces(core_joined(v, w)) for v, w in ((g_gate, gate_core), (g_up, up_core))]
+    pieces = [jnp.concatenate(v, 1) for v in zip(*pieces)]
+    grad_low, g_qkv, g_out, pieces = region(grad_low, g_qkv, g_out, pieces)
+
     g_qkv = across_far(g_qkv)
-    g_out = across_y(g_out, 0)
-    gate_pieces = gate_pieces[:1] + [hop(gate_pieces[j], j) for j in early] + gate_pieces[cut + 1 :]
-    grad_low, g_out, g_up, g_qkv, gate_pieces = region(grad_low, g_out, g_up, g_qkv, gate_pieces)
-
+    g_out = place_rows(g_out, lambda core, y, far, g: g * shards + (core * (shards // 4) + y) * 2 + far)
+    pieces = [hop(v, j) if j else v for j, v in enumerate(pieces)]
+    pieces, g_qkv, g_out = region(pieces, g_qkv, g_out)
+    qkv_pieces = column_pieces(core_joined(g_qkv, core_away(g_qkv)))
+    qkv_pieces, pieces = region(qkv_pieces, pieces)
+    qkv_pieces = [hop(v, j) if j else v for j, v in enumerate(qkv_pieces)]
     count = sums[1, 0, 0]
     loss = sums[0, 0, 0] / (count * width)
     factor = (rows * world) / count
     grad_input = grad_low.astype(F32) * factor
     ff_order = lambda v: v.reshape(planes, unit, shards, -1).transpose(1, 2, 0, 3).reshape(unit, ff)
-    gate_pieces = gate_pieces[: cut + 1] + [hop(gate_pieces[j], j) for j in late[1:]]
-    up_core = core_away(g_up)
-    qkv_core = core_away(g_qkv)
-    g_out = across_far(g_out)
-    gate_pieces, up_core, qkv_core, g_out, g_qkv, g_up = region(gate_pieces, up_core, qkv_core, g_out, g_qkv, g_up)
-    up_pieces = [hop(v, j) if j else v for j, v in enumerate(column_pieces(core_joined(g_up, up_core)))]
-    g_gate = ff_order(columns_placed(gate_pieces)).astype(F32)
-    up_pieces, g_qkv, qkv_core, g_out = region(up_pieces, g_qkv, qkv_core, g_out)
-    qkv_pieces = [hop(v, j) if j else v for j, v in enumerate(column_pieces(core_joined(g_qkv, qkv_core)))]
-    g_out = place_rows(g_out, lambda core, y, far, g: g * shards + (core * (shards // 4) + y) * 2 + far)
-    g_up = ff_order(columns_placed(up_pieces)).astype(F32)
-    g_qkv = columns_placed(qkv_pieces).reshape(planes, unit, 3, mine).transpose(2, 1, 0, 3).reshape(3, unit, width)
-    g_qkv = g_qkv.astype(F32)
+    placed = columns_placed(pieces)
+    g_gate = ff_order(placed[:, :, :part_ff]).astype(F32)
+    g_up = ff_order(placed[:, :, part_ff:]).astype(F32)
+    g_qkv = columns_placed(qkv_pieces).reshape(planes, unit, 3, mine).transpose(2, 1, 0, 3)
+    g_qkv = g_qkv.reshape(3, unit, width).astype(F32)
     return (
         activations.reshape(tokens.shape),
         loss,

time: 1000 us -> 965 us (0.965)
  waiting for transfers between devices: 437 us -> 386 us
  starting transfers between devices: 111 us -> 133 us
    ppermute x18 -> x24, waiting for transfers between devices: 186 us -> 154 us  [flip_ctx(): return lax.ppermute(array, 'ctx', [(i, i ^ bits) for i in range(planes)])]
    ppermute x43 -> x49, waiting for transfers between devices: 140 us -> 117 us  [flip(): return lax.ppermute(array, 'fsdp', [(i, i ^ bits) for i in range(shards)])]
    ppermute x18 -> x24, starting transfers between devices: 29.2 us -> 51.7 us  [flip_ctx(): return lax.ppermute(array, 'ctx', [(i, i ^ bits) for i in range(planes)])]
    ppermute x43 -> x49, starting transfers between devices: 25 us -> 40.4 us  [flip(): return lax.ppermute(array, 'fsdp', [(i, i ^ bits) for i in range(shards)])]
    ppermute x12 -> x5, waiting for transfers between devices: 16.5 us -> 3.95 us  [hop(): lax.ppermute(array, both, [(p * shards + s, (p ^ dz) * shards + (s ^ 2))...]
    ppermute x1, waiting for transfers between devices: 15.6 us -> 26.8 us  [rest(): found = found + lax.ppermute(first, both, pairs_of)]
    ppermute x12 -> x5, starting transfers between devices: 25.2 us -> 15.1 us  [hop(): lax.ppermute(array, both, [(p * shards + s, (p ^ dz) * shards + (s ^ 2))...]
    pallas_call x6 -> x5, Pallas kernels: 33.7 us -> 31.7 us  [assemble(): pl.pallas_call(kernel, grid_spec=pltpu.PrefetchScalarGridSpec(num_scalar_...]
  transfers between devices with their start and end apart: 82 -> 87, of which waited for: 37 -> 45; matrix products, arithmetic and copies ran while one was open for 8% -> 9% of each run, Pallas kernels for 29% -> 29%
where the time goes in v3:
time: 965 us; the launch traced here: 959 us
  waiting for transfers between devices  386 us (40%)
  Pallas kernels  292 us (30%)
  starting transfers between devices  133 us (14%)
  other arithmetic  74.4 us (8%)
  local copies, waits for them, and re-layouts  68.2 us (7%)
    ppermute x24, waiting for transfers between devices, flip_ctx(): return lax.ppermute(array, 'ctx', [(i, i ^ bits) for i in range(planes)])  154 us
    ppermute x49, waiting for transfers between devices, flip(): return lax.ppermute(array, 'fsdp', [(i, i ^ bits) for i in range(shards)])  117 us
    ppermute x7, waiting for transfers between devices, send(): lax.ppermute(array, both, [(i, to) for i, to in enumerate(homes) if i !=...  85.3 us
    pallas_call x10, Pallas kernels, outer(): pl.pallas_call(kernel, grid_spec=pltpu.PrefetchScalarGridSpec(num_scalar_...  76.1 us
    pallas_call x2, Pallas kernels, mlp_back(): pl.pallas_call(functools.partial(down_kernel, count), grid=(tiles,), in_s...  57.5 us
    ppermute x24, starting transfers between devices, flip_ctx(): return lax.ppermute(array, 'ctx', [(i, i ^ bits) for i in range(planes)])  51.7 us
    pallas_call x2, Pallas kernels, mlp(): pl.pallas_call(functools.partial(up_kernel, count), grid=(tiles,), in_spe...  42 us
    ppermute x49, starting transfers between devices, flip(): return lax.ppermute(array, 'fsdp', [(i, i ^ bits) for i in range(shards)])  40.4 us
  transfers between devices with their start and end apart: 87, of which 45 were waited for; matrix products, arithmetic and copies ran while one was open for 9% of the time, Pallas kernels for 29%

profile of v3, /device:TPU:16, one launch (start us, length us, event | category | flops | bytes accessed | tf_op | source)
XLA Modules:
  0.0 959.2 jit_solution(13899371576709229723)
XLA Ops:
  18.7 27.3 %collective-permute-done.1 = bf16[256,1536]{1,0:T(8,128)(2,1)} collective-permute-done((bf16[256,1536]{1,0:T(8,128)(2,1)}, bf16[256,1536]{1,0:T(8,128)(2,1)}, u32[]{:S(2)}, u32[]{:S(2)}) %collective-permute-start.1) | collective-permute-done | bytes 786464 | tf_op jit(solution)/shard_map/ppermute | solution.py:490
  63.3 10.5 %collective-permute-start.4 = (bf16[256,2048]{1,0:T(8,128)(2,1)S(1)}, bf16[256,2048]{1,0:T(8,128)(2,1)S(1)}, u32[]{:S(2)}, u32[]{:S(2)}) collective-permute-start(bf16[256,2048]{1,0:T(8,128)(2,1)S(1)} %fusion.4.refs_0_), channel_id=1, source_target_pairs={{0,8},{8,0},{16,24},{24,16},{1,9},{9,1},{17,25},{25,17},{2,10},{10... | collective-permute-start | bytes 3145736 | tf_op jit(solution)/shard_map/ppermute | solution.py:493
  78.1 19.6 %collective-permute-done.4.refs_1_ = bf16[256,2048]{1,0:T(8,128)(2,1)S(1)} collective-permute-done((bf16[256,2048]{1,0:T(8,128)(2,1)S(1)}, bf16[256,2048]{1,0:T(8,128)(2,1)S(1)}, u32[]{:S(2)}, u32[]{:S(2)}) %collective-permute-start.4) | collective-permute-done | bytes 1048608 | tf_op jit(solution)/shard_map/ppermute | solution.py:493
  104.2 26.8 %collective-permute-done.9 = bf16[256,2048]{1,0:T(8,128)(2,1)S(1)} collective-permute-done((bf16[256,2048]{1,0:T(8,128)(2,1)}, bf16[256,2048]{1,0:T(8,128)(2,1)S(1)}, u32[]{:S(2)}, u32[]{:S(2)}) %collective-permute-start.9) | collective-permute-done | bytes 1048608 | tf_op jit(solution)/shard_map/ppermute | solution.py:569
  168.2 21.5 %attend.1 = (bf16[4,1,2,128,512]{4,3,2,1,0:T(8,128)(2,1)}, f32[4,1,2,128,512]{4,3,2,1,0:T(8,128)}) custom-call(s32[8]{0:T(128)} %fusion.41.order, f32[4,1,2,128,1536]{4,3,2,1,0:T(8,128)} %bitcast.142, f32[1024,128]{1,0:T(8,128)} %get-tuple-element.501.cos, f32[1024,128]{1,0:T(8,128)} %get-tuple-element.502.sin), custom_call_target="tpu_custom_call" | custom-call | flops 1024 | bytes 1024 | tf_op jit(solution)/shard_map/attend/pallas_call | solution.py:153
  199.1 11.8 %collective-permute-done.16 = bf16[128,2048]{1,0:T(8,128)(2,1)S(1)} collective-permute-done((bf16[128,2048]{1,0:T(8,128)(2,1)S(1)}, bf16[128,2048]{1,0:T(8,128)(2,1)S(1)}, u32[]{:S(2)}, u32[]{:S(2)}) %collective-permute-start.16) | collective-permute-done | bytes 524320 | tf_op jit(solution)/shard_map/ppermute | solution.py:490
  217.7 20.2 %collective-permute-done.20 = bf16[256,2048]{1,0:T(8,128)(2,1)S(1)} collective-permute-done((bf16[256,2048]{1,0:T(8,128)(2,1)S(1)}, bf16[256,2048]{1,0:T(8,128)(2,1)S(1)}, u32[]{:S(2)}, u32[]{:S(2)}) %collective-permute-start.20) | collective-permute-done | bytes 1048608 | tf_op jit(solution)/shard_map/ppermute | solution.py:493
  241.0 21.2 %collective-permute-done.22.refs_6_ = bf16[256,4096]{1,0:T(8,128)(2,1)} collective-permute-done((bf16[256,4096]{1,0:T(8,128)(2,1)}, bf16[256,4096]{1,0:T(8,128)(2,1)}, u32[]{:S(2)}, u32[]{:S(2)}) %collective-permute-start.22) | collective-permute-done | bytes 2097184 | tf_op jit(solution)/shard_map/ppermute | solution.py:490
  273.8 12.6 %assemble.6 = bf16[8,256,4096]{2,1,0:T(8,128)(2,1)} custom-call(s32[8]{0:T(128)} %stack.93.places, bf16[256,4096]{1,0:T(8,128)(2,1)} %get-tuple-element.258.refs_0_, bf16[256,4096]{1,0:T(8,128)(2,1)} %copy-done.56, bf16[256,4096]{1,0:T(8,128)(2,1)} %collective-permute-done.14.refs_2_, bf16[256,4096]{1,0:T(8,128)(2,1)} %collective-permute-done.27.refs_3_, ...), custom_call_target="tpu_custom_call" | custom-call | flops 1024 | bytes 1024 | tf_op jit(solution)/shard_map/assemble/pallas_call | solution.py:411
  294.3 21.0 %mlp.2 = (bf16[1024,2048]{1,0:T(8,128)(2,1)}, f32[1024,2048]{1,0:T(8,128)}, f32[1024,2048]{1,0:T(8,128)}, bf16[1024,2048]{1,0:T(8,128)(2,1)}, bf16[256,2048]{1,0...) custom-call(bf16[256,2048]{1,0:T(8,128)(2,1)S(1)} %collective-permute-done.25.refs_0_, ...), custom_call_target="tpu_custom_call" | custom-call | flops 1024 | bytes 1024 | tf_op jit(solution)/shard_map/mlp/pallas_call | solution.py:233
  315.3 11.5 %collective-permute-done.29 = bf16[128,2048]{1,0:T(8,128)(2,1)S(1)} collective-permute-done((bf16[128,2048]{1,0:T(8,128)(2,1)S(1)}, bf16[128,2048]{1,0:T(8,128)(2,1)S(1)}, u32[]{:S(2)}, u32[]{:S(2)}) %collective-permute-start.29) | collective-permute-done | bytes 524320 | tf_op jit(solution)/shard_map/ppermute | solution.py:490
  326.9 21.0 %mlp.3 = (bf16[1024,2048]{1,0:T(8,128)(2,1)}, f32[1024,2048]{1,0:T(8,128)}, f32[1024,2048]{1,0:T(8,128)}, bf16[1024,2048]{1,0:T(8,128)(2,1)}, f32[256,2048]{1,0:T(8,128)S(1)}, /*index=5*/bf16[256,2048]{1,0:T(8,128)(2,1)S(1)}) custom-call(bf16[256,2048]{1,0:T(8,128)(2,1)S(1)} %fusion.11.refs_0_, ...), custom_call_target="tpu_custom_call", output_to_operand_aliasing={{0}: (5, {}), {1}: (6, {}), {2}: (7, {}), {3}: (8, {})} | custom-call | flops 1024 | bytes 1024 | tf_op jit(solution)/shard_map/mlp/pallas_call | solution.py:233
  364.4 21.4 %collective-permute-done.34 = s32[256,1]{0,1:T(1,128)S(1)} collective-permute-done((s32[256,1]{0,1:T(1,128)S(1)}, s32[256,1]{0,1:T(1,128)S(1)}, u32[]{:S(2)}, u32[]{:S(2)}) %collective-permute-start.34) | collective-permute-done | bytes 1056 | tf_op jit(solution)/shard_map/ppermute | solution.py:508
  409.2 13.5 %collective-permute-done.40.refs_0_.refs_1_ = bf16[256,2048]{1,0:T(8,128)(2,1)S(1)} collective-permute-done((bf16[256,2048]{1,0:T(8,128)(2,1)S(1)}, bf16[256,2048]{1,0:T(8,128)(2,1)S(1)}, u32[]{:S(2)}, u32[]{:S(2)}) %collective-permute-start.40) | collective-permute-done | bytes 1048608 | tf_op jit(solution)/shard_map/ppermute | solution.py:493
  428.4 28.6 %mlp_back.2 = (bf16[1024,2048]{1,0:T(8,128)(2,1)}, bf16[1024,2048]{1,0:T(8,128)(2,1)}, bf16[1024,2048]{1,0:T(8,128)(2,1)}, bf16[256,2048]{1,0:T(8,128)(2,1)S(1)}, bf16[256,2048]{1,0:T(8,128)(2,1)S(1)}) custom-call(bf16[256,2048]{1,0:T(8,128)(2,1)S(1)} %collective-permute-done.40.refs_0_.refs_1_, ...), custom_call_target="tpu_custom_call" | custom-call | flops 1024 | bytes 1024 | tf_op jit(solution)/shard_map/mlp_back/pallas_call | solution.py:294
  468.5 28.9 %mlp_back.3 = (bf16[1024,2048]{1,0:T(8,128)(2,1)}, bf16[1024,2048]{1,0:T(8,128)(2,1)}, bf16[1024,2048]{1,0:T(8,128)(2,1)}, f32[256,2048]{1,0:T(8,128)S(1)}, bf16[256,2048]{1,0:T(8,128)(2,1)}) custom-call(bf16[256,2048]{1,0:T(8,128)(2,1)S(1)} %convert_element_type.248.refs_0_.refs_3_, ...), custom_call_target="tpu_custom_call", output_to_operand_aliasing={{0}: (7, {}), {1}: (8, {}), {2}: (9, {})} | custom-call | flops 1024 | bytes 1024 | tf_op jit(solution)/shard_map/mlp_back/pallas_call | solution.py:294
  541.3 19.5 %collective-permute-done.51 = bf16[256,2048]{1,0:T(8,128)(2,1)} collective-permute-done((bf16[256,2048]{1,0:T(8,128)(2,1)}, bf16[256,2048]{1,0:T(8,128)(2,1)}, u32[]{:S(2)}, u32[]{:S(2)}) %collective-permute-start.51) | collective-permute-done | bytes 1048608 | tf_op jit(solution)/shard_map/ppermute | solution.py:508
  632.2 27.6 %attend_back.1 = bf16[4,1,2,128,1536]{4,3,2,1,0:T(8,128)(2,1)} custom-call(s32[8]{0:T(128)} %fusion.41.order, f32[4,1,2,128,1536]{4,3,2,1,0:T(8,128)} %bitcast.143, f32[4,1,2,128,512]{4,3,2,1,0:T(8,128)} %get-tuple-element.353.lse, bf16[4,1,2,128,512]{4,3,2,1,0:T(8,128)(2,1)} %bitcast.123, f32[1024,128]{1,0:T(8,128)} %get-tuple-element.501.cos, ...), custom_call_target="tpu_custom_call" | custom-call | flops 1024 | bytes 1024 | tf_op jit(solution)/shard_map/attend_back/pallas_call | solution.py:177
  694.0 13.3 %collective-permute-done.64 = bf16[1,2,1,2,2,64,512]{6,5,4,3,2,1,0:T(8,128)(2,1)S(1)} collective-permute-done((bf16[1,2,1,2,2,64,512]{6,5,4,3,2,1,0:T(8,128)(2,1)}, bf16[1,2,1,2,2,64,512]{6,5,4,3,2,1,0:T(8,128)(2,1)S(1)}, u32[]{:S(2)}, u32[]{:S(2)}) %collective-permute-start.64) | collective-permute-done | bytes 524320 | tf_op jit(solution)/shard_map/ppermute | solution.py:493
  760.9 27.6 %collective-permute-done.68 = bf16[256,2048]{1,0:T(8,128)(2,1)} collective-permute-done((bf16[256,2048]{1,0:T(8,128)(2,1)}, bf16[256,2048]{1,0:T(8,128)(2,1)}, u32[]{:S(2)}, u32[]{:S(2)}) %collective-permute-start.68) | collective-permute-done | bytes 1048608 | tf_op jit(solution)/shard_map/ppermute | solution.py:493
  813.7 26.8 %collective-permute-done.75 = bf16[64,2048]{1,0:T(8,128)(2,1)S(1)} collective-permute-done((bf16[64,2048]{1,0:T(8,128)(2,1)S(1)}, bf16[64,2048]{1,0:T(8,128)(2,1)S(1)}, u32[]{:S(2)}, u32[]{:S(2)}) %collective-permute-start.75) | collective-permute-done | bytes 262176 | tf_op jit(solution)/shard_map/ppermute | solution.py:493
  842.0 21.0 %collective-permute-done.73 = bf16[256,2048]{1,0:T(8,128)(2,1)S(1)} collective-permute-done((bf16[256,2048]{1,0:T(8,128)(2,1)S(1)}, bf16[256,2048]{1,0:T(8,128)(2,1)S(1)}, u32[]{:S(2)}, u32[]{:S(2)}) %collective-permute-start.73) | collective-permute-done | bytes 1048608 | tf_op jit(solution)/shard_map/ppermute | solution.py:508
  876.1 19.2 %collective-permute-done.82 = bf16[64,2048]{1,0:T(8,128)(2,1)S(1)} collective-permute-done((bf16[64,2048]{1,0:T(8,128)(2,1)S(1)}, bf16[64,2048]{1,0:T(8,128)(2,1)S(1)}, u32[]{:S(2)}, u32[]{:S(2)}) %collective-permute-start.82) | collective-permute-done | bytes 262176 | tf_op jit(solution)/shard_map/ppermute | solution.py:508
  896.1 15.5 %collective-permute-done.81 = bf16[1,2,1,2,2,64,768]{6,5,4,3,2,1,0:T(8,128)(2,1)S(1)} collective-permute-done((bf16[1,2,1,2,2,64,768]{6,5,4,3,2,1,0:T(8,128)(2,1)S(1)}, bf16[1,2,1,2,2,64,768]{6,5,4,3,2,1,0:T(8,128)(2,1)S(1)}, u32[]{:S(2)}, u32[]{:S(2)}) %collective-permute-start.81) | collective-permute-done | bytes 786464 | tf_op jit(solution)/shard_map/ppermute | solution.py:493
  (504 shorter events, 465.3 us)
Async XLA Ops:
  4.0 42.1 %collective-permute-start.1 = (bf16[256,1536]{1,0:T(8,128)(2,1)}, bf16[256,1536]{1,0:T(8,128)(2,1)}, u32[]{:S(2)}, u32[]{:S(2)}) collective-permute-start(bf16[256,1536]{1,0:T(8,128)(2,1)} %pad_maximum_fusion.9), channel_id=1, source_target_pairs={{0,2},{1,3},{2,0},{3,1},{4,6},{5,7},{6,4},{7,5},{8,10},{9,11},{10,... | collective-permute-start | bytes 2359304 | tf_op jit(solution)/shard_map/ppermute | solution.py:490
  5.5 47.1 %collective-permute-start = (bf16[256,2048]{1,0:T(8,128)(2,1)}, bf16[256,2048]{1,0:T(8,128)(2,1)}, u32[]{:S(2)}, u32[]{:S(2)}) collective-permute-start(bf16[256,2048]{1,0:T(8,128)(2,1)} %bitcast.1), channel_id=1, source_target_pairs={{2,16},{3,17},{6,20},{7,21},{10,24},{11,25},{14,28},{15,29},{16,2}... | collective-permute-start | bytes 3145736 | tf_op jit(solution)/shard_map/ppermute | solution.py:508
  14.6 47.3 %collective-permute-start.2 = (bf16[256,4096]{1,0:T(8,128)(2,1)}, bf16[256,4096]{1,0:T(8,128)(2,1)S(1)}, u32[]{:S(2)}, u32[]{:S(2)}) collective-permute-start(bf16[256,4096]{1,0:T(8,128)(2,1)} %get-tuple-element.258.refs_0_), channel_id=1, source_target_pairs={{0,4},{1,5},{2,6},{3,7},{4,0},{5,1},{6,2},{7,3},{8,12},{9,13},{10,... | collective-permute-start | bytes 6291464 | tf_op jit(solution)/shard_map/ppermute | solution.py:490
  73.8 58.5 %collective-permute-start.11 = (bf16[512,1536]{1,0:T(8,128)(2,1)}, bf16[512,1536]{1,0:T(8,128)(2,1)}, u32[]{:S(2)}, u32[]{:S(2)}) collective-permute-start(bf16[512,1536]{1,0:T(8,128)(2,1)} %pad_maximum_fusion.2.refs_0_), channel_id=1, source_target_pairs={{0,4},{1,5},{2,6},{3,7},{4,0},{5,1},{6,2},{7,3},{8,12},{9,13},{10,... | collective-permute-start | bytes 4718600 | tf_op jit(solution)/shard_map/ppermute | solution.py:490
  73.8 57.1 %collective-permute-start.9 = (bf16[256,2048]{1,0:T(8,128)(2,1)}, bf16[256,2048]{1,0:T(8,128)(2,1)S(1)}, u32[]{:S(2)}, u32[]{:S(2)}) collective-permute-start(bf16[256,2048]{1,0:T(8,128)(2,1)} %broadcast_select_fusion.2), channel_id=1, source_target_pairs={{0,4},{1,5},{6,2},{7,3},{8,12},{9,13},{14,10},{15,11},{16,20},{17,... | collective-permute-start | bytes 3145736 | tf_op jit(solution)/shard_map/ppermute | solution.py:569
  139.4 56.6 %collective-permute-start.15 = (bf16[512,2048]{1,0:T(8,128)(2,1)}, bf16[512,2048]{1,0:T(8,128)(2,1)}, u32[]{:S(2)}, u32[]{:S(2)}) collective-permute-start(bf16[512,2048]{1,0:T(8,128)(2,1)} %constant_dynamic-update-slice_fusion.2.refs_0_), channel_id=1, source_target_pairs={{0,4},{1,5},{2,6},{3,7},{4,0},{5,1},{6,2},{7,3},{8,12},{9,13},{10,... | collective-permute-start | bytes 6291464 | tf_op jit(solution)/shard_map/ppermute | solution.py:490
  139.4 56.5 %collective-permute-start.14 = (bf16[256,4096]{1,0:T(8,128)(2,1)}, bf16[256,4096]{1,0:T(8,128)(2,1)}, u32[]{:S(2)}, u32[]{:S(2)}) collective-permute-start(bf16[256,4096]{1,0:T(8,128)(2,1)} %get-tuple-element.245), channel_id=1, source_target_pairs={{0,2},{1,3},{2,0},{3,1},{4,6},{5,7},{6,4},{7,5},{8,10},{9,11},{10,... | collective-permute-start | bytes 6291464 | tf_op jit(solution)/shard_map/ppermute | solution.py:490
  215.3 46.8 %collective-permute-start.22 = (bf16[256,4096]{1,0:T(8,128)(2,1)}, bf16[256,4096]{1,0:T(8,128)(2,1)}, u32[]{:S(2)}, u32[]{:S(2)}) collective-permute-start(bf16[256,4096]{1,0:T(8,128)(2,1)} %collective-permute-done.14.refs_2_), channel_id=1, source_target_pairs={{0,4},{1,5},{2,6},{3,7},{4,0},{5,1},{6,2},{7,3},{8,12},{9,13},{10,... | collective-permute-start | bytes 6291464 | tf_op jit(solution)/shard_map/ppermute | solution.py:490
  217.2 45.0 %collective-permute-start.23 = (bf16[512,2048]{1,0:T(8,128)(2,1)}, bf16[512,2048]{1,0:T(8,128)(2,1)S(1)}, u32[]{:S(2)}, u32[]{:S(2)}) collective-permute-start(bf16[512,2048]{1,0:T(8,128)(2,1)} %collective-permute-done.15.refs_2_), channel_id=1, source_target_pairs={{0,1},{1,0},{2,3},{3,2},{4,5},{5,4},{6,7},{7,6},{8,9},{9,8},{10,11... | collective-permute-start | bytes 6291464 | tf_op jit(solution)/shard_map/ppermute | solution.py:490
  217.2 45.0 %collective-permute-start.24 = (bf16[256,4096]{1,0:T(8,128)(2,1)S(1)}, bf16[256,4096]{1,0:T(8,128)(2,1)S(1)}, u32[]{:S(2)}, u32[]{:S(2)}) collective-permute-start(bf16[256,4096]{1,0:T(8,128)(2,1)S(1)} %copy-done.55), channel_id=1, source_target_pairs={{0,1},{1,0},{2,3},{3,2},{4,5},{5,4},{6,7},{7,6},{8,9},{9,8},{10,11... | collective-permute-start | bytes 6291464 | tf_op jit(solution)/shard_map/ppermute | solution.py:490
  288.7 59.3 %collective-permute-start.33 = (bf16[256,2048]{1,0:T(8,128)(2,1)S(1)}, bf16[256,2048]{1,0:T(8,128)(2,1)S(1)}, u32[]{:S(2)}, u32[]{:S(2)}) collective-permute-start(bf16[256,2048]{1,0:T(8,128)(2,1)S(1)} %bitcast.162), channel_id=1, source_target_pairs={{2,16},{3,17},{6,20},{7,21},{10,24},{11,25},{14,28},{15,29},{16,2}... | collective-permute-start | bytes 3145736 | tf_op jit(solution)/shard_map/ppermute | solution.py:508
  511.2 49.7 %collective-permute-start.51 = (bf16[256,2048]{1,0:T(8,128)(2,1)}, bf16[256,2048]{1,0:T(8,128)(2,1)}, u32[]{:S(2)}, u32[]{:S(2)}) collective-permute-start(bf16[256,2048]{1,0:T(8,128)(2,1)} %convert_element_type.249), channel_id=1, source_target_pairs={{2,16},{3,17},{6,20},{7,21},{10,24},{11,25},{14,28},{15,29},{16,2}... | collective-permute-start | bytes 3145736 | tf_op jit(solution)/shard_map/ppermute | solution.py:508
  519.2 47.1 %collective-permute-start.50 = (bf16[2,1,256,2048]{3,2,1,0:T(8,128)(2,1)}, bf16[2,1,256,2048]{3,2,1,0:T(8,128)(2,1)S(1)}, u32[]{:S(2)}, u32[]{:S(2)}) collective-permute-start(bf16[2,1,256,2048]{3,2,1,0:T(8,128)(2,1)} %constant_dynamic-slice_fusion.11), channel_id=1, source_target_pairs={{0,4},{1,5},{2,6},{3,7},{4,0},{5,1},{6,2},{7,3},{8,12},{9,13},{10,... | collective-permute-start | bytes 6291464 | tf_op jit(solution)/shard_map/ppermute | solution.py:490
  602.1 74.5 %collective-permute-start.58 = (bf16[2,2,1,2,2,64,1024]{6,5,4,3,2,1,0:T(8,128)(2,1)}, bf16[2,2,1,2,2,64,1024]{6,5,4,3,2,1,0:T(8,128)(2,1)}, u32[]{:S(2)}, u32[]{:S(2)}) collective-permute-start(bf16[2,2,1,2,2,64,1024]{6,5,4,3,2,1,0:T(8,128)(2,1)} %constant_dynamic-slice_fusion.10), channel_id=1, source_target_pairs={{0,4},{1,5},{2,6},{3,7},{4,0},{5,1},{6,2},{7,3},{8,12},{9,13},{10,... | collective-permute-start | bytes 6291464 | tf_op jit(solution)/shard_map/ppermute | solution.py:490
  617.6 53.7 %collective-permute-start.60 = (bf16[2,2,1,2,2,64,512]{6,5,4,3,2,1,0:T(8,128)(2,1)}, bf16[2,2,1,2,2,64,512]{6,5,4,3,2,1,0:T(8,128)(2,1)}, u32[]{:S(2)}, u32[]{:S(2)}) collective-permute-start(bf16[2,2,1,2,2,64,512]{6,5,4,3,2,1,0:T(8,128)(2,1)} %constant_dynamic-slice_fusion.8), channel_id=1, source_target_pairs={{0,4},{1,5},{2,6},{3,7},{4,0},{5,1},{6,2},{7,3},{8,12},{9,13},{10,... | collective-permute-start | bytes 3145736 | tf_op jit(solution)/shard_map/ppermute | solution.py:490
  620.4 53.6 %collective-permute-start.59 = (bf16[1,1,256,2048]{3,2,1,0:T(8,128)(2,1)}, bf16[1,1,256,2048]{3,2,1,0:T(8,128)(2,1)}, u32[]{:S(2)}, u32[]{:S(2)}) collective-permute-start(bf16[1,1,256,2048]{3,2,1,0:T(8,128)(2,1)} %constant_dynamic-slice_fusion.9), channel_id=1, source_target_pairs={{0,16},{8,24},{16,0},{24,8},{1,17},{9,25},{17,1},{25,9},{2,18},{10... | collective-permute-start | bytes 3145736 | tf_op jit(solution)/shard_map/ppermute | solution.py:493
  739.9 48.5 %collective-permute-start.68 = (bf16[256,2048]{1,0:T(8,128)(2,1)}, bf16[256,2048]{1,0:T(8,128)(2,1)}, u32[]{:S(2)}, u32[]{:S(2)}) collective-permute-start(bf16[256,2048]{1,0:T(8,128)(2,1)} %pad_maximum_fusion.6), channel_id=1, source_target_pairs={{0,8},{8,0},{16,24},{24,16},{1,9},{9,1},{17,25},{25,17},{2,10},{10... | collective-permute-start | bytes 3145736 | tf_op jit(solution)/shard_map/ppermute | solution.py:493
  744.8 43.6 %collective-permute-start.69 = (bf16[256,2048]{1,0:T(8,128)(2,1)}, bf16[256,2048]{1,0:T(8,128)(2,1)}, u32[]{:S(2)}, u32[]{:S(2)}) collective-permute-start(bf16[256,2048]{1,0:T(8,128)(2,1)} %pad_maximum_fusion.7), channel_id=1, source_target_pairs={{0,2},{1,3},{2,0},{3,1},{4,6},{5,7},{6,4},{7,5},{8,10},{9,11},{10,... | collective-permute-start | bytes 3145736 | tf_op jit(solution)/shard_map/ppermute | solution.py:490
  795.6 45.0 %collective-permute-start.76 = (bf16[2,2,64,1024]{3,2,1,0:T(8,128)(2,1)S(1)}, bf16[2,2,64,1024]{3,2,1,0:T(8,128)(2,1)S(1)}, u32[]{:S(2)}, u32[]{:S(2)}) collective-permute-start(bf16[2,2,64,1024]{3,2,1,0:T(8,128)(2,1)S(1)} %dynamic-slice_bitcast_fusion.1), channel_id=1, source_target_pairs={{0,1},{1,0},{2,3},{3,2},{4,5},{5,4},{6,7},{7,6},{8,9},{9,8},{10,11... | collective-permute-start | bytes 1572872 | tf_op jit(solution)/shard_map/ppermute | solution.py:490
  808.4 55.3 %collective-permute-start.74 = (bf16[2,2,1,2,2,64,768]{6,5,4,3,2,1,0:T(8,128)(2,1)S(1)}, bf16[2,2,1,2,2,64,768]{6,5,4,3,2,1,0:T(8,128)(2,1)S(1)}, u32[]{:S(2)}, u32[]{:S(2)}) collective-permute-start(bf16[2,2,1,2,2,64,768]{6,5,4,3,2,1,0:T(8,128)(2,1)S(1)} %constant_dynamic-slice_fusion.2), channel_id=1, source_target_pairs={{0,4},{1,5},{2,6},{3,7},{4,0},{5,1},{6,2},{7,3},{8,12},{9,13},{10,... | collective-permute-start | bytes 4718600 | tf_op jit(solution)/shard_map/ppermute | solution.py:490
  809.6 53.4 %collective-permute-start.73 = (bf16[256,2048]{1,0:T(8,128)(2,1)S(1)}, bf16[256,2048]{1,0:T(8,128)(2,1)S(1)}, u32[]{:S(2)}, u32[]{:S(2)}) collective-permute-start(bf16[256,2048]{1,0:T(8,128)(2,1)S(1)} %fusion.9), channel_id=1, source_target_pairs={{2,16},{3,17},{6,20},{7,21},{10,24},{11,25},{14,28},{15,29},{16,2}... | collective-permute-start | bytes 3145736 | tf_op jit(solution)/shard_map/ppermute | solution.py:508
  866.2 45.3 %collective-permute-start.81 = (bf16[1,2,1,2,2,64,768]{6,5,4,3,2,1,0:T(8,128)(2,1)S(1)}, bf16[1,2,1,2,2,64,768]{6,5,4,3,2,1,0:T(8,128)(2,1)S(1)}, u32[]{:S(2)}, u32[]{:S(2)}) collective-permute-start(bf16[1,2,1,2,2,64,768]{6,5,4,3,2,1,0:T(8,128)(2,1)S(1)} %constant_dynamic-slice_fusion), channel_id=1, source_target_pairs={{0,16},{8,24},{16,0},{24,8},{1,17},{9,25},{17,1},{25,9},{2,18},{10... | collective-permute-start | bytes 2359304 | tf_op jit(solution)/shard_map/ppermute | solution.py:493
  866.3 45.5 %collective-permute-start.78 = (bf16[64,4096]{1,0:T(8,128)(2,1)S(1)}, bf16[64,4096]{1,0:T(8,128)(2,1)S(1)}, u32[]{:S(2)}, u32[]{:S(2)}) collective-permute-start(bf16[64,4096]{1,0:T(8,128)(2,1)S(1)} %pad_maximum_fusion.13), channel_id=1, source_target_pairs={{0,8},{8,0},{16,24},{24,16},{1,9},{9,1},{17,25},{25,17},{2,10},{10... | collective-permute-start | bytes 1572872 | tf_op jit(solution)/shard_map/ppermute | solution.py:493
  870.3 41.5 %collective-permute-start.79 = (bf16[64,4096]{1,0:T(8,128)(2,1)S(1)}, bf16[64,4096]{1,0:T(8,128)(2,1)S(1)}, u32[]{:S(2)}, u32[]{:S(2)}) collective-permute-start(bf16[64,4096]{1,0:T(8,128)(2,1)S(1)} %pad_maximum_fusion.14), channel_id=1, source_target_pairs={{0,2},{1,3},{2,0},{3,1},{4,6},{5,7},{6,4},{7,5},{8,10},{9,11},{10,... | collective-permute-start | bytes 1572872 | tf_op jit(solution)/shard_map/ppermute | solution.py:490
  (150 other events, 2546.8 us)

commit v4 on v3

--- a/solution.py
+++ b/solution.py
@@ -190,7 +190,7 @@
     )(order, qkv, lse, grad, cos, sin)
 
 
-TILE = 256
+TILE = 512
 
 
 def up_kernel(count, *refs):
@@ -224,10 +224,12 @@
 def mlp(hs, gu_w, down_w, types, parts, which, held=None):
     rows, width = hs[0].shape
     part_ff = down_w.shape[0]
-    count, tiles = len(hs), part_ff // TILE
+    count = len(hs)
     span = rows * count
+    depth = TILE if span <= TILE else TILE // 2
+    tiles = part_ff // depth
     whole = pl.BlockSpec((rows, width), lambda i: (0, 0))
-    tile = pl.BlockSpec((span, TILE), lambda i: (which, i))
+    tile = pl.BlockSpec((span, depth), lambda i: (which, i))
     kept = [(width, BF), (part_ff, F32), (part_ff, F32), (part_ff, BF)]
     extra = [] if held is None else list(held)
     result = pl.pallas_call(
@@ -235,9 +237,9 @@
         grid=(tiles,),
         in_specs=[whole] * count
         + [
-            pl.BlockSpec((width, TILE), lambda i: (0, i)),
-            pl.BlockSpec((width, TILE), lambda i: (0, tiles + i)),
-            pl.BlockSpec((TILE, width), lambda i: (i, 0)),
+            pl.BlockSpec((width, depth), lambda i: (0, i)),
+            pl.BlockSpec((width, depth), lambda i: (0, tiles + i)),
+            pl.BlockSpec((depth, width), lambda i: (i, 0)),
         ]
         + [pl.BlockSpec(memory_space=pl.ANY)] * len(extra),
         out_specs=[pl.BlockSpec((span, width), lambda i: (which, 0)), tile, tile, tile] + [whole] * count,
@@ -285,10 +287,12 @@
 def mlp_back(ds, g, u, gu_w, down_w, types, parts, which, held=None):
     rows, width = ds[0].shape
     part_ff = down_w.shape[0]
-    count, tiles = len(ds), part_ff // TILE
+    count = len(ds)
     span = rows * count
+    depth = TILE if span <= TILE else TILE // 2
+    tiles = part_ff // depth
     whole = pl.BlockSpec((rows, width), lambda i: (0, 0))
-    tile = pl.BlockSpec((span, TILE), lambda i: (which, i))
+    tile = pl.BlockSpec((span, depth), lambda i: (which, i))
     kept = [(width, BF), (part_ff, BF), (part_ff, BF)]
     extra = [] if held is None else list(held)
     result = pl.pallas_call(
@@ -298,9 +302,9 @@
         + [
             tile,
             tile,
-            pl.BlockSpec((width, TILE), lambda i: (0, i)),
-            pl.BlockSpec((width, TILE), lambda i: (0, tiles + i)),
-            pl.BlockSpec((TILE, width), lambda i: (i, 0)),
+            pl.BlockSpec((width, depth), lambda i: (0, i)),
+            pl.BlockSpec((width, depth), lambda i: (0, tiles + i)),
+            pl.BlockSpec((depth, width), lambda i: (i, 0)),
         ]
         + [pl.BlockSpec(memory_space=pl.ANY)] * len(extra),
         out_specs=[pl.BlockSpec((span, width), lambda i: (which, 0)), tile, tile] + [whole] * count,
@@ -653,14 +657,16 @@
     )
 
     received = reduce_far(products)
-    gu_other_y = over_y(gu_other)
+    gate_other_y = over_y(gu_other[:, :part_ff])
     down_pair = flip(down_both, 1)
     gu_own_pair = flip(gu_own, 1)
-    received, products, down_pair, gu_other, down_y, gu_own_pair, gu_own_y = region(
-        received, products, down_pair, gu_other, down_y, gu_own_pair, gu_own_y
+    received, products, down_pair, gu_other, gate_other_y, down_y, gu_own_pair, gu_own_y = region(
+        received, products, down_pair, gu_other, gate_other_y, down_y, gu_own_pair, gu_own_y
     )
 
     own, received = reduce_near(products, received)
+    up_other_y = over_y(gu_other[:, part_ff:])
+    gu_other_y = [jnp.concatenate(v, 1) for v in zip(gate_other_y, up_other_y)]
     down_y_pair = [flip(v, 1) for v in down_y]
     gu_own_y_pair = [flip(v, 1) for v in gu_own_y]
     residual = stream + add_all(own, received)

time: 965 us -> 944 us (0.978)
  Pallas kernels: 292 us -> 266 us
    pallas_call x2, Pallas kernels: 57.5 us -> 43.3 us  [mlp_back(): pl.pallas_call(functools.partial(down_kernel, count), grid=(tiles,), in_s...]
    pallas_call x10, Pallas kernels: 76.1 us -> 66.2 us  [outer(): pl.pallas_call(kernel, grid_spec=pltpu.PrefetchScalarGridSpec(num_scalar_...]
    ppermute x49 -> x50, waiting for transfers between devices: 117 us -> 111 us  [flip(): return lax.ppermute(array, 'fsdp', [(i, i ^ bits) for i in range(shards)])]
    ppermute x49 -> x50, starting transfers between devices: 40.4 us -> 43.1 us  [flip(): return lax.ppermute(array, 'fsdp', [(i, i ^ bits) for i in range(shards)])]
  transfers between devices with their start and end apart: 87 -> 88, of which waited for: 45 -> 48; matrix products, arithmetic and copies ran while one was open for 9% -> 9% of each run, Pallas kernels for 29% -> 27%
where the time goes in v4:
time: 944 us; the launch traced here: 939 us
  waiting for transfers between devices  388 us (41%)
  Pallas kernels  266 us (28%)
  starting transfers between devices  134 us (14%)
  other arithmetic  75.6 us (8%)
  local copies, waits for them, and re-layouts  70.2 us (7%)
    ppermute x24, waiting for transfers between devices, flip_ctx(): return lax.ppermute(array, 'ctx', [(i, i ^ bits) for i in range(planes)])  157 us
    ppermute x50, waiting for transfers between devices, flip(): return lax.ppermute(array, 'fsdp', [(i, i ^ bits) for i in range(shards)])  111 us
    ppermute x7, waiting for transfers between devices, send(): lax.ppermute(array, both, [(i, to) for i, to in enumerate(homes) if i !=...  88.4 us
    pallas_call x10, Pallas kernels, outer(): pl.pallas_call(kernel, grid_spec=pltpu.PrefetchScalarGridSpec(num_scalar_...  66.2 us
    ppermute x24, starting transfers between devices, flip_ctx(): return lax.ppermute(array, 'ctx', [(i, i ^ bits) for i in range(planes)])  50.7 us
    pallas_call x2, Pallas kernels, mlp_back(): pl.pallas_call(functools.partial(down_kernel, count), grid=(tiles,), in_s...  43.3 us
    ppermute x50, starting transfers between devices, flip(): return lax.ppermute(array, 'fsdp', [(i, i ^ bits) for i in range(shards)])  43.1 us
    pallas_call x2, Pallas kernels, mlp(): pl.pallas_call(functools.partial(up_kernel, count), grid=(tiles,), in_spe...  40.5 us
  transfers between devices with their start and end apart: 88, of which 48 were waited for; matrix products, arithmetic and copies ran while one was open for 9% of the time, Pallas kernels for 27%

profile of v4, /device:TPU:16, one launch (start us, length us, event | category | flops | bytes accessed | tf_op | source)
XLA Modules:
  0.0 939.2 jit_solution(7590564302240398869)
XLA Ops:
  18.7 27.4 %collective-permute-done.1 = bf16[256,1536]{1,0:T(8,128)(2,1)} collective-permute-done((bf16[256,1536]{1,0:T(8,128)(2,1)}, bf16[256,1536]{1,0:T(8,128)(2,1)}, u32[]{:S(2)}, u32[]{:S(2)}) %collective-permute-start.1) | collective-permute-done | bytes 786464 | tf_op jit(solution)/shard_map/ppermute | solution.py:494
  63.3 10.6 %collective-permute-start.4 = (bf16[256,2048]{1,0:T(8,128)(2,1)S(1)}, bf16[256,2048]{1,0:T(8,128)(2,1)S(1)}, u32[]{:S(2)}, u32[]{:S(2)}) collective-permute-start(bf16[256,2048]{1,0:T(8,128)(2,1)S(1)} %fusion.4.refs_0_), channel_id=1, source_target_pairs={{0,8},{8,0},{16,24},{24,16},{1,9},{9,1},{17,25},{25,17},{2,10},{10... | collective-permute-start | bytes 3145736 | tf_op jit(solution)/shard_map/ppermute | solution.py:497
  78.0 19.7 %collective-permute-done.4.refs_1_ = bf16[256,2048]{1,0:T(8,128)(2,1)S(1)} collective-permute-done((bf16[256,2048]{1,0:T(8,128)(2,1)S(1)}, bf16[256,2048]{1,0:T(8,128)(2,1)S(1)}, u32[]{:S(2)}, u32[]{:S(2)}) %collective-permute-start.4) | collective-permute-done | bytes 1048608 | tf_op jit(solution)/shard_map/ppermute | solution.py:497
  104.2 26.8 %collective-permute-done.9 = bf16[256,2048]{1,0:T(8,128)(2,1)S(1)} collective-permute-done((bf16[256,2048]{1,0:T(8,128)(2,1)}, bf16[256,2048]{1,0:T(8,128)(2,1)S(1)}, u32[]{:S(2)}, u32[]{:S(2)}) %collective-permute-start.9) | collective-permute-done | bytes 1048608 | tf_op jit(solution)/shard_map/ppermute | solution.py:573
  158.0 9.9 %project.4 = f32[1024,1536]{1,0:T(8,128)} custom-call(bf16[256,2048]{1,0:T(8,128)(2,1)S(1)} %fusion.4.refs_0_, bf16[256,2048]{1,0:T(8,128)(2,1)S(1)} %collective-permute-done.4.refs_1_, bf16[256,2048]{1,0:T(8,128)(2,1)S(1)} %collective-permute-done.5.refs_2_, bf16[256,2048]{1,0:T(8,128)(2,1)S(1)} %constant_dynamic-update-slice_fusion.refs_3_, ...), custom_call_target="tpu_custom_call" | custom-call | flops 1024 | bytes 1024 | tf_op jit(solution)/shard_map/project/pallas_call | solution.py:378
  167.9 21.5 %attend.1 = (bf16[4,1,2,128,512]{4,3,2,1,0:T(8,128)(2,1)}, f32[4,1,2,128,512]{4,3,2,1,0:T(8,128)}) custom-call(s32[8]{0:T(128)} %fusion.41.order, f32[4,1,2,128,1536]{4,3,2,1,0:T(8,128)} %bitcast.142, f32[1024,128]{1,0:T(8,128)} %get-tuple-element.503.cos, f32[1024,128]{1,0:T(8,128)} %get-tuple-element.504.sin), custom_call_target="tpu_custom_call" | custom-call | flops 1024 | bytes 1024 | tf_op jit(solution)/shard_map/attend/pallas_call | solution.py:153
  202.1 11.4 %collective-permute-done.16 = bf16[128,2048]{1,0:T(8,128)(2,1)S(1)} collective-permute-done((bf16[128,2048]{1,0:T(8,128)(2,1)S(1)}, bf16[128,2048]{1,0:T(8,128)(2,1)S(1)}, u32[]{:S(2)}, u32[]{:S(2)}) %collective-permute-start.16) | collective-permute-done | bytes 524320 | tf_op jit(solution)/shard_map/ppermute | solution.py:494
  231.3 18.3 %collective-permute-done.21 = bf16[256,2048]{1,0:T(8,128)(2,1)S(1)} collective-permute-done((bf16[256,2048]{1,0:T(8,128)(2,1)S(1)}, bf16[256,2048]{1,0:T(8,128)(2,1)S(1)}, u32[]{:S(2)}, u32[]{:S(2)}) %collective-permute-start.21) | collective-permute-done | bytes 1048608 | tf_op jit(solution)/shard_map/ppermute | solution.py:497
  268.1 12.6 %assemble.6 = bf16[8,256,4096]{2,1,0:T(8,128)(2,1)} custom-call(s32[8]{0:T(128)} %stack.93.places, bf16[256,4096]{1,0:T(8,128)(2,1)} %get-tuple-element.259.refs_0_, bf16[256,4096]{1,0:T(8,128)(2,1)} %copy-done.56, bf16[256,4096]{1,0:T(8,128)(2,1)} %collective-permute-done.14.refs_2_, bf16[256,4096]{1,0:T(8,128)(2,1)} %collective-permute-done.28.refs_3_, ...), custom_call_target="tpu_custom_call" | custom-call | flops 1024 | bytes 1024 | tf_op jit(solution)/shard_map/assemble/pallas_call | solution.py:415
  288.4 20.2 %mlp.2 = (bf16[1024,2048]{1,0:T(8,128)(2,1)}, f32[1024,2048]{1,0:T(8,128)}, f32[1024,2048]{1,0:T(8,128)}, bf16[1024,2048]{1,0:T(8,128)(2,1)}, bf16[256,2048]{1,0...) custom-call(bf16[256,2048]{1,0:T(8,128)(2,1)S(1)} %collective-permute-done.26.refs_0_, ...), custom_call_target="tpu_custom_call" | custom-call | flops 1024 | bytes 1024 | tf_op jit(solution)/shard_map/mlp/pallas_call | solution.py:235
  308.6 12.6 %collective-permute-done.30 = bf16[128,2048]{1,0:T(8,128)(2,1)S(1)} collective-permute-done((bf16[128,2048]{1,0:T(8,128)(2,1)S(1)}, bf16[128,2048]{1,0:T(8,128)(2,1)S(1)}, u32[]{:S(2)}, u32[]{:S(2)}) %collective-permute-start.30) | collective-permute-done | bytes 524320 | tf_op jit(solution)/shard_map/ppermute | solution.py:494
  321.3 20.3 %mlp.3 = (bf16[1024,2048]{1,0:T(8,128)(2,1)}, f32[1024,2048]{1,0:T(8,128)}, f32[1024,2048]{1,0:T(8,128)}, bf16[1024,2048]{1,0:T(8,128)(2,1)}, f32[256,2048]{1,0:T(8,128)S(1)}, /*index=5*/bf16[256,2048]{1,0:T(8,128)(2,1)S(1)}) custom-call(bf16[256,2048]{1,0:T(8,128)(2,1)S(1)} %fusion.11.refs_0_, ...), custom_call_target="tpu_custom_call", output_to_operand_aliasing={{0}: (5, {}), {1}: (6, {}), {2}: (7, {}), {3}: (8, {})} | custom-call | flops 1024 | bytes 1024 | tf_op jit(solution)/shard_map/mlp/pallas_call | solution.py:235
  358.7 21.4 %collective-permute-done.35 = s32[256,1]{0,1:T(1,128)S(1)} collective-permute-done((s32[256,1]{0,1:T(1,128)S(1)}, s32[256,1]{0,1:T(1,128)S(1)}, u32[]{:S(2)}, u32[]{:S(2)}) %collective-permute-start.35) | collective-permute-done | bytes 1056 | tf_op jit(solution)/shard_map/ppermute | solution.py:512
  403.6 13.5 %collective-permute-done.41.refs_0_.refs_1_ = bf16[256,2048]{1,0:T(8,128)(2,1)S(1)} collective-permute-done((bf16[256,2048]{1,0:T(8,128)(2,1)S(1)}, bf16[256,2048]{1,0:T(8,128)(2,1)S(1)}, u32[]{:S(2)}, u32[]{:S(2)}) %collective-permute-start.41) | collective-permute-done | bytes 1048608 | tf_op jit(solution)/shard_map/ppermute | solution.py:497
  422.9 21.7 %mlp_back.2 = (bf16[1024,2048]{1,0:T(8,128)(2,1)}, bf16[1024,2048]{1,0:T(8,128)(2,1)}, bf16[1024,2048]{1,0:T(8,128)(2,1)}, bf16[256,2048]{1,0:T(8,128)(2,1)S(1)}, bf16[256,2048]{1,0:T(8,128)(2,1)S(1)}) custom-call(bf16[256,2048]{1,0:T(8,128)(2,1)S(1)} %collective-permute-done.41.refs_0_.refs_1_, ...), custom_call_target="tpu_custom_call" | custom-call | flops 1024 | bytes 1024 | tf_op jit(solution)/shard_map/mlp_back/pallas_call | solution.py:298
  456.0 21.6 %mlp_back.3 = (bf16[1024,2048]{1,0:T(8,128)(2,1)}, bf16[1024,2048]{1,0:T(8,128)(2,1)}, bf16[1024,2048]{1,0:T(8,128)(2,1)}, f32[256,2048]{1,0:T(8,128)S(1)}, bf16[256,2048]{1,0:T(8,128)(2,1)}) custom-call(bf16[256,2048]{1,0:T(8,128)(2,1)S(1)} %convert_element_type.248.refs_0_.refs_3_, ...), custom_call_target="tpu_custom_call", output_to_operand_aliasing={{0}: (7, {}), {1}: (8, {}), {2}: (9, {})} | custom-call | flops 1024 | bytes 1024 | tf_op jit(solution)/shard_map/mlp_back/pallas_call | solution.py:298
  518.8 22.2 %collective-permute-done.52 = bf16[256,2048]{1,0:T(8,128)(2,1)} collective-permute-done((bf16[256,2048]{1,0:T(8,128)(2,1)}, bf16[256,2048]{1,0:T(8,128)(2,1)}, u32[]{:S(2)}, u32[]{:S(2)}) %collective-permute-start.52) | collective-permute-done | bytes 1048608 | tf_op jit(solution)/shard_map/ppermute | solution.py:512
  612.1 27.9 %attend_back.1 = bf16[4,1,2,128,1536]{4,3,2,1,0:T(8,128)(2,1)} custom-call(s32[8]{0:T(128)} %fusion.41.order, f32[4,1,2,128,1536]{4,3,2,1,0:T(8,128)} %bitcast.143, f32[4,1,2,128,512]{4,3,2,1,0:T(8,128)} %get-tuple-element.355.lse, bf16[4,1,2,128,512]{4,3,2,1,0:T(8,128)(2,1)} %bitcast.123, f32[1024,128]{1,0:T(8,128)} %get-tuple-element.503.cos, ...), custom_call_target="tpu_custom_call" | custom-call | flops 1024 | bytes 1024 | tf_op jit(solution)/shard_map/attend_back/pallas_call | solution.py:177
  674.1 13.3 %collective-permute-done.65 = bf16[1,2,1,2,2,64,512]{6,5,4,3,2,1,0:T(8,128)(2,1)S(1)} collective-permute-done((bf16[1,2,1,2,2,64,512]{6,5,4,3,2,1,0:T(8,128)(2,1)}, bf16[1,2,1,2,2,64,512]{6,5,4,3,2,1,0:T(8,128)(2,1)S(1)}, u32[]{:S(2)}, u32[]{:S(2)}) %collective-permute-start.65) | collective-permute-done | bytes 524320 | tf_op jit(solution)/shard_map/ppermute | solution.py:497
  741.0 27.8 %collective-permute-done.69 = bf16[256,2048]{1,0:T(8,128)(2,1)} collective-permute-done((bf16[256,2048]{1,0:T(8,128)(2,1)}, bf16[256,2048]{1,0:T(8,128)(2,1)}, u32[]{:S(2)}, u32[]{:S(2)}) %collective-permute-start.69) | collective-permute-done | bytes 1048608 | tf_op jit(solution)/shard_map/ppermute | solution.py:497
  793.4 27.4 %collective-permute-done.76 = bf16[64,2048]{1,0:T(8,128)(2,1)S(1)} collective-permute-done((bf16[64,2048]{1,0:T(8,128)(2,1)S(1)}, bf16[64,2048]{1,0:T(8,128)(2,1)S(1)}, u32[]{:S(2)}, u32[]{:S(2)}) %collective-permute-start.76) | collective-permute-done | bytes 262176 | tf_op jit(solution)/shard_map/ppermute | solution.py:497
  822.2 21.0 %collective-permute-done.74 = bf16[256,2048]{1,0:T(8,128)(2,1)S(1)} collective-permute-done((bf16[256,2048]{1,0:T(8,128)(2,1)S(1)}, bf16[256,2048]{1,0:T(8,128)(2,1)S(1)}, u32[]{:S(2)}, u32[]{:S(2)}) %collective-permute-start.74) | collective-permute-done | bytes 1048608 | tf_op jit(solution)/shard_map/ppermute | solution.py:512
  856.1 19.5 %collective-permute-done.83 = bf16[64,2048]{1,0:T(8,128)(2,1)S(1)} collective-permute-done((bf16[64,2048]{1,0:T(8,128)(2,1)S(1)}, bf16[64,2048]{1,0:T(8,128)(2,1)S(1)}, u32[]{:S(2)}, u32[]{:S(2)}) %collective-permute-start.83) | collective-permute-done | bytes 262176 | tf_op jit(solution)/shard_map/ppermute | solution.py:512
  876.2 15.6 %collective-permute-done.82 = bf16[1,2,1,2,2,64,768]{6,5,4,3,2,1,0:T(8,128)(2,1)S(1)} collective-permute-done((bf16[1,2,1,2,2,64,768]{6,5,4,3,2,1,0:T(8,128)(2,1)S(1)}, bf16[1,2,1,2,2,64,768]{6,5,4,3,2,1,0:T(8,128)(2,1)S(1)}, u32[]{:S(2)}, u32[]{:S(2)}) %collective-permute-start.82) | collective-permute-done | bytes 786464 | tf_op jit(solution)/shard_map/ppermute | solution.py:497
  (509 shorter events, 469.4 us)
Async XLA Ops:
  4.0 42.1 %collective-permute-start.1 = (bf16[256,1536]{1,0:T(8,128)(2,1)}, bf16[256,1536]{1,0:T(8,128)(2,1)}, u32[]{:S(2)}, u32[]{:S(2)}) collective-permute-start(bf16[256,1536]{1,0:T(8,128)(2,1)} %pad_maximum_fusion.10), channel_id=1, source_target_pairs={{0,2},{1,3},{2,0},{3,1},{4,6},{5,7},{6,4},{7,5},{8,10},{9,11},{10,... | collective-permute-start | bytes 2359304 | tf_op jit(solution)/shard_map/ppermute | solution.py:494
  5.5 47.1 %collective-permute-start = (bf16[256,2048]{1,0:T(8,128)(2,1)}, bf16[256,2048]{1,0:T(8,128)(2,1)}, u32[]{:S(2)}, u32[]{:S(2)}) collective-permute-start(bf16[256,2048]{1,0:T(8,128)(2,1)} %bitcast.1), channel_id=1, source_target_pairs={{2,16},{3,17},{6,20},{7,21},{10,24},{11,25},{14,28},{15,29},{16,2}... | collective-permute-start | bytes 3145736 | tf_op jit(solution)/shard_map/ppermute | solution.py:512
  14.6 47.3 %collective-permute-start.2 = (bf16[256,4096]{1,0:T(8,128)(2,1)}, bf16[256,4096]{1,0:T(8,128)(2,1)S(1)}, u32[]{:S(2)}, u32[]{:S(2)}) collective-permute-start(bf16[256,4096]{1,0:T(8,128)(2,1)} %get-tuple-element.259.refs_0_), channel_id=1, source_target_pairs={{0,4},{1,5},{2,6},{3,7},{4,0},{5,1},{6,2},{7,3},{8,12},{9,13},{10,... | collective-permute-start | bytes 6291464 | tf_op jit(solution)/shard_map/ppermute | solution.py:494
  16.4 40.2 %collective-permute-start.3 = (bf16[256,2048]{1,0:T(8,128)(2,1)}, bf16[256,2048]{1,0:T(8,128)(2,1)}, u32[]{:S(2)}, u32[]{:S(2)}) collective-permute-start(bf16[256,2048]{1,0:T(8,128)(2,1)} %param.25), channel_id=1, source_target_pairs={{4,6},{5,7},{10,8},{11,9},{20,22},{21,23},{26,24},{27,25}} | collective-permute-start | bytes 3145736 | tf_op jit(solution)/shard_map/ppermute | solution.py:568
  73.9 58.5 %collective-permute-start.11 = (bf16[512,1536]{1,0:T(8,128)(2,1)}, bf16[512,1536]{1,0:T(8,128)(2,1)}, u32[]{:S(2)}, u32[]{:S(2)}) collective-permute-start(bf16[512,1536]{1,0:T(8,128)(2,1)} %pad_maximum_fusion.3.refs_0_), channel_id=1, source_target_pairs={{0,4},{1,5},{2,6},{3,7},{4,0},{5,1},{6,2},{7,3},{8,12},{9,13},{10,... | collective-permute-start | bytes 4718600 | tf_op jit(solution)/shard_map/ppermute | solution.py:494
  73.9 57.1 %collective-permute-start.9 = (bf16[256,2048]{1,0:T(8,128)(2,1)}, bf16[256,2048]{1,0:T(8,128)(2,1)S(1)}, u32[]{:S(2)}, u32[]{:S(2)}) collective-permute-start(bf16[256,2048]{1,0:T(8,128)(2,1)} %broadcast_select_fusion.2), channel_id=1, source_target_pairs={{0,4},{1,5},{6,2},{7,3},{8,12},{9,13},{14,10},{15,11},{16,20},{17,... | collective-permute-start | bytes 3145736 | tf_op jit(solution)/shard_map/ppermute | solution.py:573
  139.4 56.3 %collective-permute-start.15 = (bf16[512,2048]{1,0:T(8,128)(2,1)}, bf16[512,2048]{1,0:T(8,128)(2,1)}, u32[]{:S(2)}, u32[]{:S(2)}) collective-permute-start(bf16[512,2048]{1,0:T(8,128)(2,1)} %constant_dynamic-update-slice_fusion.2.refs_0_), channel_id=1, source_target_pairs={{0,4},{1,5},{2,6},{3,7},{4,0},{5,1},{6,2},{7,3},{8,12},{9,13},{10,... | collective-permute-start | bytes 6291464 | tf_op jit(solution)/shard_map/ppermute | solution.py:494
  139.5 56.2 %collective-permute-start.14 = (bf16[256,4096]{1,0:T(8,128)(2,1)}, bf16[256,4096]{1,0:T(8,128)(2,1)}, u32[]{:S(2)}, u32[]{:S(2)}) collective-permute-start(bf16[256,4096]{1,0:T(8,128)(2,1)} %get-tuple-element.246), channel_id=1, source_target_pairs={{0,2},{1,3},{2,0},{3,1},{4,6},{5,7},{6,4},{7,5},{8,10},{9,11},{10,... | collective-permute-start | bytes 6291464 | tf_op jit(solution)/shard_map/ppermute | solution.py:494
  283.0 58.6 %collective-permute-start.34 = (bf16[256,2048]{1,0:T(8,128)(2,1)S(1)}, bf16[256,2048]{1,0:T(8,128)(2,1)S(1)}, u32[]{:S(2)}, u32[]{:S(2)}) collective-permute-start(bf16[256,2048]{1,0:T(8,128)(2,1)S(1)} %bitcast.162), channel_id=1, source_target_pairs={{2,16},{3,17},{6,20},{7,21},{10,24},{11,25},{14,28},{15,29},{16,2}... | collective-permute-start | bytes 3145736 | tf_op jit(solution)/shard_map/ppermute | solution.py:512
  491.4 49.6 %collective-permute-start.52 = (bf16[256,2048]{1,0:T(8,128)(2,1)}, bf16[256,2048]{1,0:T(8,128)(2,1)}, u32[]{:S(2)}, u32[]{:S(2)}) collective-permute-start(bf16[256,2048]{1,0:T(8,128)(2,1)} %convert_element_type.249), channel_id=1, source_target_pairs={{2,16},{3,17},{6,20},{7,21},{10,24},{11,25},{14,28},{15,29},{16,2}... | collective-permute-start | bytes 3145736 | tf_op jit(solution)/shard_map/ppermute | solution.py:512
  499.3 47.1 %collective-permute-start.51 = (bf16[2,1,256,2048]{3,2,1,0:T(8,128)(2,1)}, bf16[2,1,256,2048]{3,2,1,0:T(8,128)(2,1)S(1)}, u32[]{:S(2)}, u32[]{:S(2)}) collective-permute-start(bf16[2,1,256,2048]{3,2,1,0:T(8,128)(2,1)} %constant_dynamic-slice_fusion.11), channel_id=1, source_target_pairs={{0,4},{1,5},{2,6},{3,7},{4,0},{5,1},{6,2},{7,3},{8,12},{9,13},{10,... | collective-permute-start | bytes 6291464 | tf_op jit(solution)/shard_map/ppermute | solution.py:494
  582.1 74.5 %collective-permute-start.59 = (bf16[2,2,1,2,2,64,1024]{6,5,4,3,2,1,0:T(8,128)(2,1)}, bf16[2,2,1,2,2,64,1024]{6,5,4,3,2,1,0:T(8,128)(2,1)}, u32[]{:S(2)}, u32[]{:S(2)}) collective-permute-start(bf16[2,2,1,2,2,64,1024]{6,5,4,3,2,1,0:T(8,128)(2,1)} %constant_dynamic-slice_fusion.10), channel_id=1, source_target_pairs={{0,4},{1,5},{2,6},{3,7},{4,0},{5,1},{6,2},{7,3},{8,12},{9,13},{10,... | collective-permute-start | bytes 6291464 | tf_op jit(solution)/shard_map/ppermute | solution.py:494
  597.6 53.7 %collective-permute-start.61 = (bf16[2,2,1,2,2,64,512]{6,5,4,3,2,1,0:T(8,128)(2,1)}, bf16[2,2,1,2,2,64,512]{6,5,4,3,2,1,0:T(8,128)(2,1)}, u32[]{:S(2)}, u32[]{:S(2)}) collective-permute-start(bf16[2,2,1,2,2,64,512]{6,5,4,3,2,1,0:T(8,128)(2,1)} %constant_dynamic-slice_fusion.8), channel_id=1, source_target_pairs={{0,4},{1,5},{2,6},{3,7},{4,0},{5,1},{6,2},{7,3},{8,12},{9,13},{10,... | collective-permute-start | bytes 3145736 | tf_op jit(solution)/shard_map/ppermute | solution.py:494
  600.4 53.6 %collective-permute-start.60 = (bf16[1,1,256,2048]{3,2,1,0:T(8,128)(2,1)}, bf16[1,1,256,2048]{3,2,1,0:T(8,128)(2,1)}, u32[]{:S(2)}, u32[]{:S(2)}) collective-permute-start(bf16[1,1,256,2048]{3,2,1,0:T(8,128)(2,1)} %constant_dynamic-slice_fusion.9), channel_id=1, source_target_pairs={{0,16},{8,24},{16,0},{24,8},{1,17},{9,25},{17,1},{25,9},{2,18},{10... | collective-permute-start | bytes 3145736 | tf_op jit(solution)/shard_map/ppermute | solution.py:497
  720.1 48.7 %collective-permute-start.69 = (bf16[256,2048]{1,0:T(8,128)(2,1)}, bf16[256,2048]{1,0:T(8,128)(2,1)}, u32[]{:S(2)}, u32[]{:S(2)}) collective-permute-start(bf16[256,2048]{1,0:T(8,128)(2,1)} %pad_maximum_fusion.7), channel_id=1, source_target_pairs={{0,8},{8,0},{16,24},{24,16},{1,9},{9,1},{17,25},{25,17},{2,10},{10... | collective-permute-start | bytes 3145736 | tf_op jit(solution)/shard_map/ppermute | solution.py:497
  725.0 43.8 %collective-permute-start.70 = (bf16[256,2048]{1,0:T(8,128)(2,1)}, bf16[256,2048]{1,0:T(8,128)(2,1)}, u32[]{:S(2)}, u32[]{:S(2)}) collective-permute-start(bf16[256,2048]{1,0:T(8,128)(2,1)} %pad_maximum_fusion.8), channel_id=1, source_target_pairs={{0,2},{1,3},{2,0},{3,1},{4,6},{5,7},{6,4},{7,5},{8,10},{9,11},{10,... | collective-permute-start | bytes 3145736 | tf_op jit(solution)/shard_map/ppermute | solution.py:494
  732.3 39.4 %collective-permute-start.73 = (bf16[256,2048]{1,0:T(8,128)(2,1)S(1)}, bf16[256,2048]{1,0:T(8,128)(2,1)S(1)}, u32[]{:S(2)}, u32[]{:S(2)}) collective-permute-start(bf16[256,2048]{1,0:T(8,128)(2,1)S(1)} %bitcast.157), channel_id=1, source_target_pairs={{1,8},{3,10},{5,12},{7,14},{8,1},{10,3},{12,5},{14,7},{17,24},{19,... | collective-permute-start | bytes 3145736 | tf_op jit(solution)/shard_map/ppermute | solution.py:512
  776.0 44.8 %collective-permute-start.77 = (bf16[2,2,64,1024]{3,2,1,0:T(8,128)(2,1)S(1)}, bf16[2,2,64,1024]{3,2,1,0:T(8,128)(2,1)S(1)}, u32[]{:S(2)}, u32[]{:S(2)}) collective-permute-start(bf16[2,2,64,1024]{3,2,1,0:T(8,128)(2,1)S(1)} %dynamic-slice_bitcast_fusion.1), channel_id=1, source_target_pairs={{0,1},{1,0},{2,3},{3,2},{4,5},{5,4},{6,7},{7,6},{8,9},{9,8},{10,11... | collective-permute-start | bytes 1572872 | tf_op jit(solution)/shard_map/ppermute | solution.py:494
  788.3 55.7 %collective-permute-start.75 = (bf16[2,2,1,2,2,64,768]{6,5,4,3,2,1,0:T(8,128)(2,1)S(1)}, bf16[2,2,1,2,2,64,768]{6,5,4,3,2,1,0:T(8,128)(2,1)S(1)}, u32[]{:S(2)}, u32[]{:S(2)}) collective-permute-start(bf16[2,2,1,2,2,64,768]{6,5,4,3,2,1,0:T(8,128)(2,1)S(1)} %constant_dynamic-slice_fusion.2), channel_id=1, source_target_pairs={{0,4},{1,5},{2,6},{3,7},{4,0},{5,1},{6,2},{7,3},{8,12},{9,13},{10,... | collective-permute-start | bytes 4718600 | tf_op jit(solution)/shard_map/ppermute | solution.py:494
  789.5 53.8 %collective-permute-start.74 = (bf16[256,2048]{1,0:T(8,128)(2,1)S(1)}, bf16[256,2048]{1,0:T(8,128)(2,1)S(1)}, u32[]{:S(2)}, u32[]{:S(2)}) collective-permute-start(bf16[256,2048]{1,0:T(8,128)(2,1)S(1)} %fusion.9), channel_id=1, source_target_pairs={{2,16},{3,17},{6,20},{7,21},{10,24},{11,25},{14,28},{15,29},{16,2}... | collective-permute-start | bytes 3145736 | tf_op jit(solution)/shard_map/ppermute | solution.py:512
  846.5 45.3 %collective-permute-start.82 = (bf16[1,2,1,2,2,64,768]{6,5,4,3,2,1,0:T(8,128)(2,1)S(1)}, bf16[1,2,1,2,2,64,768]{6,5,4,3,2,1,0:T(8,128)(2,1)S(1)}, u32[]{:S(2)}, u32[]{:S(2)}) collective-permute-start(bf16[1,2,1,2,2,64,768]{6,5,4,3,2,1,0:T(8,128)(2,1)S(1)} %constant_dynamic-slice_fusion), channel_id=1, source_target_pairs={{0,16},{8,24},{16,0},{24,8},{1,17},{9,25},{17,1},{25,9},{2,18},{10... | collective-permute-start | bytes 2359304 | tf_op jit(solution)/shard_map/ppermute | solution.py:497
  846.6 45.5 %collective-permute-start.79 = (bf16[64,4096]{1,0:T(8,128)(2,1)S(1)}, bf16[64,4096]{1,0:T(8,128)(2,1)S(1)}, u32[]{:S(2)}, u32[]{:S(2)}) collective-permute-start(bf16[64,4096]{1,0:T(8,128)(2,1)S(1)} %pad_maximum_fusion.14), channel_id=1, source_target_pairs={{0,8},{8,0},{16,24},{24,16},{1,9},{9,1},{17,25},{25,17},{2,10},{10... | collective-permute-start | bytes 1572872 | tf_op jit(solution)/shard_map/ppermute | solution.py:497
  850.2 41.9 %collective-permute-start.80 = (bf16[64,4096]{1,0:T(8,128)(2,1)S(1)}, bf16[64,4096]{1,0:T(8,128)(2,1)S(1)}, u32[]{:S(2)}, u32[]{:S(2)}) collective-permute-start(bf16[64,4096]{1,0:T(8,128)(2,1)S(1)} %pad_maximum_fusion.15), channel_id=1, source_target_pairs={{0,2},{1,3},{2,0},{3,1},{4,6},{5,7},{6,4},{7,5},{8,10},{9,11},{10,... | collective-permute-start | bytes 1572872 | tf_op jit(solution)/shard_map/ppermute | solution.py:494
  854.5 40.0 %collective-permute-start.81 = (bf16[64,4096]{1,0:T(8,128)(2,1)S(1)}, bf16[64,4096]{1,0:T(8,128)(2,1)S(1)}, u32[]{:S(2)}, u32[]{:S(2)}) collective-permute-start(bf16[64,4096]{1,0:T(8,128)(2,1)S(1)} %pad_maximum_fusion.16), channel_id=1, source_target_pairs={{0,10},{1,11},{2,8},{3,9},{4,14},{5,15},{6,12},{7,13},{8,2},{9,3},... | collective-permute-start | bytes 1572872 | tf_op jit(solution)/shard_map/ppermute | solution.py:505
  (151 other events, 2534.4 us)

commit v5 on v4

--- a/solution.py
+++ b/solution.py
@@ -612,18 +612,22 @@
 
     region = lambda *values: lax.optimization_barrier(values)
 
-    gu_own, gu_send = take_columns([group, group ^ near], [w_gate, w_up], shards, planes)
+    gate_own, gate_send = take_columns([group, group ^ near], [w_gate], shards, planes)
+    gate_own_y = over_y(gate_own)
+    up_own, up_send = take_columns([group, group ^ near], [w_up], shards, planes)
+    up_own_y = over_y(up_own)
     stream_low = swap(tokens.reshape(rows, width))
     qkv_own = head_columns(group)
     qkv_other = flip(head_columns(group ^ near), 2)
-    gu_own_y = over_y(gu_own)
     heads_first, heads_rest = own_heads(w_out)
     stream = stream_low.astype(F32)
     normed_one, inverse_one = normalize(stream)
     qkv_both = jnp.concatenate([qkv_own, qkv_other], 0)
-    h1, stream_low, qkv_both, gu_own, gu_own_y, gu_send, heads_first, w_down = region(
-        [normed_one.astype(BF)], stream_low, qkv_both, gu_own, gu_own_y, gu_send, heads_first, w_down
-    )
+    gate_parts, up_parts = [gate_own, gate_send, *gate_own_y], [up_own, up_send, *up_own_y]
+    h1, stream_low, qkv_both, gate_parts, up_parts, heads_first, w_down = region(
+        [normed_one.astype(BF)], stream_low, qkv_both, gate_parts, up_parts, heads_first, w_down
+    )
+    gu_own, gu_send, *gu_own_y = [jnp.concatenate(v, 1) for v in zip(gate_parts, up_parts)]
 
     h1 = h1 + [hop(h1[0], j) for j in early]
     qkv_y = over_y(qkv_both)
@@ -709,9 +713,8 @@
     sums0, grad_output, output = region(sums0, grad_output, output)
 
     sums = sums0
-    for j in range(1, planes):
-        sums = sums + hop(sums0, j)
-    sums = sums + flip_ctx(sums, near)
+    for bits in range(1, planes):
+        sums = sums + flip_ctx(sums0, bits)
     low_grad, low_output, sums = region(grad_output.astype(BF), output.astype(BF), sums)
 
     steps = [1 << b for b in reversed(range(2, shards.bit_length() - 1))]
@@ -810,17 +813,18 @@
     qkv_half = outer(h1, [dqkv], 1 - core, False)
     mixed = mixed.reshape(planes * rows, mine)
     out_half = outer([mixed], dab, 1 - core, True)
-    dqkv, qkv_half, out_half, g_gate, g_down, up_first, up_second = region(
-        dqkv, qkv_half, out_half, g_gate, g_down, up_first, up_second
+    dqkv, qkv_half, out_half, g_gate, g_down, up_first, up_second, sums = region(
+        dqkv, qkv_half, out_half, g_gate, g_down, up_first, up_second, sums
     )
 
     qkv_away, out_away = flip(qkv_half, 1), flip(out_half, 1)
     backs = project([dqkv[i * rows : (i + 1) * rows] for i in range(planes)], w_qkv, True, group_types)
     up_second = across_y(up_second, 2)
+    sums = sums + flip(sums, 2)
     gate_first, gate_second = jnp.split(g_gate, 2, -1)
     gate_first = across_far(gate_first)
-    backs, dqkv, qkv_away, out_away, up_second, gate_first, gate_second = region(
-        backs, dqkv, qkv_away, out_away, up_second, gate_first, gate_second
+    backs, dqkv, qkv_away, out_away, up_second, gate_first, gate_second, sums = region(
+        backs, dqkv, qkv_away, out_away, up_second, gate_first, gate_second, sums
     )
 
     gate_second = across_far(gate_second)

time: 944 us -> 943 us (level)
  waiting for transfers between devices: 388 us -> 378 us
    ppermute x50 -> x51, waiting for transfers between devices: 111 us -> 107 us  [flip(): return lax.ppermute(array, 'fsdp', [(i, i ^ bits) for i in range(shards)])]
    ppermute x50 -> x51, starting transfers between devices: 43.1 us -> 40.1 us  [flip(): return lax.ppermute(array, 'fsdp', [(i, i ^ bits) for i in range(shards)])]
    ppermute x24 -> x25, waiting for transfers between devices: 157 us -> 155 us  [flip_ctx(): return lax.ppermute(array, 'ctx', [(i, i ^ bits) for i in range(planes)])]
    unnamed x184 -> x192, local copies, waits for them, and re-layouts: 23.8 us -> 22.2 us
    ppermute x24 -> x25, starting transfers between devices: 50.7 us -> 51.3 us  [flip_ctx(): return lax.ppermute(array, 'ctx', [(i, i ^ bits) for i in range(planes)])]
  transfers between devices with their start and end apart: 88 -> 89, of which waited for: 48 -> 46; matrix products, arithmetic and copies ran while one was open for 9% -> 10% of each run, Pallas kernels for 27% -> 27%
where the time goes in v5:
time: 943 us; the launch traced here: 935 us
  waiting for transfers between devices  378 us (40%)
  Pallas kernels  270 us (29%)
  starting transfers between devices  131 us (14%)
  other arithmetic  83.5 us (9%)
  local copies, waits for them, and re-layouts  66.6 us (7%)
    ppermute x25, waiting for transfers between devices, flip_ctx(): return lax.ppermute(array, 'ctx', [(i, i ^ bits) for i in range(planes)])  155 us
    ppermute x51, waiting for transfers between devices, flip(): return lax.ppermute(array, 'fsdp', [(i, i ^ bits) for i in range(shards)])  107 us
    ppermute x7, waiting for transfers between devices, send(): lax.ppermute(array, both, [(i, to) for i, to in enumerate(homes) if i !=...  88.7 us
    pallas_call x10, Pallas kernels, outer(): pl.pallas_call(kernel, grid_spec=pltpu.PrefetchScalarGridSpec(num_scalar_...  66.2 us
    ppermute x25, starting transfers between devices, flip_ctx(): return lax.ppermute(array, 'ctx', [(i, i ^ bits) for i in range(planes)])  51.3 us
    pallas_call x2, Pallas kernels, mlp_back(): pl.pallas_call(functools.partial(down_kernel, count), grid=(tiles,), in_s...  43.3 us
    pallas_call x2, Pallas kernels, mlp(): pl.pallas_call(functools.partial(up_kernel, count), grid=(tiles,), in_spe...  40.6 us
    ppermute x51, starting transfers between devices, flip(): return lax.ppermute(array, 'fsdp', [(i, i ^ bits) for i in range(shards)])  40.1 us
  transfers between devices with their start and end apart: 89, of which 46 were waited for; matrix products, arithmetic and copies ran while one was open for 10% of the time, Pallas kernels for 27%

profile of v5, /device:TPU:16, one launch (start us, length us, event | category | flops | bytes accessed | tf_op | source)
XLA Modules:
  0.0 934.6 jit_solution(5947328729269407829)
XLA Ops:
  23.3 23.7 %collective-permute-done.1 = bf16[256,1536]{1,0:T(8,128)(2,1)} collective-permute-done((bf16[256,1536]{1,0:T(8,128)(2,1)}, bf16[256,1536]{1,0:T(8,128)(2,1)}, u32[]{:S(2)}, u32[]{:S(2)}) %collective-permute-start.1) | collective-permute-done | bytes 786464 | tf_op jit(solution)/shard_map/ppermute | solution.py:494
  61.3 12.2 %collective-permute-start.5 = (bf16[256,2048]{1,0:T(8,128)(2,1)S(1)}, bf16[256,2048]{1,0:T(8,128)(2,1)S(1)}, u32[]{:S(2)}, u32[]{:S(2)}) collective-permute-start(bf16[256,2048]{1,0:T(8,128)(2,1)S(1)} %fusion.4.refs_0_), channel_id=1, source_target_pairs={{0,8},{8,0},{16,24},{24,16},{1,9},{9,1},{17,25},{25,17},{2,10},{10... | collective-permute-start | bytes 3145736 | tf_op jit(solution)/shard_map/ppermute | solution.py:497
  81.7 15.5 %collective-permute-done.5.refs_1_ = bf16[256,2048]{1,0:T(8,128)(2,1)S(1)} collective-permute-done((bf16[256,2048]{1,0:T(8,128)(2,1)S(1)}, bf16[256,2048]{1,0:T(8,128)(2,1)S(1)}, u32[]{:S(2)}, u32[]{:S(2)}) %collective-permute-start.5) | collective-permute-done | bytes 1048608 | tf_op jit(solution)/shard_map/ppermute | solution.py:497
  107.3 24.3 %collective-permute-done.10 = bf16[256,2048]{1,0:T(8,128)(2,1)S(1)} collective-permute-done((bf16[256,2048]{1,0:T(8,128)(2,1)}, bf16[256,2048]{1,0:T(8,128)(2,1)S(1)}, u32[]{:S(2)}, u32[]{:S(2)}) %collective-permute-start.10) | collective-permute-done | bytes 1048608 | tf_op jit(solution)/shard_map/ppermute | solution.py:573
  154.2 10.1 %project.4 = f32[1024,1536]{1,0:T(8,128)} custom-call(bf16[256,2048]{1,0:T(8,128)(2,1)S(1)} %fusion.4.refs_0_, bf16[256,2048]{1,0:T(8,128)(2,1)S(1)} %collective-permute-done.5.refs_1_, bf16[256,2048]{1,0:T(8,128)(2,1)S(1)} %collective-permute-done.6.refs_2_, bf16[256,2048]{1,0:T(8,128)(2,1)S(1)} %constant_dynamic-update-slice_fusion.refs_3_, ...), custom_call_target="tpu_custom_call" | custom-call | flops 1024 | bytes 1024 | tf_op jit(solution)/shard_map/project/pallas_call | solution.py:378
  164.3 21.5 %attend.1 = (bf16[4,1,2,128,512]{4,3,2,1,0:T(8,128)(2,1)}, f32[4,1,2,128,512]{4,3,2,1,0:T(8,128)}) custom-call(s32[8]{0:T(128)} %fusion.41.order, f32[4,1,2,128,1536]{4,3,2,1,0:T(8,128)} %bitcast.142, f32[1024,128]{1,0:T(8,128)} %get-tuple-element.517.cos, f32[1024,128]{1,0:T(8,128)} %get-tuple-element.518.sin), custom_call_target="tpu_custom_call" | custom-call | flops 1024 | bytes 1024 | tf_op jit(solution)/shard_map/attend/pallas_call | solution.py:153
  196.4 13.3 %collective-permute-done.17 = bf16[128,2048]{1,0:T(8,128)(2,1)S(1)} collective-permute-done((bf16[128,2048]{1,0:T(8,128)(2,1)S(1)}, bf16[128,2048]{1,0:T(8,128)(2,1)S(1)}, u32[]{:S(2)}, u32[]{:S(2)}) %collective-permute-start.17) | collective-permute-done | bytes 524320 | tf_op jit(solution)/shard_map/ppermute | solution.py:494
  226.5 19.7 %collective-permute-done.22 = bf16[256,2048]{1,0:T(8,128)(2,1)S(1)} collective-permute-done((bf16[256,2048]{1,0:T(8,128)(2,1)S(1)}, bf16[256,2048]{1,0:T(8,128)(2,1)S(1)}, u32[]{:S(2)}, u32[]{:S(2)}) %collective-permute-start.22) | collective-permute-done | bytes 1048608 | tf_op jit(solution)/shard_map/ppermute | solution.py:497
  264.0 12.6 %assemble.6 = bf16[8,256,4096]{2,1,0:T(8,128)(2,1)} custom-call(s32[8]{0:T(128)} %stack.96.places, bf16[256,4096]{1,0:T(8,128)(2,1)} %copy-done.40, bf16[256,4096]{1,0:T(8,128)(2,1)} %copy-done.55, bf16[256,4096]{1,0:T(8,128)(2,1)} %collective-permute-done.15.refs_2_, bf16[256,4096]{1,0:T(8,128)(2,1)} %collective-permute-done.29.refs_3_, ...), custom_call_target="tpu_custom_call" | custom-call | flops 1024 | bytes 1024 | tf_op jit(solution)/shard_map/assemble/pallas_call | solution.py:415
  286.0 20.4 %mlp.2 = (bf16[1024,2048]{1,0:T(8,128)(2,1)}, f32[1024,2048]{1,0:T(8,128)}, f32[1024,2048]{1,0:T(8,128)}, bf16[1024,2048]{1,0:T(8,128)(2,1)}, bf16[256,2048]{1,0...) custom-call(bf16[256,2048]{1,0:T(8,128)(2,1)S(1)} %collective-permute-done.27.refs_0_, ...), custom_call_target="tpu_custom_call" | custom-call | flops 1024 | bytes 1024 | tf_op jit(solution)/shard_map/mlp/pallas_call | solution.py:235
  306.4 12.1 %collective-permute-done.31 = bf16[128,2048]{1,0:T(8,128)(2,1)S(1)} collective-permute-done((bf16[128,2048]{1,0:T(8,128)(2,1)S(1)}, bf16[128,2048]{1,0:T(8,128)(2,1)S(1)}, u32[]{:S(2)}, u32[]{:S(2)}) %collective-permute-start.31) | collective-permute-done | bytes 524320 | tf_op jit(solution)/shard_map/ppermute | solution.py:494
  318.7 20.2 %mlp.3 = (bf16[1024,2048]{1,0:T(8,128)(2,1)}, f32[1024,2048]{1,0:T(8,128)}, f32[1024,2048]{1,0:T(8,128)}, bf16[1024,2048]{1,0:T(8,128)(2,1)}, f32[256,2048]{1,0:T(8,128)S(1)}, /*index=5*/bf16[256,2048]{1,0:T(8,128)(2,1)S(1)}) custom-call(bf16[256,2048]{1,0:T(8,128)(2,1)S(1)} %fusion.11.refs_0_, ...), custom_call_target="tpu_custom_call", output_to_operand_aliasing={{0}: (5, {}), {1}: (6, {}), {2}: (7, {}), {3}: (8, {})} | custom-call | flops 1024 | bytes 1024 | tf_op jit(solution)/shard_map/mlp/pallas_call | solution.py:235
  357.3 21.4 %collective-permute-done.36 = s32[256,1]{0,1:T(1,128)S(1)} collective-permute-done((s32[256,1]{0,1:T(1,128)S(1)}, s32[256,1]{0,1:T(1,128)S(1)}, u32[]{:S(2)}, u32[]{:S(2)}) %collective-permute-start.36) | collective-permute-done | bytes 1056 | tf_op jit(solution)/shard_map/ppermute | solution.py:512
  398.4 14.3 %collective-permute-done.41.refs_0_.refs_1_ = bf16[256,2048]{1,0:T(8,128)(2,1)S(1)} collective-permute-done((bf16[256,2048]{1,0:T(8,128)(2,1)S(1)}, bf16[256,2048]{1,0:T(8,128)(2,1)S(1)}, u32[]{:S(2)}, u32[]{:S(2)}) %collective-permute-start.41) | collective-permute-done | bytes 1048608 | tf_op jit(solution)/shard_map/ppermute | solution.py:497
  417.7 21.7 %mlp_back.2 = (bf16[1024,2048]{1,0:T(8,128)(2,1)}, bf16[1024,2048]{1,0:T(8,128)(2,1)}, bf16[1024,2048]{1,0:T(8,128)(2,1)}, bf16[256,2048]{1,0:T(8,128)(2,1)S(1)}, bf16[256,2048]{1,0:T(8,128)(2,1)S(1)}) custom-call(bf16[256,2048]{1,0:T(8,128)(2,1)S(1)} %collective-permute-done.41.refs_0_.refs_1_, ...), custom_call_target="tpu_custom_call" | custom-call | flops 1024 | bytes 1024 | tf_op jit(solution)/shard_map/mlp_back/pallas_call | solution.py:298
  451.1 21.6 %mlp_back.3 = (bf16[1024,2048]{1,0:T(8,128)(2,1)}, bf16[1024,2048]{1,0:T(8,128)(2,1)}, bf16[1024,2048]{1,0:T(8,128)(2,1)}, f32[256,2048]{1,0:T(8,128)S(1)}, bf16[256,2048]{1,0:T(8,128)(2,1)}) custom-call(bf16[256,2048]{1,0:T(8,128)(2,1)S(1)} %convert_element_type.248.refs_0_.refs_3_, ...), custom_call_target="tpu_custom_call", output_to_operand_aliasing={{0}: (7, {}), {1}: (8, {}), {2}: (9, {})} | custom-call | flops 1024 | bytes 1024 | tf_op jit(solution)/shard_map/mlp_back/pallas_call | solution.py:298
  513.6 22.0 %collective-permute-done.52 = bf16[256,2048]{1,0:T(8,128)(2,1)} collective-permute-done((bf16[256,2048]{1,0:T(8,128)(2,1)}, bf16[256,2048]{1,0:T(8,128)(2,1)}, u32[]{:S(2)}, u32[]{:S(2)}) %collective-permute-start.52) | collective-permute-done | bytes 1048608 | tf_op jit(solution)/shard_map/ppermute | solution.py:512
  605.9 27.9 %attend_back.1 = bf16[4,1,2,128,1536]{4,3,2,1,0:T(8,128)(2,1)} custom-call(s32[8]{0:T(128)} %fusion.41.order, f32[4,1,2,128,1536]{4,3,2,1,0:T(8,128)} %bitcast.143, f32[4,1,2,128,512]{4,3,2,1,0:T(8,128)} %get-tuple-element.366.lse, bf16[4,1,2,128,512]{4,3,2,1,0:T(8,128)(2,1)} %bitcast.123, f32[1024,128]{1,0:T(8,128)} %get-tuple-element.517.cos, ...), custom_call_target="tpu_custom_call" | custom-call | flops 1024 | bytes 1024 | tf_op jit(solution)/shard_map/attend_back/pallas_call | solution.py:177
  668.9 12.9 %collective-permute-done.65 = bf16[1,2,1,2,2,64,512]{6,5,4,3,2,1,0:T(8,128)(2,1)S(1)} collective-permute-done((bf16[1,2,1,2,2,64,512]{6,5,4,3,2,1,0:T(8,128)(2,1)}, bf16[1,2,1,2,2,64,512]{6,5,4,3,2,1,0:T(8,128)(2,1)S(1)}, u32[]{:S(2)}, u32[]{:S(2)}) %collective-permute-start.65) | collective-permute-done | bytes 524320 | tf_op jit(solution)/shard_map/ppermute | solution.py:497
  736.8 27.4 %collective-permute-done.70 = bf16[256,2048]{1,0:T(8,128)(2,1)} collective-permute-done((bf16[256,2048]{1,0:T(8,128)(2,1)}, bf16[256,2048]{1,0:T(8,128)(2,1)}, u32[]{:S(2)}, u32[]{:S(2)}) %collective-permute-start.70) | collective-permute-done | bytes 1048608 | tf_op jit(solution)/shard_map/ppermute | solution.py:497
  788.8 28.1 %collective-permute-done.77 = bf16[64,2048]{1,0:T(8,128)(2,1)S(1)} collective-permute-done((bf16[64,2048]{1,0:T(8,128)(2,1)S(1)}, bf16[64,2048]{1,0:T(8,128)(2,1)S(1)}, u32[]{:S(2)}, u32[]{:S(2)}) %collective-permute-start.77) | collective-permute-done | bytes 262176 | tf_op jit(solution)/shard_map/ppermute | solution.py:497
  818.4 21.0 %collective-permute-done.75 = bf16[256,2048]{1,0:T(8,128)(2,1)S(1)} collective-permute-done((bf16[256,2048]{1,0:T(8,128)(2,1)S(1)}, bf16[256,2048]{1,0:T(8,128)(2,1)S(1)}, u32[]{:S(2)}, u32[]{:S(2)}) %collective-permute-start.75) | collective-permute-done | bytes 1048608 | tf_op jit(solution)/shard_map/ppermute | solution.py:512
  851.3 20.5 %collective-permute-done.84 = bf16[64,2048]{1,0:T(8,128)(2,1)S(1)} collective-permute-done((bf16[64,2048]{1,0:T(8,128)(2,1)S(1)}, bf16[64,2048]{1,0:T(8,128)(2,1)S(1)}, u32[]{:S(2)}, u32[]{:S(2)}) %collective-permute-start.84) | collective-permute-done | bytes 262176 | tf_op jit(solution)/shard_map/ppermute | solution.py:512
  872.4 15.7 %collective-permute-done.83 = bf16[1,2,1,2,2,64,768]{6,5,4,3,2,1,0:T(8,128)(2,1)S(1)} collective-permute-done((bf16[1,2,1,2,2,64,768]{6,5,4,3,2,1,0:T(8,128)(2,1)S(1)}, bf16[1,2,1,2,2,64,768]{6,5,4,3,2,1,0:T(8,128)(2,1)S(1)}, u32[]{:S(2)}, u32[]{:S(2)}) %collective-permute-start.83) | collective-permute-done | bytes 786464 | tf_op jit(solution)/shard_map/ppermute | solution.py:497
  (523 shorter events, 468.7 us)
Async XLA Ops:
  4.9 42.1 %collective-permute-start.1 = (bf16[256,1536]{1,0:T(8,128)(2,1)}, bf16[256,1536]{1,0:T(8,128)(2,1)}, u32[]{:S(2)}, u32[]{:S(2)}) collective-permute-start(bf16[256,1536]{1,0:T(8,128)(2,1)} %pad_maximum_fusion.13), channel_id=1, source_target_pairs={{0,2},{1,3},{2,0},{3,1},{4,6},{5,7},{6,4},{7,5},{8,10},{9,11},{10,... | collective-permute-start | bytes 2359304 | tf_op jit(solution)/shard_map/ppermute | solution.py:494
  6.4 46.8 %collective-permute-start = (bf16[256,2048]{1,0:T(8,128)(2,1)S(1)}, bf16[256,2048]{1,0:T(8,128)(2,1)S(1)}, u32[]{:S(2)}, u32[]{:S(2)}) collective-permute-start(bf16[256,2048]{1,0:T(8,128)(2,1)S(1)} %bitcast.162), channel_id=1, source_target_pairs={{2,16},{3,17},{6,20},{7,21},{10,24},{11,25},{14,28},{15,29},{16,2}... | collective-permute-start | bytes 3145736 | tf_op jit(solution)/shard_map/ppermute | solution.py:512
  13.9 42.5 %collective-permute-start.2 = (bf16[256,2048]{1,0:T(8,128)(2,1)}, bf16[256,2048]{1,0:T(8,128)(2,1)}, u32[]{:S(2)}, u32[]{:S(2)}) collective-permute-start(bf16[256,2048]{1,0:T(8,128)(2,1)} %get-tuple-element.260), channel_id=1, source_target_pairs={{0,4},{1,5},{2,6},{3,7},{4,0},{5,1},{6,2},{7,3},{8,12},{9,13},{10,... | collective-permute-start | bytes 3145736 | tf_op jit(solution)/shard_map/ppermute | solution.py:494
  20.6 40.7 %collective-permute-start.3 = (bf16[256,2048]{1,0:T(8,128)(2,1)}, bf16[256,2048]{1,0:T(8,128)(2,1)}, u32[]{:S(2)}, u32[]{:S(2)}) collective-permute-start(bf16[256,2048]{1,0:T(8,128)(2,1)} %get-tuple-element.261), channel_id=1, source_target_pairs={{0,4},{1,5},{2,6},{3,7},{4,0},{5,1},{6,2},{7,3},{8,12},{9,13},{10,... | collective-permute-start | bytes 3145736 | tf_op jit(solution)/shard_map/ppermute | solution.py:494
  74.6 58.4 %collective-permute-start.12 = (bf16[512,1536]{1,0:T(8,128)(2,1)}, bf16[512,1536]{1,0:T(8,128)(2,1)S(1)}, u32[]{:S(2)}, u32[]{:S(2)}) collective-permute-start(bf16[512,1536]{1,0:T(8,128)(2,1)} %pad_maximum_fusion.6.refs_0_), channel_id=1, source_target_pairs={{0,4},{1,5},{2,6},{3,7},{4,0},{5,1},{6,2},{7,3},{8,12},{9,13},{10,... | collective-permute-start | bytes 4718600 | tf_op jit(solution)/shard_map/ppermute | solution.py:494
  74.6 57.0 %collective-permute-start.10 = (bf16[256,2048]{1,0:T(8,128)(2,1)}, bf16[256,2048]{1,0:T(8,128)(2,1)S(1)}, u32[]{:S(2)}, u32[]{:S(2)}) collective-permute-start(bf16[256,2048]{1,0:T(8,128)(2,1)} %broadcast_select_fusion.2), channel_id=1, source_target_pairs={{0,4},{1,5},{6,2},{7,3},{8,12},{9,13},{14,10},{15,11},{16,20},{17,... | collective-permute-start | bytes 3145736 | tf_op jit(solution)/shard_map/ppermute | solution.py:573
  137.0 54.9 %collective-permute-start.16 = (bf16[512,2048]{1,0:T(8,128)(2,1)}, bf16[512,2048]{1,0:T(8,128)(2,1)}, u32[]{:S(2)}, u32[]{:S(2)}) collective-permute-start(bf16[512,2048]{1,0:T(8,128)(2,1)} %constant_dynamic-update-slice_fusion.2.refs_0_), channel_id=1, source_target_pairs={{0,4},{1,5},{2,6},{3,7},{4,0},{5,1},{6,2},{7,3},{8,12},{9,13},{10,... | collective-permute-start | bytes 6291464 | tf_op jit(solution)/shard_map/ppermute | solution.py:494
  137.9 53.9 %collective-permute-start.15 = (bf16[256,4096]{1,0:T(8,128)(2,1)}, bf16[256,4096]{1,0:T(8,128)(2,1)}, u32[]{:S(2)}, u32[]{:S(2)}) collective-permute-start(bf16[256,4096]{1,0:T(8,128)(2,1)} %pad_maximum_fusion), channel_id=1, source_target_pairs={{0,2},{1,3},{2,0},{3,1},{4,6},{5,7},{6,4},{7,5},{8,10},{9,11},{10,... | collective-permute-start | bytes 6291464 | tf_op jit(solution)/shard_map/ppermute | solution.py:494
  279.9 59.1 %collective-permute-start.35 = (bf16[256,2048]{1,0:T(8,128)(2,1)S(1)}, bf16[256,2048]{1,0:T(8,128)(2,1)S(1)}, u32[]{:S(2)}, u32[]{:S(2)}) collective-permute-start(bf16[256,2048]{1,0:T(8,128)(2,1)S(1)} %bitcast.163), channel_id=1, source_target_pairs={{2,16},{3,17},{6,20},{7,21},{10,24},{11,25},{14,28},{15,29},{16,2}... | collective-permute-start | bytes 3145736 | tf_op jit(solution)/shard_map/ppermute | solution.py:512
  486.2 49.5 %collective-permute-start.52 = (bf16[256,2048]{1,0:T(8,128)(2,1)}, bf16[256,2048]{1,0:T(8,128)(2,1)}, u32[]{:S(2)}, u32[]{:S(2)}) collective-permute-start(bf16[256,2048]{1,0:T(8,128)(2,1)} %convert_element_type.249), channel_id=1, source_target_pairs={{2,16},{3,17},{6,20},{7,21},{10,24},{11,25},{14,28},{15,29},{16,2}... | collective-permute-start | bytes 3145736 | tf_op jit(solution)/shard_map/ppermute | solution.py:512
  493.9 47.1 %collective-permute-start.51 = (bf16[2,1,256,2048]{3,2,1,0:T(8,128)(2,1)}, bf16[2,1,256,2048]{3,2,1,0:T(8,128)(2,1)S(1)}, u32[]{:S(2)}, u32[]{:S(2)}) collective-permute-start(bf16[2,1,256,2048]{3,2,1,0:T(8,128)(2,1)} %constant_dynamic-slice_fusion.11), channel_id=1, source_target_pairs={{0,4},{1,5},{2,6},{3,7},{4,0},{5,1},{6,2},{7,3},{8,12},{9,13},{10,... | collective-permute-start | bytes 6291464 | tf_op jit(solution)/shard_map/ppermute | solution.py:494
  576.9 74.5 %collective-permute-start.59 = (bf16[2,2,1,2,2,64,1024]{6,5,4,3,2,1,0:T(8,128)(2,1)}, bf16[2,2,1,2,2,64,1024]{6,5,4,3,2,1,0:T(8,128)(2,1)}, u32[]{:S(2)}, u32[]{:S(2)}) collective-permute-start(bf16[2,2,1,2,2,64,1024]{6,5,4,3,2,1,0:T(8,128)(2,1)} %constant_dynamic-slice_fusion.10), channel_id=1, source_target_pairs={{0,4},{1,5},{2,6},{3,7},{4,0},{5,1},{6,2},{7,3},{8,12},{9,13},{10,... | collective-permute-start | bytes 6291464 | tf_op jit(solution)/shard_map/ppermute | solution.py:494
  592.5 53.7 %collective-permute-start.61 = (bf16[2,2,1,2,2,64,512]{6,5,4,3,2,1,0:T(8,128)(2,1)}, bf16[2,2,1,2,2,64,512]{6,5,4,3,2,1,0:T(8,128)(2,1)}, u32[]{:S(2)}, u32[]{:S(2)}) collective-permute-start(bf16[2,2,1,2,2,64,512]{6,5,4,3,2,1,0:T(8,128)(2,1)} %constant_dynamic-slice_fusion.8), channel_id=1, source_target_pairs={{0,4},{1,5},{2,6},{3,7},{4,0},{5,1},{6,2},{7,3},{8,12},{9,13},{10,... | collective-permute-start | bytes 3145736 | tf_op jit(solution)/shard_map/ppermute | solution.py:494
  595.3 53.6 %collective-permute-start.60 = (bf16[1,1,256,2048]{3,2,1,0:T(8,128)(2,1)}, bf16[1,1,256,2048]{3,2,1,0:T(8,128)(2,1)}, u32[]{:S(2)}, u32[]{:S(2)}) collective-permute-start(bf16[1,1,256,2048]{3,2,1,0:T(8,128)(2,1)} %constant_dynamic-slice_fusion.9), channel_id=1, source_target_pairs={{0,16},{8,24},{16,0},{24,8},{1,17},{9,25},{17,1},{25,9},{2,18},{10... | collective-permute-start | bytes 3145736 | tf_op jit(solution)/shard_map/ppermute | solution.py:497
  715.2 49.0 %collective-permute-start.70 = (bf16[256,2048]{1,0:T(8,128)(2,1)}, bf16[256,2048]{1,0:T(8,128)(2,1)}, u32[]{:S(2)}, u32[]{:S(2)}) collective-permute-start(bf16[256,2048]{1,0:T(8,128)(2,1)} %pad_maximum_fusion.10), channel_id=1, source_target_pairs={{0,8},{8,0},{16,24},{24,16},{1,9},{9,1},{17,25},{25,17},{2,10},{10... | collective-permute-start | bytes 3145736 | tf_op jit(solution)/shard_map/ppermute | solution.py:497
  720.3 43.9 %collective-permute-start.71 = (bf16[256,2048]{1,0:T(8,128)(2,1)}, bf16[256,2048]{1,0:T(8,128)(2,1)}, u32[]{:S(2)}, u32[]{:S(2)}) collective-permute-start(bf16[256,2048]{1,0:T(8,128)(2,1)} %pad_maximum_fusion.11), channel_id=1, source_target_pairs={{0,2},{1,3},{2,0},{3,1},{4,6},{5,7},{6,4},{7,5},{8,10},{9,11},{10,... | collective-permute-start | bytes 3145736 | tf_op jit(solution)/shard_map/ppermute | solution.py:494
  727.7 39.4 %collective-permute-start.74 = (bf16[256,2048]{1,0:T(8,128)(2,1)S(1)}, bf16[256,2048]{1,0:T(8,128)(2,1)S(1)}, u32[]{:S(2)}, u32[]{:S(2)}) collective-permute-start(bf16[256,2048]{1,0:T(8,128)(2,1)S(1)} %bitcast.157), channel_id=1, source_target_pairs={{1,8},{3,10},{5,12},{7,14},{8,1},{10,3},{12,5},{14,7},{17,24},{19,... | collective-permute-start | bytes 3145736 | tf_op jit(solution)/shard_map/ppermute | solution.py:512
  771.4 45.6 %collective-permute-start.78 = (bf16[2,2,64,1024]{3,2,1,0:T(8,128)(2,1)S(1)}, bf16[2,2,64,1024]{3,2,1,0:T(8,128)(2,1)S(1)}, u32[]{:S(2)}, u32[]{:S(2)}) collective-permute-start(bf16[2,2,64,1024]{3,2,1,0:T(8,128)(2,1)S(1)} %dynamic-slice_bitcast_fusion.1), channel_id=1, source_target_pairs={{0,1},{1,0},{2,3},{3,2},{4,5},{5,4},{6,7},{7,6},{8,9},{9,8},{10,11... | collective-permute-start | bytes 1572872 | tf_op jit(solution)/shard_map/ppermute | solution.py:494
  784.0 56.2 %collective-permute-start.76 = (bf16[2,2,1,2,2,64,768]{6,5,4,3,2,1,0:T(8,128)(2,1)S(1)}, bf16[2,2,1,2,2,64,768]{6,5,4,3,2,1,0:T(8,128)(2,1)S(1)}, u32[]{:S(2)}, u32[]{:S(2)}) collective-permute-start(bf16[2,2,1,2,2,64,768]{6,5,4,3,2,1,0:T(8,128)(2,1)S(1)} %constant_dynamic-slice_fusion.2), channel_id=1, source_target_pairs={{0,4},{1,5},{2,6},{3,7},{4,0},{5,1},{6,2},{7,3},{8,12},{9,13},{10,... | collective-permute-start | bytes 4718600 | tf_op jit(solution)/shard_map/ppermute | solution.py:494
  784.5 54.9 %collective-permute-start.75 = (bf16[256,2048]{1,0:T(8,128)(2,1)S(1)}, bf16[256,2048]{1,0:T(8,128)(2,1)S(1)}, u32[]{:S(2)}, u32[]{:S(2)}) collective-permute-start(bf16[256,2048]{1,0:T(8,128)(2,1)S(1)} %fusion.9), channel_id=1, source_target_pairs={{2,16},{3,17},{6,20},{7,21},{10,24},{11,25},{14,28},{15,29},{16,2}... | collective-permute-start | bytes 3145736 | tf_op jit(solution)/shard_map/ppermute | solution.py:512
  842.7 45.3 %collective-permute-start.83 = (bf16[1,2,1,2,2,64,768]{6,5,4,3,2,1,0:T(8,128)(2,1)S(1)}, bf16[1,2,1,2,2,64,768]{6,5,4,3,2,1,0:T(8,128)(2,1)S(1)}, u32[]{:S(2)}, u32[]{:S(2)}) collective-permute-start(bf16[1,2,1,2,2,64,768]{6,5,4,3,2,1,0:T(8,128)(2,1)S(1)} %constant_dynamic-slice_fusion), channel_id=1, source_target_pairs={{0,16},{8,24},{16,0},{24,8},{1,17},{9,25},{17,1},{25,9},{2,18},{10... | collective-permute-start | bytes 2359304 | tf_op jit(solution)/shard_map/ppermute | solution.py:497
  842.8 45.5 %collective-permute-start.80 = (bf16[64,4096]{1,0:T(8,128)(2,1)S(1)}, bf16[64,4096]{1,0:T(8,128)(2,1)S(1)}, u32[]{:S(2)}, u32[]{:S(2)}) collective-permute-start(bf16[64,4096]{1,0:T(8,128)(2,1)S(1)} %pad_maximum_fusion.17), channel_id=1, source_target_pairs={{0,8},{8,0},{16,24},{24,16},{1,9},{9,1},{17,25},{25,17},{2,10},{10... | collective-permute-start | bytes 1572872 | tf_op jit(solution)/shard_map/ppermute | solution.py:497
  845.4 42.9 %collective-permute-start.81 = (bf16[64,4096]{1,0:T(8,128)(2,1)S(1)}, bf16[64,4096]{1,0:T(8,128)(2,1)S(1)}, u32[]{:S(2)}, u32[]{:S(2)}) collective-permute-start(bf16[64,4096]{1,0:T(8,128)(2,1)S(1)} %pad_maximum_fusion.18), channel_id=1, source_target_pairs={{0,2},{1,3},{2,0},{3,1},{4,6},{5,7},{6,4},{7,5},{8,10},{9,11},{10,... | collective-permute-start | bytes 1572872 | tf_op jit(solution)/shard_map/ppermute | solution.py:494
  849.7 40.2 %collective-permute-start.82 = (bf16[64,4096]{1,0:T(8,128)(2,1)S(1)}, bf16[64,4096]{1,0:T(8,128)(2,1)S(1)}, u32[]{:S(2)}, u32[]{:S(2)}) collective-permute-start(bf16[64,4096]{1,0:T(8,128)(2,1)S(1)} %pad_maximum_fusion.19), channel_id=1, source_target_pairs={{0,10},{1,11},{2,8},{3,9},{4,14},{5,15},{6,12},{7,13},{8,2},{9,3},... | collective-permute-start | bytes 1572872 | tf_op jit(solution)/shard_map/ppermute | solution.py:505
  (156 other events, 2649.6 us)

commit v6 on v5

--- a/solution.py
+++ b/solution.py
@@ -828,16 +828,17 @@
     )
 
     gate_second = across_far(gate_second)
-    g_up = jnp.concatenate([up_first, up_second], -1)
+    up_parts = jnp.concatenate([up_first, up_second], -1)
+    up_keep, up_away = (lax.dynamic_slice_in_dim(up_parts, k, 1, 0) for k in (far, 1 - far))
     received = reduce_far(backs)
     g_qkv = parts(outer(h1, [dqkv], core, False, qkv_away))
     g_out = outer([mixed], dab, core, True, out_away)
-    received, backs, g_qkv, g_out, g_down, gate_first, gate_second, g_up = region(
-        received, backs, g_qkv, g_out, g_down, gate_first, gate_second, g_up
+    received, backs, g_qkv, g_out, g_down, gate_first, gate_second, up_keep, up_away = region(
+        received, backs, g_qkv, g_out, g_down, gate_first, gate_second, up_keep, up_away
     )
 
     own, received = reduce_near(backs, received)
-    g_up = across_far(g_up)
+    g_up = (up_keep.astype(F32) + flip_ctx(up_away, near).astype(F32)).astype(BF)
     g_out = across_y(g_out, 0)
     g_gate = jnp.concatenate([gate_first, gate_second], -1)
     g_down = place_rows(

time: 943 us -> 948 us (level)
    unnamed x192 -> x189, local copies, waits for them, and re-layouts: 22.2 us -> 21.5 us
where the time goes in v6:
time: 948 us; the launch traced here: 940 us
  waiting for transfers between devices  383 us (40%)
  Pallas kernels  270 us (28%)
  starting transfers between devices  129 us (14%)
  other arithmetic  82.8 us (9%)
  local copies, waits for them, and re-layouts  69.6 us (7%)
    ppermute x25, waiting for transfers between devices, flip_ctx(): return lax.ppermute(array, 'ctx', [(i, i ^ bits) for i in range(planes)])  162 us
    ppermute x51, waiting for transfers between devices, flip(): return lax.ppermute(array, 'fsdp', [(i, i ^ bits) for i in range(shards)])  104 us
    ppermute x7, waiting for transfers between devices, send(): lax.ppermute(array, both, [(i, to) for i, to in enumerate(homes) if i !=...  87.6 us
    pallas_call x10, Pallas kernels, outer(): pl.pallas_call(kernel, grid_spec=pltpu.PrefetchScalarGridSpec(num_scalar_...  65.8 us
    ppermute x25, starting transfers between devices, flip_ctx(): return lax.ppermute(array, 'ctx', [(i, i ^ bits) for i in range(planes)])  50.8 us
    pallas_call x2, Pallas kernels, mlp_back(): pl.pallas_call(functools.partial(down_kernel, count), grid=(tiles,), in_s...  43.3 us
    pallas_call x2, Pallas kernels, mlp(): pl.pallas_call(functools.partial(up_kernel, count), grid=(tiles,), in_spe...  40.6 us
    ppermute x51, starting transfers between devices, flip(): return lax.ppermute(array, 'fsdp', [(i, i ^ bits) for i in range(shards)])  38.5 us
  transfers between devices with their start and end apart: 89, of which 46 were waited for; matrix products, arithmetic and copies ran while one was open for 10% of the time, Pallas kernels for 27%

profile of v6, /device:TPU:16, one launch (start us, length us, event | category | flops | bytes accessed | tf_op | source)
XLA Modules:
  0.0 939.7 jit_solution(17506084788003104762)
XLA Ops:
  23.2 23.7 %collective-permute-done.1 = bf16[256,1536]{1,0:T(8,128)(2,1)} collective-permute-done((bf16[256,1536]{1,0:T(8,128)(2,1)}, bf16[256,1536]{1,0:T(8,128)(2,1)}, u32[]{:S(2)}, u32[]{:S(2)}) %collective-permute-start.1) | collective-permute-done | bytes 786464 | tf_op jit(solution)/shard_map/ppermute | solution.py:494
  61.3 12.2 %collective-permute-start.5 = (bf16[256,2048]{1,0:T(8,128)(2,1)S(1)}, bf16[256,2048]{1,0:T(8,128)(2,1)S(1)}, u32[]{:S(2)}, u32[]{:S(2)}) collective-permute-start(bf16[256,2048]{1,0:T(8,128)(2,1)S(1)} %fusion.4.refs_0_), channel_id=1, source_target_pairs={{0,8},{8,0},{16,24},{24,16},{1,9},{9,1},{17,25},{25,17},{2,10},{10... | collective-permute-start | bytes 3145736 | tf_op jit(solution)/shard_map/ppermute | solution.py:497
  81.7 15.5 %collective-permute-done.5.refs_1_ = bf16[256,2048]{1,0:T(8,128)(2,1)S(1)} collective-permute-done((bf16[256,2048]{1,0:T(8,128)(2,1)S(1)}, bf16[256,2048]{1,0:T(8,128)(2,1)S(1)}, u32[]{:S(2)}, u32[]{:S(2)}) %collective-permute-start.5) | collective-permute-done | bytes 1048608 | tf_op jit(solution)/shard_map/ppermute | solution.py:497
  107.4 24.3 %collective-permute-done.10 = bf16[256,2048]{1,0:T(8,128)(2,1)S(1)} collective-permute-done((bf16[256,2048]{1,0:T(8,128)(2,1)}, bf16[256,2048]{1,0:T(8,128)(2,1)S(1)}, u32[]{:S(2)}, u32[]{:S(2)}) %collective-permute-start.10) | collective-permute-done | bytes 1048608 | tf_op jit(solution)/shard_map/ppermute | solution.py:573
  154.1 10.2 %project.4 = f32[1024,1536]{1,0:T(8,128)} custom-call(bf16[256,2048]{1,0:T(8,128)(2,1)S(1)} %fusion.4.refs_0_, bf16[256,2048]{1,0:T(8,128)(2,1)S(1)} %collective-permute-done.5.refs_1_, bf16[256,2048]{1,0:T(8,128)(2,1)S(1)} %collective-permute-done.6.refs_2_, bf16[256,2048]{1,0:T(8,128)(2,1)S(1)} %constant_dynamic-update-slice_fusion.refs_3_, ...), custom_call_target="tpu_custom_call" | custom-call | flops 1024 | bytes 1024 | tf_op jit(solution)/shard_map/project/pallas_call | solution.py:378
  164.3 21.6 %attend.1 = (bf16[4,1,2,128,512]{4,3,2,1,0:T(8,128)(2,1)}, f32[4,1,2,128,512]{4,3,2,1,0:T(8,128)}) custom-call(s32[8]{0:T(128)} %fusion.41.order, f32[4,1,2,128,1536]{4,3,2,1,0:T(8,128)} %bitcast.142, f32[1024,128]{1,0:T(8,128)} %get-tuple-element.521.cos, f32[1024,128]{1,0:T(8,128)} %get-tuple-element.522.sin), custom_call_target="tpu_custom_call" | custom-call | flops 1024 | bytes 1024 | tf_op jit(solution)/shard_map/attend/pallas_call | solution.py:153
  196.4 13.3 %collective-permute-done.17 = bf16[128,2048]{1,0:T(8,128)(2,1)S(1)} collective-permute-done((bf16[128,2048]{1,0:T(8,128)(2,1)S(1)}, bf16[128,2048]{1,0:T(8,128)(2,1)S(1)}, u32[]{:S(2)}, u32[]{:S(2)}) %collective-permute-start.17) | collective-permute-done | bytes 524320 | tf_op jit(solution)/shard_map/ppermute | solution.py:494
  226.4 19.6 %collective-permute-done.22 = bf16[256,2048]{1,0:T(8,128)(2,1)S(1)} collective-permute-done((bf16[256,2048]{1,0:T(8,128)(2,1)S(1)}, bf16[256,2048]{1,0:T(8,128)(2,1)S(1)}, u32[]{:S(2)}, u32[]{:S(2)}) %collective-permute-start.22) | collective-permute-done | bytes 1048608 | tf_op jit(solution)/shard_map/ppermute | solution.py:497
  263.9 12.6 %assemble.6 = bf16[8,256,4096]{2,1,0:T(8,128)(2,1)} custom-call(s32[8]{0:T(128)} %stack.96.places, bf16[256,4096]{1,0:T(8,128)(2,1)} %copy-done.38, bf16[256,4096]{1,0:T(8,128)(2,1)} %copy-done.55, bf16[256,4096]{1,0:T(8,128)(2,1)} %collective-permute-done.15.refs_2_, bf16[256,4096]{1,0:T(8,128)(2,1)} %collective-permute-done.29.refs_3_, ...), custom_call_target="tpu_custom_call" | custom-call | flops 1024 | bytes 1024 | tf_op jit(solution)/shard_map/assemble/pallas_call | solution.py:415
  286.0 20.3 %mlp.2 = (bf16[1024,2048]{1,0:T(8,128)(2,1)}, f32[1024,2048]{1,0:T(8,128)}, f32[1024,2048]{1,0:T(8,128)}, bf16[1024,2048]{1,0:T(8,128)(2,1)}, bf16[256,2048]{1,0...) custom-call(bf16[256,2048]{1,0:T(8,128)(2,1)S(1)} %collective-permute-done.27.refs_0_, ...), custom_call_target="tpu_custom_call" | custom-call | flops 1024 | bytes 1024 | tf_op jit(solution)/shard_map/mlp/pallas_call | solution.py:235
  306.3 12.1 %collective-permute-done.31 = bf16[128,2048]{1,0:T(8,128)(2,1)S(1)} collective-permute-done((bf16[128,2048]{1,0:T(8,128)(2,1)S(1)}, bf16[128,2048]{1,0:T(8,128)(2,1)S(1)}, u32[]{:S(2)}, u32[]{:S(2)}) %collective-permute-start.31) | collective-permute-done | bytes 524320 | tf_op jit(solution)/shard_map/ppermute | solution.py:494
  318.7 20.2 %mlp.3 = (bf16[1024,2048]{1,0:T(8,128)(2,1)}, f32[1024,2048]{1,0:T(8,128)}, f32[1024,2048]{1,0:T(8,128)}, bf16[1024,2048]{1,0:T(8,128)(2,1)}, f32[256,2048]{1,0:T(8,128)S(1)}, /*index=5*/bf16[256,2048]{1,0:T(8,128)(2,1)S(1)}) custom-call(bf16[256,2048]{1,0:T(8,128)(2,1)S(1)} %fusion.11.refs_0_, ...), custom_call_target="tpu_custom_call", output_to_operand_aliasing={{0}: (5, {}), {1}: (6, {}), {2}: (7, {}), {3}: (8, {})} | custom-call | flops 1024 | bytes 1024 | tf_op jit(solution)/shard_map/mlp/pallas_call | solution.py:235
  357.2 21.4 %collective-permute-done.36 = s32[256,1]{0,1:T(1,128)S(1)} collective-permute-done((s32[256,1]{0,1:T(1,128)S(1)}, s32[256,1]{0,1:T(1,128)S(1)}, u32[]{:S(2)}, u32[]{:S(2)}) %collective-permute-start.36) | collective-permute-done | bytes 1056 | tf_op jit(solution)/shard_map/ppermute | solution.py:512
  398.3 14.3 %collective-permute-done.41.refs_0_.refs_1_ = bf16[256,2048]{1,0:T(8,128)(2,1)S(1)} collective-permute-done((bf16[256,2048]{1,0:T(8,128)(2,1)S(1)}, bf16[256,2048]{1,0:T(8,128)(2,1)S(1)}, u32[]{:S(2)}, u32[]{:S(2)}) %collective-permute-start.41) | collective-permute-done | bytes 1048608 | tf_op jit(solution)/shard_map/ppermute | solution.py:497
  417.7 21.7 %mlp_back.2 = (bf16[1024,2048]{1,0:T(8,128)(2,1)}, bf16[1024,2048]{1,0:T(8,128)(2,1)}, bf16[1024,2048]{1,0:T(8,128)(2,1)}, bf16[256,2048]{1,0:T(8,128)(2,1)S(1)}, bf16[256,2048]{1,0:T(8,128)(2,1)S(1)}) custom-call(bf16[256,2048]{1,0:T(8,128)(2,1)S(1)} %collective-permute-done.41.refs_0_.refs_1_, ...), custom_call_target="tpu_custom_call" | custom-call | flops 1024 | bytes 1024 | tf_op jit(solution)/shard_map/mlp_back/pallas_call | solution.py:298
  451.1 21.6 %mlp_back.3 = (bf16[1024,2048]{1,0:T(8,128)(2,1)}, bf16[1024,2048]{1,0:T(8,128)(2,1)}, bf16[1024,2048]{1,0:T(8,128)(2,1)}, f32[256,2048]{1,0:T(8,128)S(1)}, bf16[256,2048]{1,0:T(8,128)(2,1)}) custom-call(bf16[256,2048]{1,0:T(8,128)(2,1)S(1)} %convert_element_type.248.refs_0_.refs_3_, ...), custom_call_target="tpu_custom_call", output_to_operand_aliasing={{0}: (7, {}), {1}: (8, {}), {2}: (9, {})} | custom-call | flops 1024 | bytes 1024 | tf_op jit(solution)/shard_map/mlp_back/pallas_call | solution.py:298
  513.7 21.8 %collective-permute-done.52 = bf16[256,2048]{1,0:T(8,128)(2,1)} collective-permute-done((bf16[256,2048]{1,0:T(8,128)(2,1)}, bf16[256,2048]{1,0:T(8,128)(2,1)}, u32[]{:S(2)}, u32[]{:S(2)}) %collective-permute-start.52) | collective-permute-done | bytes 1048608 | tf_op jit(solution)/shard_map/ppermute | solution.py:512
  606.7 27.9 %attend_back.1 = bf16[4,1,2,128,1536]{4,3,2,1,0:T(8,128)(2,1)} custom-call(s32[8]{0:T(128)} %fusion.41.order, f32[4,1,2,128,1536]{4,3,2,1,0:T(8,128)} %bitcast.143, f32[4,1,2,128,512]{4,3,2,1,0:T(8,128)} %get-tuple-element.367.lse, bf16[4,1,2,128,512]{4,3,2,1,0:T(8,128)(2,1)} %bitcast.123, f32[1024,128]{1,0:T(8,128)} %get-tuple-element.521.cos, ...), custom_call_target="tpu_custom_call" | custom-call | flops 1024 | bytes 1024 | tf_op jit(solution)/shard_map/attend_back/pallas_call | solution.py:177
  673.4 12.7 %collective-permute-done.65 = bf16[1,2,1,2,2,64,512]{6,5,4,3,2,1,0:T(8,128)(2,1)S(1)} collective-permute-done((bf16[1,2,1,2,2,64,512]{6,5,4,3,2,1,0:T(8,128)(2,1)}, bf16[1,2,1,2,2,64,512]{6,5,4,3,2,1,0:T(8,128)(2,1)S(1)}, u32[]{:S(2)}, u32[]{:S(2)}) %collective-permute-start.65) | collective-permute-done | bytes 524320 | tf_op jit(solution)/shard_map/ppermute | solution.py:497
  740.3 29.5 %collective-permute-done.70 = bf16[256,2048]{1,0:T(8,128)(2,1)} collective-permute-done((bf16[256,2048]{1,0:T(8,128)(2,1)}, bf16[256,2048]{1,0:T(8,128)(2,1)}, u32[]{:S(2)}, u32[]{:S(2)}) %collective-permute-start.70) | collective-permute-done | bytes 1048608 | tf_op jit(solution)/shard_map/ppermute | solution.py:497
  793.2 27.8 %collective-permute-done.77 = bf16[64,2048]{1,0:T(8,128)(2,1)S(1)} collective-permute-done((bf16[64,2048]{1,0:T(8,128)(2,1)S(1)}, bf16[64,2048]{1,0:T(8,128)(2,1)S(1)}, u32[]{:S(2)}, u32[]{:S(2)}) %collective-permute-start.77) | collective-permute-done | bytes 262176 | tf_op jit(solution)/shard_map/ppermute | solution.py:497
  822.5 20.9 %collective-permute-done.75 = bf16[256,2048]{1,0:T(8,128)(2,1)S(1)} collective-permute-done((bf16[256,2048]{1,0:T(8,128)(2,1)S(1)}, bf16[256,2048]{1,0:T(8,128)(2,1)S(1)}, u32[]{:S(2)}, u32[]{:S(2)}) %collective-permute-start.75) | collective-permute-done | bytes 1048608 | tf_op jit(solution)/shard_map/ppermute | solution.py:512
  856.1 19.7 %collective-permute-done.84 = bf16[64,2048]{1,0:T(8,128)(2,1)S(1)} collective-permute-done((bf16[64,2048]{1,0:T(8,128)(2,1)S(1)}, bf16[64,2048]{1,0:T(8,128)(2,1)S(1)}, u32[]{:S(2)}, u32[]{:S(2)}) %collective-permute-start.84) | collective-permute-done | bytes 262176 | tf_op jit(solution)/shard_map/ppermute | solution.py:512
  876.3 15.6 %collective-permute-done.83 = bf16[1,2,1,2,2,64,768]{6,5,4,3,2,1,0:T(8,128)(2,1)S(1)} collective-permute-done((bf16[1,2,1,2,2,64,768]{6,5,4,3,2,1,0:T(8,128)(2,1)S(1)}, bf16[1,2,1,2,2,64,768]{6,5,4,3,2,1,0:T(8,128)(2,1)S(1)}, u32[]{:S(2)}, u32[]{:S(2)}) %collective-permute-start.83) | collective-permute-done | bytes 786464 | tf_op jit(solution)/shard_map/ppermute | solution.py:497
  (520 shorter events, 473.3 us)
Async XLA Ops:
  4.9 42.1 %collective-permute-start.1 = (bf16[256,1536]{1,0:T(8,128)(2,1)}, bf16[256,1536]{1,0:T(8,128)(2,1)}, u32[]{:S(2)}, u32[]{:S(2)}) collective-permute-start(bf16[256,1536]{1,0:T(8,128)(2,1)} %pad_maximum_fusion.12), channel_id=1, source_target_pairs={{0,2},{1,3},{2,0},{3,1},{4,6},{5,7},{6,4},{7,5},{8,10},{9,11},{10,... | collective-permute-start | bytes 2359304 | tf_op jit(solution)/shard_map/ppermute | solution.py:494
  6.4 46.8 %collective-permute-start = (bf16[256,2048]{1,0:T(8,128)(2,1)S(1)}, bf16[256,2048]{1,0:T(8,128)(2,1)S(1)}, u32[]{:S(2)}, u32[]{:S(2)}) collective-permute-start(bf16[256,2048]{1,0:T(8,128)(2,1)S(1)} %bitcast.162), channel_id=1, source_target_pairs={{2,16},{3,17},{6,20},{7,21},{10,24},{11,25},{14,28},{15,29},{16,2}... | collective-permute-start | bytes 3145736 | tf_op jit(solution)/shard_map/ppermute | solution.py:512
  13.8 42.5 %collective-permute-start.2 = (bf16[256,2048]{1,0:T(8,128)(2,1)}, bf16[256,2048]{1,0:T(8,128)(2,1)}, u32[]{:S(2)}, u32[]{:S(2)}) collective-permute-start(bf16[256,2048]{1,0:T(8,128)(2,1)} %get-tuple-element.261), channel_id=1, source_target_pairs={{0,4},{1,5},{2,6},{3,7},{4,0},{5,1},{6,2},{7,3},{8,12},{9,13},{10,... | collective-permute-start | bytes 3145736 | tf_op jit(solution)/shard_map/ppermute | solution.py:494
  20.6 40.7 %collective-permute-start.3 = (bf16[256,2048]{1,0:T(8,128)(2,1)}, bf16[256,2048]{1,0:T(8,128)(2,1)}, u32[]{:S(2)}, u32[]{:S(2)}) collective-permute-start(bf16[256,2048]{1,0:T(8,128)(2,1)} %get-tuple-element.262), channel_id=1, source_target_pairs={{0,4},{1,5},{2,6},{3,7},{4,0},{5,1},{6,2},{7,3},{8,12},{9,13},{10,... | collective-permute-start | bytes 3145736 | tf_op jit(solution)/shard_map/ppermute | solution.py:494
  74.6 58.4 %collective-permute-start.12 = (bf16[512,1536]{1,0:T(8,128)(2,1)}, bf16[512,1536]{1,0:T(8,128)(2,1)S(1)}, u32[]{:S(2)}, u32[]{:S(2)}) collective-permute-start(bf16[512,1536]{1,0:T(8,128)(2,1)} %pad_maximum_fusion.5.refs_0_), channel_id=1, source_target_pairs={{0,4},{1,5},{2,6},{3,7},{4,0},{5,1},{6,2},{7,3},{8,12},{9,13},{10,... | collective-permute-start | bytes 4718600 | tf_op jit(solution)/shard_map/ppermute | solution.py:494
  74.6 57.0 %collective-permute-start.10 = (bf16[256,2048]{1,0:T(8,128)(2,1)}, bf16[256,2048]{1,0:T(8,128)(2,1)S(1)}, u32[]{:S(2)}, u32[]{:S(2)}) collective-permute-start(bf16[256,2048]{1,0:T(8,128)(2,1)} %broadcast_select_fusion.2), channel_id=1, source_target_pairs={{0,4},{1,5},{6,2},{7,3},{8,12},{9,13},{14,10},{15,11},{16,20},{17,... | collective-permute-start | bytes 3145736 | tf_op jit(solution)/shard_map/ppermute | solution.py:573
  137.0 54.9 %collective-permute-start.16 = (bf16[512,2048]{1,0:T(8,128)(2,1)}, bf16[512,2048]{1,0:T(8,128)(2,1)}, u32[]{:S(2)}, u32[]{:S(2)}) collective-permute-start(bf16[512,2048]{1,0:T(8,128)(2,1)} %constant_dynamic-update-slice_fusion.2.refs_0_), channel_id=1, source_target_pairs={{0,4},{1,5},{2,6},{3,7},{4,0},{5,1},{6,2},{7,3},{8,12},{9,13},{10,... | collective-permute-start | bytes 6291464 | tf_op jit(solution)/shard_map/ppermute | solution.py:494
  138.0 54.0 %collective-permute-start.15 = (bf16[256,4096]{1,0:T(8,128)(2,1)}, bf16[256,4096]{1,0:T(8,128)(2,1)}, u32[]{:S(2)}, u32[]{:S(2)}) collective-permute-start(bf16[256,4096]{1,0:T(8,128)(2,1)} %pad_maximum_fusion), channel_id=1, source_target_pairs={{0,2},{1,3},{2,0},{3,1},{4,6},{5,7},{6,4},{7,5},{8,10},{9,11},{10,... | collective-permute-start | bytes 6291464 | tf_op jit(solution)/shard_map/ppermute | solution.py:494
  279.8 59.1 %collective-permute-start.35 = (bf16[256,2048]{1,0:T(8,128)(2,1)S(1)}, bf16[256,2048]{1,0:T(8,128)(2,1)S(1)}, u32[]{:S(2)}, u32[]{:S(2)}) collective-permute-start(bf16[256,2048]{1,0:T(8,128)(2,1)S(1)} %bitcast.163), channel_id=1, source_target_pairs={{2,16},{3,17},{6,20},{7,21},{10,24},{11,25},{14,28},{15,29},{16,2}... | collective-permute-start | bytes 3145736 | tf_op jit(solution)/shard_map/ppermute | solution.py:512
  486.2 49.4 %collective-permute-start.52 = (bf16[256,2048]{1,0:T(8,128)(2,1)}, bf16[256,2048]{1,0:T(8,128)(2,1)}, u32[]{:S(2)}, u32[]{:S(2)}) collective-permute-start(bf16[256,2048]{1,0:T(8,128)(2,1)} %convert_element_type.249), channel_id=1, source_target_pairs={{2,16},{3,17},{6,20},{7,21},{10,24},{11,25},{14,28},{15,29},{16,2}... | collective-permute-start | bytes 3145736 | tf_op jit(solution)/shard_map/ppermute | solution.py:512
  493.9 47.1 %collective-permute-start.51 = (bf16[2,1,256,2048]{3,2,1,0:T(8,128)(2,1)}, bf16[2,1,256,2048]{3,2,1,0:T(8,128)(2,1)S(1)}, u32[]{:S(2)}, u32[]{:S(2)}) collective-permute-start(bf16[2,1,256,2048]{3,2,1,0:T(8,128)(2,1)} %constant_dynamic-slice_fusion.12), channel_id=1, source_target_pairs={{0,4},{1,5},{2,6},{3,7},{4,0},{5,1},{6,2},{7,3},{8,12},{9,13},{10,... | collective-permute-start | bytes 6291464 | tf_op jit(solution)/shard_map/ppermute | solution.py:494
  576.9 74.5 %collective-permute-start.59 = (bf16[2,2,1,2,2,64,1024]{6,5,4,3,2,1,0:T(8,128)(2,1)}, bf16[2,2,1,2,2,64,1024]{6,5,4,3,2,1,0:T(8,128)(2,1)}, u32[]{:S(2)}, u32[]{:S(2)}) collective-permute-start(bf16[2,2,1,2,2,64,1024]{6,5,4,3,2,1,0:T(8,128)(2,1)} %constant_dynamic-slice_fusion.11), channel_id=1, source_target_pairs={{0,4},{1,5},{2,6},{3,7},{4,0},{5,1},{6,2},{7,3},{8,12},{9,13},{10,... | collective-permute-start | bytes 6291464 | tf_op jit(solution)/shard_map/ppermute | solution.py:494
  592.4 53.7 %collective-permute-start.61 = (bf16[2,2,1,2,2,64,512]{6,5,4,3,2,1,0:T(8,128)(2,1)}, bf16[2,2,1,2,2,64,512]{6,5,4,3,2,1,0:T(8,128)(2,1)}, u32[]{:S(2)}, u32[]{:S(2)}) collective-permute-start(bf16[2,2,1,2,2,64,512]{6,5,4,3,2,1,0:T(8,128)(2,1)} %constant_dynamic-slice_fusion.9), channel_id=1, source_target_pairs={{0,4},{1,5},{2,6},{3,7},{4,0},{5,1},{6,2},{7,3},{8,12},{9,13},{10,... | collective-permute-start | bytes 3145736 | tf_op jit(solution)/shard_map/ppermute | solution.py:494
  595.1 53.8 %collective-permute-start.60 = (bf16[1,1,256,2048]{3,2,1,0:T(8,128)(2,1)}, bf16[1,1,256,2048]{3,2,1,0:T(8,128)(2,1)}, u32[]{:S(2)}, u32[]{:S(2)}) collective-permute-start(bf16[1,1,256,2048]{3,2,1,0:T(8,128)(2,1)} %constant_dynamic-slice_fusion.10), channel_id=1, source_target_pairs={{0,16},{8,24},{16,0},{24,8},{1,17},{9,25},{17,1},{25,9},{2,18},{10... | collective-permute-start | bytes 3145736 | tf_op jit(solution)/shard_map/ppermute | solution.py:497
  721.0 48.8 %collective-permute-start.70 = (bf16[256,2048]{1,0:T(8,128)(2,1)}, bf16[256,2048]{1,0:T(8,128)(2,1)}, u32[]{:S(2)}, u32[]{:S(2)}) collective-permute-start(bf16[256,2048]{1,0:T(8,128)(2,1)} %pad_maximum_fusion.9), channel_id=1, source_target_pairs={{0,8},{8,0},{16,24},{24,16},{1,9},{9,1},{17,25},{25,17},{2,10},{10... | collective-permute-start | bytes 3145736 | tf_op jit(solution)/shard_map/ppermute | solution.py:497
  724.7 45.1 %collective-permute-start.71 = (bf16[256,2048]{1,0:T(8,128)(2,1)}, bf16[256,2048]{1,0:T(8,128)(2,1)}, u32[]{:S(2)}, u32[]{:S(2)}) collective-permute-start(bf16[256,2048]{1,0:T(8,128)(2,1)} %pad_maximum_fusion.10), channel_id=1, source_target_pairs={{0,2},{1,3},{2,0},{3,1},{4,6},{5,7},{6,4},{7,5},{8,10},{9,11},{10,... | collective-permute-start | bytes 3145736 | tf_op jit(solution)/shard_map/ppermute | solution.py:494
  733.3 40.4 %collective-permute-start.73 = (bf16[1,2,1,2,2,64,1024]{6,5,4,3,2,1,0:T(8,128)(2,1)}, bf16[1,2,1,2,2,64,1024]{6,5,4,3,2,1,0:T(8,128)(2,1)S(1)}, u32[]{:S(2)}, u32[]{:S(2)}) collective-permute-start(bf16[1,2,1,2,2,64,1024]{6,5,4,3,2,1,0:T(8,128)(2,1)} %get-tuple-element.419), channel_id=1, source_target_pairs={{0,16},{8,24},{16,0},{24,8},{1,17},{9,25},{17,1},{25,9},{2,18},{10... | collective-permute-start | bytes 3145736 | tf_op jit(solution)/shard_map/ppermute | solution.py:497
  778.2 42.9 %collective-permute-start.78 = (bf16[2,2,64,1024]{3,2,1,0:T(8,128)(2,1)S(1)}, bf16[2,2,64,1024]{3,2,1,0:T(8,128)(2,1)S(1)}, u32[]{:S(2)}, u32[]{:S(2)}) collective-permute-start(bf16[2,2,64,1024]{3,2,1,0:T(8,128)(2,1)S(1)} %dynamic-slice_bitcast_fusion.1), channel_id=1, source_target_pairs={{0,1},{1,0},{2,3},{3,2},{4,5},{5,4},{6,7},{7,6},{8,9},{9,8},{10,11... | collective-permute-start | bytes 1572872 | tf_op jit(solution)/shard_map/ppermute | solution.py:494
  786.8 57.4 %collective-permute-start.76 = (bf16[2,2,1,2,2,64,768]{6,5,4,3,2,1,0:T(8,128)(2,1)S(1)}, bf16[2,2,1,2,2,64,768]{6,5,4,3,2,1,0:T(8,128)(2,1)S(1)}, u32[]{:S(2)}, u32[]{:S(2)}) collective-permute-start(bf16[2,2,1,2,2,64,768]{6,5,4,3,2,1,0:T(8,128)(2,1)S(1)} %constant_dynamic-slice_fusion.2), channel_id=1, source_target_pairs={{0,4},{1,5},{2,6},{3,7},{4,0},{5,1},{6,2},{7,3},{8,12},{9,13},{10,... | collective-permute-start | bytes 4718600 | tf_op jit(solution)/shard_map/ppermute | solution.py:494
  788.3 55.1 %collective-permute-start.75 = (bf16[256,2048]{1,0:T(8,128)(2,1)S(1)}, bf16[256,2048]{1,0:T(8,128)(2,1)S(1)}, u32[]{:S(2)}, u32[]{:S(2)}) collective-permute-start(bf16[256,2048]{1,0:T(8,128)(2,1)S(1)} %fusion.9), channel_id=1, source_target_pairs={{2,16},{3,17},{6,20},{7,21},{10,24},{11,25},{14,28},{15,29},{16,2}... | collective-permute-start | bytes 3145736 | tf_op jit(solution)/shard_map/ppermute | solution.py:512
  846.6 45.3 %collective-permute-start.83 = (bf16[1,2,1,2,2,64,768]{6,5,4,3,2,1,0:T(8,128)(2,1)S(1)}, bf16[1,2,1,2,2,64,768]{6,5,4,3,2,1,0:T(8,128)(2,1)S(1)}, u32[]{:S(2)}, u32[]{:S(2)}) collective-permute-start(bf16[1,2,1,2,2,64,768]{6,5,4,3,2,1,0:T(8,128)(2,1)S(1)} %constant_dynamic-slice_fusion), channel_id=1, source_target_pairs={{0,16},{8,24},{16,0},{24,8},{1,17},{9,25},{17,1},{25,9},{2,18},{10... | collective-permute-start | bytes 2359304 | tf_op jit(solution)/shard_map/ppermute | solution.py:497
  846.7 45.4 %collective-permute-start.80 = (bf16[64,4096]{1,0:T(8,128)(2,1)S(1)}, bf16[64,4096]{1,0:T(8,128)(2,1)S(1)}, u32[]{:S(2)}, u32[]{:S(2)}) collective-permute-start(bf16[64,4096]{1,0:T(8,128)(2,1)S(1)} %pad_maximum_fusion.16), channel_id=1, source_target_pairs={{0,8},{8,0},{16,24},{24,16},{1,9},{9,1},{17,25},{25,17},{2,10},{10... | collective-permute-start | bytes 1572872 | tf_op jit(solution)/shard_map/ppermute | solution.py:497
  850.2 42.0 %collective-permute-start.81 = (bf16[64,4096]{1,0:T(8,128)(2,1)S(1)}, bf16[64,4096]{1,0:T(8,128)(2,1)S(1)}, u32[]{:S(2)}, u32[]{:S(2)}) collective-permute-start(bf16[64,4096]{1,0:T(8,128)(2,1)S(1)} %pad_maximum_fusion.17), channel_id=1, source_target_pairs={{0,2},{1,3},{2,0},{3,1},{4,6},{5,7},{6,4},{7,5},{8,10},{9,11},{10,... | collective-permute-start | bytes 1572872 | tf_op jit(solution)/shard_map/ppermute | solution.py:494
  854.5 40.2 %collective-permute-start.82 = (bf16[64,4096]{1,0:T(8,128)(2,1)S(1)}, bf16[64,4096]{1,0:T(8,128)(2,1)S(1)}, u32[]{:S(2)}, u32[]{:S(2)}) collective-permute-start(bf16[64,4096]{1,0:T(8,128)(2,1)S(1)} %pad_maximum_fusion.18), channel_id=1, source_target_pairs={{0,10},{1,11},{2,8},{3,9},{4,14},{5,15},{6,12},{7,13},{8,2},{9,3},... | collective-permute-start | bytes 1572872 | tf_op jit(solution)/shard_map/ppermute | solution.py:505
  (154 other events, 2656.3 us)

commit v7 on v5

--- a/solution.py
+++ b/solution.py
@@ -870,7 +870,7 @@
     factor = (rows * world) / count
     grad_input = grad_low.astype(F32) * factor
     ff_order = lambda v: v.reshape(planes, unit, shards, -1).transpose(1, 2, 0, 3).reshape(unit, ff)
-    placed = columns_placed(pieces)
+    placed, qkv_pieces = region(columns_placed(pieces), qkv_pieces)
     g_gate = ff_order(placed[:, :, :part_ff]).astype(F32)
     g_up = ff_order(placed[:, :, part_ff:]).astype(F32)
     g_qkv = columns_placed(qkv_pieces).reshape(planes, unit, 3, mine).transpose(2, 1, 0, 3)

time: 943 us -> 945 us (level)
  transfers between devices with their start and end apart: 89 -> 89, of which waited for: 46 -> 46; matrix products, arithmetic and copies ran while one was open for 10% -> 10% of each run, Pallas kernels for 27% -> 28%
where the time goes in v7:
time: 945 us; the launch traced here: 937 us
  waiting for transfers between devices  379 us (40%)
  Pallas kernels  270 us (29%)
  starting transfers between devices  132 us (14%)
  other arithmetic  85.1 us (9%)
  local copies, waits for them, and re-layouts  65.3 us (7%)
    ppermute x25, waiting for transfers between devices, flip_ctx(): return lax.ppermute(array, 'ctx', [(i, i ^ bits) for i in range(planes)])  156 us
    ppermute x51, waiting for transfers between devices, flip(): return lax.ppermute(array, 'fsdp', [(i, i ^ bits) for i in range(shards)])  107 us
    ppermute x7, waiting for transfers between devices, send(): lax.ppermute(array, both, [(i, to) for i, to in enumerate(homes) if i !=...  88.8 us
    pallas_call x10, Pallas kernels, outer(): pl.pallas_call(kernel, grid_spec=pltpu.PrefetchScalarGridSpec(num_scalar_...  66.2 us
    ppermute x25, starting transfers between devices, flip_ctx(): return lax.ppermute(array, 'ctx', [(i, i ^ bits) for i in range(planes)])  52.6 us
    pallas_call x2, Pallas kernels, mlp_back(): pl.pallas_call(functools.partial(down_kernel, count), grid=(tiles,), in_s...  43.3 us
    pallas_call x2, Pallas kernels, mlp(): pl.pallas_call(functools.partial(up_kernel, count), grid=(tiles,), in_spe...  40.6 us
    ppermute x51, starting transfers between devices, flip(): return lax.ppermute(array, 'fsdp', [(i, i ^ bits) for i in range(shards)])  40.2 us
  transfers between devices with their start and end apart: 89, of which 46 were waited for; matrix products, arithmetic and copies ran while one was open for 10% of the time, Pallas kernels for 28%

profile of v7, /device:TPU:16, one launch (start us, length us, event | category | flops | bytes accessed | tf_op | source)
XLA Modules:
  0.0 937.0 jit_solution(4579599664732836218)
XLA Ops:
  23.3 23.7 %collective-permute-done.1 = bf16[256,1536]{1,0:T(8,128)(2,1)} collective-permute-done((bf16[256,1536]{1,0:T(8,128)(2,1)}, bf16[256,1536]{1,0:T(8,128)(2,1)}, u32[]{:S(2)}, u32[]{:S(2)}) %collective-permute-start.1) | collective-permute-done | bytes 786464 | tf_op jit(solution)/shard_map/ppermute | solution.py:494
  61.3 12.2 %collective-permute-start.5 = (bf16[256,2048]{1,0:T(8,128)(2,1)S(1)}, bf16[256,2048]{1,0:T(8,128)(2,1)S(1)}, u32[]{:S(2)}, u32[]{:S(2)}) collective-permute-start(bf16[256,2048]{1,0:T(8,128)(2,1)S(1)} %fusion.4.refs_0_), channel_id=1, source_target_pairs={{0,8},{8,0},{16,24},{24,16},{1,9},{9,1},{17,25},{25,17},{2,10},{10... | collective-permute-start | bytes 3145736 | tf_op jit(solution)/shard_map/ppermute | solution.py:497
  81.7 15.5 %collective-permute-done.5.refs_1_ = bf16[256,2048]{1,0:T(8,128)(2,1)S(1)} collective-permute-done((bf16[256,2048]{1,0:T(8,128)(2,1)S(1)}, bf16[256,2048]{1,0:T(8,128)(2,1)S(1)}, u32[]{:S(2)}, u32[]{:S(2)}) %collective-permute-start.5) | collective-permute-done | bytes 1048608 | tf_op jit(solution)/shard_map/ppermute | solution.py:497
  107.3 24.3 %collective-permute-done.10 = bf16[256,2048]{1,0:T(8,128)(2,1)S(1)} collective-permute-done((bf16[256,2048]{1,0:T(8,128)(2,1)}, bf16[256,2048]{1,0:T(8,128)(2,1)S(1)}, u32[]{:S(2)}, u32[]{:S(2)}) %collective-permute-start.10) | collective-permute-done | bytes 1048608 | tf_op jit(solution)/shard_map/ppermute | solution.py:573
  154.2 10.1 %project.4 = f32[1024,1536]{1,0:T(8,128)} custom-call(bf16[256,2048]{1,0:T(8,128)(2,1)S(1)} %fusion.4.refs_0_, bf16[256,2048]{1,0:T(8,128)(2,1)S(1)} %collective-permute-done.5.refs_1_, bf16[256,2048]{1,0:T(8,128)(2,1)S(1)} %collective-permute-done.6.refs_2_, bf16[256,2048]{1,0:T(8,128)(2,1)S(1)} %constant_dynamic-update-slice_fusion.refs_3_, ...), custom_call_target="tpu_custom_call" | custom-call | flops 1024 | bytes 1024 | tf_op jit(solution)/shard_map/project/pallas_call | solution.py:378
  164.3 21.5 %attend.1 = (bf16[4,1,2,128,512]{4,3,2,1,0:T(8,128)(2,1)}, f32[4,1,2,128,512]{4,3,2,1,0:T(8,128)}) custom-call(s32[8]{0:T(128)} %fusion.41.order, f32[4,1,2,128,1536]{4,3,2,1,0:T(8,128)} %bitcast.142, f32[1024,128]{1,0:T(8,128)} %get-tuple-element.527.cos, f32[1024,128]{1,0:T(8,128)} %get-tuple-element.528.sin), custom_call_target="tpu_custom_call" | custom-call | flops 1024 | bytes 1024 | tf_op jit(solution)/shard_map/attend/pallas_call | solution.py:153
  196.4 13.3 %collective-permute-done.17 = bf16[128,2048]{1,0:T(8,128)(2,1)S(1)} collective-permute-done((bf16[128,2048]{1,0:T(8,128)(2,1)S(1)}, bf16[128,2048]{1,0:T(8,128)(2,1)S(1)}, u32[]{:S(2)}, u32[]{:S(2)}) %collective-permute-start.17) | collective-permute-done | bytes 524320 | tf_op jit(solution)/shard_map/ppermute | solution.py:494
  226.5 19.7 %collective-permute-done.22 = bf16[256,2048]{1,0:T(8,128)(2,1)S(1)} collective-permute-done((bf16[256,2048]{1,0:T(8,128)(2,1)S(1)}, bf16[256,2048]{1,0:T(8,128)(2,1)S(1)}, u32[]{:S(2)}, u32[]{:S(2)}) %collective-permute-start.22) | collective-permute-done | bytes 1048608 | tf_op jit(solution)/shard_map/ppermute | solution.py:497
  264.0 12.6 %assemble.6 = bf16[8,256,4096]{2,1,0:T(8,128)(2,1)} custom-call(s32[8]{0:T(128)} %stack.96.places, bf16[256,4096]{1,0:T(8,128)(2,1)} %copy-done.40, bf16[256,4096]{1,0:T(8,128)(2,1)} %copy-done.55, bf16[256,4096]{1,0:T(8,128)(2,1)} %collective-permute-done.15.refs_2_, bf16[256,4096]{1,0:T(8,128)(2,1)} %collective-permute-done.29.refs_3_, ...), custom_call_target="tpu_custom_call" | custom-call | flops 1024 | bytes 1024 | tf_op jit(solution)/shard_map/assemble/pallas_call | solution.py:415
  286.0 20.4 %mlp.2 = (bf16[1024,2048]{1,0:T(8,128)(2,1)}, f32[1024,2048]{1,0:T(8,128)}, f32[1024,2048]{1,0:T(8,128)}, bf16[1024,2048]{1,0:T(8,128)(2,1)}, bf16[256,2048]{1,0...) custom-call(bf16[256,2048]{1,0:T(8,128)(2,1)S(1)} %collective-permute-done.27.refs_0_, ...), custom_call_target="tpu_custom_call" | custom-call | flops 1024 | bytes 1024 | tf_op jit(solution)/shard_map/mlp/pallas_call | solution.py:235
  306.4 12.1 %collective-permute-done.31 = bf16[128,2048]{1,0:T(8,128)(2,1)S(1)} collective-permute-done((bf16[128,2048]{1,0:T(8,128)(2,1)S(1)}, bf16[128,2048]{1,0:T(8,128)(2,1)S(1)}, u32[]{:S(2)}, u32[]{:S(2)}) %collective-permute-start.31) | collective-permute-done | bytes 524320 | tf_op jit(solution)/shard_map/ppermute | solution.py:494
  318.7 20.2 %mlp.3 = (bf16[1024,2048]{1,0:T(8,128)(2,1)}, f32[1024,2048]{1,0:T(8,128)}, f32[1024,2048]{1,0:T(8,128)}, bf16[1024,2048]{1,0:T(8,128)(2,1)}, f32[256,2048]{1,0:T(8,128)S(1)}, /*index=5*/bf16[256,2048]{1,0:T(8,128)(2,1)S(1)}) custom-call(bf16[256,2048]{1,0:T(8,128)(2,1)S(1)} %fusion.11.refs_0_, ...), custom_call_target="tpu_custom_call", output_to_operand_aliasing={{0}: (5, {}), {1}: (6, {}), {2}: (7, {}), {3}: (8, {})} | custom-call | flops 1024 | bytes 1024 | tf_op jit(solution)/shard_map/mlp/pallas_call | solution.py:235
  357.3 21.4 %collective-permute-done.36 = s32[256,1]{0,1:T(1,128)S(1)} collective-permute-done((s32[256,1]{0,1:T(1,128)S(1)}, s32[256,1]{0,1:T(1,128)S(1)}, u32[]{:S(2)}, u32[]{:S(2)}) %collective-permute-start.36) | collective-permute-done | bytes 1056 | tf_op jit(solution)/shard_map/ppermute | solution.py:512
  398.4 14.3 %collective-permute-done.41.refs_0_.refs_1_ = bf16[256,2048]{1,0:T(8,128)(2,1)S(1)} collective-permute-done((bf16[256,2048]{1,0:T(8,128)(2,1)S(1)}, bf16[256,2048]{1,0:T(8,128)(2,1)S(1)}, u32[]{:S(2)}, u32[]{:S(2)}) %collective-permute-start.41) | collective-permute-done | bytes 1048608 | tf_op jit(solution)/shard_map/ppermute | solution.py:497
  417.7 21.7 %mlp_back.2 = (bf16[1024,2048]{1,0:T(8,128)(2,1)}, bf16[1024,2048]{1,0:T(8,128)(2,1)}, bf16[1024,2048]{1,0:T(8,128)(2,1)}, bf16[256,2048]{1,0:T(8,128)(2,1)S(1)}, bf16[256,2048]{1,0:T(8,128)(2,1)S(1)}) custom-call(bf16[256,2048]{1,0:T(8,128)(2,1)S(1)} %collective-permute-done.41.refs_0_.refs_1_, ...), custom_call_target="tpu_custom_call" | custom-call | flops 1024 | bytes 1024 | tf_op jit(solution)/shard_map/mlp_back/pallas_call | solution.py:298
  451.1 21.6 %mlp_back.3 = (bf16[1024,2048]{1,0:T(8,128)(2,1)}, bf16[1024,2048]{1,0:T(8,128)(2,1)}, bf16[1024,2048]{1,0:T(8,128)(2,1)}, f32[256,2048]{1,0:T(8,128)S(1)}, bf16[256,2048]{1,0:T(8,128)(2,1)}) custom-call(bf16[256,2048]{1,0:T(8,128)(2,1)S(1)} %convert_element_type.248.refs_0_.refs_3_, ...), custom_call_target="tpu_custom_call", output_to_operand_aliasing={{0}: (7, {}), {1}: (8, {}), {2}: (9, {})} | custom-call | flops 1024 | bytes 1024 | tf_op jit(solution)/shard_map/mlp_back/pallas_call | solution.py:298
  513.5 22.1 %collective-permute-done.52 = bf16[256,2048]{1,0:T(8,128)(2,1)} collective-permute-done((bf16[256,2048]{1,0:T(8,128)(2,1)}, bf16[256,2048]{1,0:T(8,128)(2,1)}, u32[]{:S(2)}, u32[]{:S(2)}) %collective-permute-start.52) | collective-permute-done | bytes 1048608 | tf_op jit(solution)/shard_map/ppermute | solution.py:512
  607.5 27.9 %attend_back.1 = bf16[4,1,2,128,1536]{4,3,2,1,0:T(8,128)(2,1)} custom-call(s32[8]{0:T(128)} %fusion.41.order, f32[4,1,2,128,1536]{4,3,2,1,0:T(8,128)} %bitcast.143, f32[4,1,2,128,512]{4,3,2,1,0:T(8,128)} %get-tuple-element.371.lse, bf16[4,1,2,128,512]{4,3,2,1,0:T(8,128)(2,1)} %bitcast.123, f32[1024,128]{1,0:T(8,128)} %get-tuple-element.527.cos, ...), custom_call_target="tpu_custom_call" | custom-call | flops 1024 | bytes 1024 | tf_op jit(solution)/shard_map/attend_back/pallas_call | solution.py:177
  670.6 12.9 %collective-permute-done.65 = bf16[1,2,1,2,2,64,512]{6,5,4,3,2,1,0:T(8,128)(2,1)S(1)} collective-permute-done((bf16[1,2,1,2,2,64,512]{6,5,4,3,2,1,0:T(8,128)(2,1)}, bf16[1,2,1,2,2,64,512]{6,5,4,3,2,1,0:T(8,128)(2,1)S(1)}, u32[]{:S(2)}, u32[]{:S(2)}) %collective-permute-start.65) | collective-permute-done | bytes 524320 | tf_op jit(solution)/shard_map/ppermute | solution.py:497
  738.4 27.4 %collective-permute-done.70 = bf16[256,2048]{1,0:T(8,128)(2,1)} collective-permute-done((bf16[256,2048]{1,0:T(8,128)(2,1)}, bf16[256,2048]{1,0:T(8,128)(2,1)}, u32[]{:S(2)}, u32[]{:S(2)}) %collective-permute-start.70) | collective-permute-done | bytes 1048608 | tf_op jit(solution)/shard_map/ppermute | solution.py:497
  789.0 29.5 %collective-permute-done.77 = bf16[64,2048]{1,0:T(8,128)(2,1)S(1)} collective-permute-done((bf16[64,2048]{1,0:T(8,128)(2,1)S(1)}, bf16[64,2048]{1,0:T(8,128)(2,1)S(1)}, u32[]{:S(2)}, u32[]{:S(2)}) %collective-permute-start.77) | collective-permute-done | bytes 262176 | tf_op jit(solution)/shard_map/ppermute | solution.py:497
  819.9 21.0 %collective-permute-done.75 = bf16[256,2048]{1,0:T(8,128)(2,1)S(1)} collective-permute-done((bf16[256,2048]{1,0:T(8,128)(2,1)S(1)}, bf16[256,2048]{1,0:T(8,128)(2,1)S(1)}, u32[]{:S(2)}, u32[]{:S(2)}) %collective-permute-start.75) | collective-permute-done | bytes 1048608 | tf_op jit(solution)/shard_map/ppermute | solution.py:512
  852.6 20.6 %collective-permute-done.84 = bf16[64,2048]{1,0:T(8,128)(2,1)S(1)} collective-permute-done((bf16[64,2048]{1,0:T(8,128)(2,1)S(1)}, bf16[64,2048]{1,0:T(8,128)(2,1)S(1)}, u32[]{:S(2)}, u32[]{:S(2)}) %collective-permute-start.84) | collective-permute-done | bytes 262176 | tf_op jit(solution)/shard_map/ppermute | solution.py:512
  873.9 15.5 %collective-permute-done.83 = bf16[1,2,1,2,2,64,768]{6,5,4,3,2,1,0:T(8,128)(2,1)S(1)} collective-permute-done((bf16[1,2,1,2,2,64,768]{6,5,4,3,2,1,0:T(8,128)(2,1)S(1)}, bf16[1,2,1,2,2,64,768]{6,5,4,3,2,1,0:T(8,128)(2,1)S(1)}, u32[]{:S(2)}, u32[]{:S(2)}) %collective-permute-start.83) | collective-permute-done | bytes 786464 | tf_op jit(solution)/shard_map/ppermute | solution.py:497
  (523 shorter events, 469.6 us)
Async XLA Ops:
  4.9 42.1 %collective-permute-start.1 = (bf16[256,1536]{1,0:T(8,128)(2,1)}, bf16[256,1536]{1,0:T(8,128)(2,1)}, u32[]{:S(2)}, u32[]{:S(2)}) collective-permute-start(bf16[256,1536]{1,0:T(8,128)(2,1)} %pad_maximum_fusion.13), channel_id=1, source_target_pairs={{0,2},{1,3},{2,0},{3,1},{4,6},{5,7},{6,4},{7,5},{8,10},{9,11},{10,... | collective-permute-start | bytes 2359304 | tf_op jit(solution)/shard_map/ppermute | solution.py:494
  6.4 46.8 %collective-permute-start = (bf16[256,2048]{1,0:T(8,128)(2,1)S(1)}, bf16[256,2048]{1,0:T(8,128)(2,1)S(1)}, u32[]{:S(2)}, u32[]{:S(2)}) collective-permute-start(bf16[256,2048]{1,0:T(8,128)(2,1)S(1)} %bitcast.162), channel_id=1, source_target_pairs={{2,16},{3,17},{6,20},{7,21},{10,24},{11,25},{14,28},{15,29},{16,2}... | collective-permute-start | bytes 3145736 | tf_op jit(solution)/shard_map/ppermute | solution.py:512
  13.9 42.5 %collective-permute-start.2 = (bf16[256,2048]{1,0:T(8,128)(2,1)}, bf16[256,2048]{1,0:T(8,128)(2,1)}, u32[]{:S(2)}, u32[]{:S(2)}) collective-permute-start(bf16[256,2048]{1,0:T(8,128)(2,1)} %get-tuple-element.265), channel_id=1, source_target_pairs={{0,4},{1,5},{2,6},{3,7},{4,0},{5,1},{6,2},{7,3},{8,12},{9,13},{10,... | collective-permute-start | bytes 3145736 | tf_op jit(solution)/shard_map/ppermute | solution.py:494
  20.6 40.7 %collective-permute-start.3 = (bf16[256,2048]{1,0:T(8,128)(2,1)}, bf16[256,2048]{1,0:T(8,128)(2,1)}, u32[]{:S(2)}, u32[]{:S(2)}) collective-permute-start(bf16[256,2048]{1,0:T(8,128)(2,1)} %get-tuple-element.266), channel_id=1, source_target_pairs={{0,4},{1,5},{2,6},{3,7},{4,0},{5,1},{6,2},{7,3},{8,12},{9,13},{10,... | collective-permute-start | bytes 3145736 | tf_op jit(solution)/shard_map/ppermute | solution.py:494
  74.6 58.4 %collective-permute-start.12 = (bf16[512,1536]{1,0:T(8,128)(2,1)}, bf16[512,1536]{1,0:T(8,128)(2,1)S(1)}, u32[]{:S(2)}, u32[]{:S(2)}) collective-permute-start(bf16[512,1536]{1,0:T(8,128)(2,1)} %pad_maximum_fusion.6.refs_0_), channel_id=1, source_target_pairs={{0,4},{1,5},{2,6},{3,7},{4,0},{5,1},{6,2},{7,3},{8,12},{9,13},{10,... | collective-permute-start | bytes 4718600 | tf_op jit(solution)/shard_map/ppermute | solution.py:494
  74.6 57.0 %collective-permute-start.10 = (bf16[256,2048]{1,0:T(8,128)(2,1)}, bf16[256,2048]{1,0:T(8,128)(2,1)S(1)}, u32[]{:S(2)}, u32[]{:S(2)}) collective-permute-start(bf16[256,2048]{1,0:T(8,128)(2,1)} %broadcast_select_fusion.2), channel_id=1, source_target_pairs={{0,4},{1,5},{6,2},{7,3},{8,12},{9,13},{14,10},{15,11},{16,20},{17,... | collective-permute-start | bytes 3145736 | tf_op jit(solution)/shard_map/ppermute | solution.py:573
  137.0 54.9 %collective-permute-start.16 = (bf16[512,2048]{1,0:T(8,128)(2,1)}, bf16[512,2048]{1,0:T(8,128)(2,1)}, u32[]{:S(2)}, u32[]{:S(2)}) collective-permute-start(bf16[512,2048]{1,0:T(8,128)(2,1)} %constant_dynamic-update-slice_fusion.2.refs_0_), channel_id=1, source_target_pairs={{0,4},{1,5},{2,6},{3,7},{4,0},{5,1},{6,2},{7,3},{8,12},{9,13},{10,... | collective-permute-start | bytes 6291464 | tf_op jit(solution)/shard_map/ppermute | solution.py:494
  137.9 53.9 %collective-permute-start.15 = (bf16[256,4096]{1,0:T(8,128)(2,1)}, bf16[256,4096]{1,0:T(8,128)(2,1)}, u32[]{:S(2)}, u32[]{:S(2)}) collective-permute-start(bf16[256,4096]{1,0:T(8,128)(2,1)} %pad_maximum_fusion), channel_id=1, source_target_pairs={{0,2},{1,3},{2,0},{3,1},{4,6},{5,7},{6,4},{7,5},{8,10},{9,11},{10,... | collective-permute-start | bytes 6291464 | tf_op jit(solution)/shard_map/ppermute | solution.py:494
  279.9 59.1 %collective-permute-start.35 = (bf16[256,2048]{1,0:T(8,128)(2,1)S(1)}, bf16[256,2048]{1,0:T(8,128)(2,1)S(1)}, u32[]{:S(2)}, u32[]{:S(2)}) collective-permute-start(bf16[256,2048]{1,0:T(8,128)(2,1)S(1)} %bitcast.163), channel_id=1, source_target_pairs={{2,16},{3,17},{6,20},{7,21},{10,24},{11,25},{14,28},{15,29},{16,2}... | collective-permute-start | bytes 3145736 | tf_op jit(solution)/shard_map/ppermute | solution.py:512
  486.2 49.5 %collective-permute-start.52 = (bf16[256,2048]{1,0:T(8,128)(2,1)}, bf16[256,2048]{1,0:T(8,128)(2,1)}, u32[]{:S(2)}, u32[]{:S(2)}) collective-permute-start(bf16[256,2048]{1,0:T(8,128)(2,1)} %convert_element_type.249), channel_id=1, source_target_pairs={{2,16},{3,17},{6,20},{7,21},{10,24},{11,25},{14,28},{15,29},{16,2}... | collective-permute-start | bytes 3145736 | tf_op jit(solution)/shard_map/ppermute | solution.py:512
  493.9 47.2 %collective-permute-start.51 = (bf16[2,1,256,2048]{3,2,1,0:T(8,128)(2,1)}, bf16[2,1,256,2048]{3,2,1,0:T(8,128)(2,1)}, u32[]{:S(2)}, u32[]{:S(2)}) collective-permute-start(bf16[2,1,256,2048]{3,2,1,0:T(8,128)(2,1)} %constant_dynamic-slice_fusion.11), channel_id=1, source_target_pairs={{0,4},{1,5},{2,6},{3,7},{4,0},{5,1},{6,2},{7,3},{8,12},{9,13},{10,... | collective-permute-start | bytes 6291464 | tf_op jit(solution)/shard_map/ppermute | solution.py:494
  578.5 74.5 %collective-permute-start.59 = (bf16[2,2,1,2,2,64,1024]{6,5,4,3,2,1,0:T(8,128)(2,1)}, bf16[2,2,1,2,2,64,1024]{6,5,4,3,2,1,0:T(8,128)(2,1)}, u32[]{:S(2)}, u32[]{:S(2)}) collective-permute-start(bf16[2,2,1,2,2,64,1024]{6,5,4,3,2,1,0:T(8,128)(2,1)} %constant_dynamic-slice_fusion.10), channel_id=1, source_target_pairs={{0,4},{1,5},{2,6},{3,7},{4,0},{5,1},{6,2},{7,3},{8,12},{9,13},{10,... | collective-permute-start | bytes 6291464 | tf_op jit(solution)/shard_map/ppermute | solution.py:494
  594.1 53.7 %collective-permute-start.61 = (bf16[2,2,1,2,2,64,512]{6,5,4,3,2,1,0:T(8,128)(2,1)}, bf16[2,2,1,2,2,64,512]{6,5,4,3,2,1,0:T(8,128)(2,1)}, u32[]{:S(2)}, u32[]{:S(2)}) collective-permute-start(bf16[2,2,1,2,2,64,512]{6,5,4,3,2,1,0:T(8,128)(2,1)} %constant_dynamic-slice_fusion.8), channel_id=1, source_target_pairs={{0,4},{1,5},{2,6},{3,7},{4,0},{5,1},{6,2},{7,3},{8,12},{9,13},{10,... | collective-permute-start | bytes 3145736 | tf_op jit(solution)/shard_map/ppermute | solution.py:494
  596.9 53.6 %collective-permute-start.60 = (bf16[1,1,256,2048]{3,2,1,0:T(8,128)(2,1)}, bf16[1,1,256,2048]{3,2,1,0:T(8,128)(2,1)}, u32[]{:S(2)}, u32[]{:S(2)}) collective-permute-start(bf16[1,1,256,2048]{3,2,1,0:T(8,128)(2,1)} %constant_dynamic-slice_fusion.9), channel_id=1, source_target_pairs={{0,16},{8,24},{16,0},{24,8},{1,17},{9,25},{17,1},{25,9},{2,18},{10... | collective-permute-start | bytes 3145736 | tf_op jit(solution)/shard_map/ppermute | solution.py:497
  716.8 49.0 %collective-permute-start.70 = (bf16[256,2048]{1,0:T(8,128)(2,1)}, bf16[256,2048]{1,0:T(8,128)(2,1)}, u32[]{:S(2)}, u32[]{:S(2)}) collective-permute-start(bf16[256,2048]{1,0:T(8,128)(2,1)} %pad_maximum_fusion.10), channel_id=1, source_target_pairs={{0,8},{8,0},{16,24},{24,16},{1,9},{9,1},{17,25},{25,17},{2,10},{10... | collective-permute-start | bytes 3145736 | tf_op jit(solution)/shard_map/ppermute | solution.py:497
  721.9 43.9 %collective-permute-start.71 = (bf16[256,2048]{1,0:T(8,128)(2,1)}, bf16[256,2048]{1,0:T(8,128)(2,1)}, u32[]{:S(2)}, u32[]{:S(2)}) collective-permute-start(bf16[256,2048]{1,0:T(8,128)(2,1)} %pad_maximum_fusion.11), channel_id=1, source_target_pairs={{0,2},{1,3},{2,0},{3,1},{4,6},{5,7},{6,4},{7,5},{8,10},{9,11},{10,... | collective-permute-start | bytes 3145736 | tf_op jit(solution)/shard_map/ppermute | solution.py:494
  729.3 39.4 %collective-permute-start.74 = (bf16[256,2048]{1,0:T(8,128)(2,1)S(1)}, bf16[256,2048]{1,0:T(8,128)(2,1)S(1)}, u32[]{:S(2)}, u32[]{:S(2)}) collective-permute-start(bf16[256,2048]{1,0:T(8,128)(2,1)S(1)} %bitcast.157), channel_id=1, source_target_pairs={{1,8},{3,10},{5,12},{7,14},{8,1},{10,3},{12,5},{14,7},{17,24},{19,... | collective-permute-start | bytes 3145736 | tf_op jit(solution)/shard_map/ppermute | solution.py:512
  773.0 45.5 %collective-permute-start.78 = (bf16[2,2,64,1024]{3,2,1,0:T(8,128)(2,1)S(1)}, bf16[2,2,64,1024]{3,2,1,0:T(8,128)(2,1)S(1)}, u32[]{:S(2)}, u32[]{:S(2)}) collective-permute-start(bf16[2,2,64,1024]{3,2,1,0:T(8,128)(2,1)S(1)} %dynamic-slice_bitcast_fusion.1), channel_id=1, source_target_pairs={{0,1},{1,0},{2,3},{3,2},{4,5},{5,4},{6,7},{7,6},{8,9},{9,8},{10,11... | collective-permute-start | bytes 1572872 | tf_op jit(solution)/shard_map/ppermute | solution.py:494
  785.6 56.0 %collective-permute-start.76 = (bf16[2,2,1,2,2,64,768]{6,5,4,3,2,1,0:T(8,128)(2,1)S(1)}, bf16[2,2,1,2,2,64,768]{6,5,4,3,2,1,0:T(8,128)(2,1)S(1)}, u32[]{:S(2)}, u32[]{:S(2)}) collective-permute-start(bf16[2,2,1,2,2,64,768]{6,5,4,3,2,1,0:T(8,128)(2,1)S(1)} %constant_dynamic-slice_fusion.2), channel_id=1, source_target_pairs={{0,4},{1,5},{2,6},{3,7},{4,0},{5,1},{6,2},{7,3},{8,12},{9,13},{10,... | collective-permute-start | bytes 4718600 | tf_op jit(solution)/shard_map/ppermute | solution.py:494
  786.1 54.8 %collective-permute-start.75 = (bf16[256,2048]{1,0:T(8,128)(2,1)S(1)}, bf16[256,2048]{1,0:T(8,128)(2,1)S(1)}, u32[]{:S(2)}, u32[]{:S(2)}) collective-permute-start(bf16[256,2048]{1,0:T(8,128)(2,1)S(1)} %fusion.9), channel_id=1, source_target_pairs={{2,16},{3,17},{6,20},{7,21},{10,24},{11,25},{14,28},{15,29},{16,2}... | collective-permute-start | bytes 3145736 | tf_op jit(solution)/shard_map/ppermute | solution.py:512
  844.2 45.3 %collective-permute-start.83 = (bf16[1,2,1,2,2,64,768]{6,5,4,3,2,1,0:T(8,128)(2,1)S(1)}, bf16[1,2,1,2,2,64,768]{6,5,4,3,2,1,0:T(8,128)(2,1)S(1)}, u32[]{:S(2)}, u32[]{:S(2)}) collective-permute-start(bf16[1,2,1,2,2,64,768]{6,5,4,3,2,1,0:T(8,128)(2,1)S(1)} %constant_dynamic-slice_fusion), channel_id=1, source_target_pairs={{0,16},{8,24},{16,0},{24,8},{1,17},{9,25},{17,1},{25,9},{2,18},{10... | collective-permute-start | bytes 2359304 | tf_op jit(solution)/shard_map/ppermute | solution.py:497
  845.7 44.0 %collective-permute-start.80 = (bf16[64,4096]{1,0:T(8,128)(2,1)S(1)}, bf16[64,4096]{1,0:T(8,128)(2,1)S(1)}, u32[]{:S(2)}, u32[]{:S(2)}) collective-permute-start(bf16[64,4096]{1,0:T(8,128)(2,1)S(1)} %pad_maximum_fusion.17), channel_id=1, source_target_pairs={{0,8},{8,0},{16,24},{24,16},{1,9},{9,1},{17,25},{25,17},{2,10},{10... | collective-permute-start | bytes 1572872 | tf_op jit(solution)/shard_map/ppermute | solution.py:497
  848.3 41.4 %collective-permute-start.81 = (bf16[64,4096]{1,0:T(8,128)(2,1)S(1)}, bf16[64,4096]{1,0:T(8,128)(2,1)S(1)}, u32[]{:S(2)}, u32[]{:S(2)}) collective-permute-start(bf16[64,4096]{1,0:T(8,128)(2,1)S(1)} %pad_maximum_fusion.18), channel_id=1, source_target_pairs={{0,2},{1,3},{2,0},{3,1},{4,6},{5,7},{6,4},{7,5},{8,10},{9,11},{10,... | collective-permute-start | bytes 1572872 | tf_op jit(solution)/shard_map/ppermute | solution.py:494
  852.6 38.7 %collective-permute-start.82 = (bf16[64,4096]{1,0:T(8,128)(2,1)S(1)}, bf16[64,4096]{1,0:T(8,128)(2,1)S(1)}, u32[]{:S(2)}, u32[]{:S(2)}) collective-permute-start(bf16[64,4096]{1,0:T(8,128)(2,1)S(1)} %pad_maximum_fusion.19), channel_id=1, source_target_pairs={{0,10},{1,11},{2,8},{3,9},{4,14},{5,15},{6,12},{7,13},{8,2},{9,3},... | collective-permute-start | bytes 1572872 | tf_op jit(solution)/shard_map/ppermute | solution.py:505
  (156 other events, 2651.3 us)
